TPU v7x, 32 devices: a whole 2x2x4 slice. The times are simulated.
32 devices in a mesh: seq: 8 (over z, y), grp: 4 (over x, core).
Axes of the slice: x: 2, y: 2, z: 4, core: 2. Of those that a mesh axis runs over, the one named last changes fastest.
Arguments:
- x_group: bfloat16 [2048, 2304], P('seq'), may hold values from -6 to 6
- decode_input: bfloat16 [3, 64, 2304], P(None, 'seq'), may hold values from -6 to 6
- prompt_len: int32 [64], P('seq'), may hold values from 1 to 768, as said below
- latent_pages: bfloat16 [8, 8, 12, 64, 576], P('seq'), may hold values from -6 to 6
- slot_target: int32 [8, 8, 12], P(None, 'seq'), may hold values from 0 to 95, as said below
- page_counts: int32 [8, 8], P(None, 'seq'), may hold values from 0 to 12, as said below
- kda_state: float32 [64, 32, 128, 128], P(None, 'grp', 'seq'), may hold values from -4 to 4
- query_proj: bfloat16 [2304, 6144], P(None, 'grp'), may hold values from -1 to 1
- latent_proj: bfloat16 [2304, 576], replicated, may hold values from -1 to 1
- key_expand: bfloat16 [512, 4096], P(None, 'grp'), may hold values from -1 to 1
- value_expand: bfloat16 [512, 4096], P(None, 'grp'), may hold values from -0.25 to 0.25
- mla_output: bfloat16 [4096, 2304], P('grp'), may hold values from -0.09375 to 0.09375
- kda_inputs: bfloat16 [2304, 3, 4096], P(None, None, 'grp'), may hold values from -0.125 to 0.125
- kda_beta: bfloat16 [2304, 32], P(None, 'grp'), may hold values from -0.125 to 0.125
- decay_down: bfloat16 [2304, 128], replicated, may hold values from -0.125 to 0.125
- decay_up: bfloat16 [128, 4096], P(None, 'grp'), may hold values from -0.5 to 0.5
- gate_down: bfloat16 [2304, 128], replicated, may hold values from -0.125 to 0.125
- gate_up: bfloat16 [128, 4096], P(None, 'grp'), may hold values from -0.5 to 0.5
- decay_log: float32 [32], P('grp'), may hold values from -2.5 to 0.5
- kda_output: bfloat16 [4096, 2304], P('grp'), may hold values from -0.09375 to 0.09375
Outputs:
- prefill_out: bfloat16 [2048, 2304], P('seq', 'grp')
- decode_out: bfloat16 [3, 64, 2304], P(None, 'seq', 'grp')
Inputs may be any that keep to these rules, and one draw needn't show every extreme that they name: A request has ceil(prompt_len / 64) pages, at most 12; on one owner drawn from the seed all 8 requests have 12 pages. `slot_target`: entry k < page_counts[s, d] holds local request * 12 + page of owner d; every page of every request is held in exactly one slot; entries past the count are 0. `page_counts`: slots are filled from slot 0; the count 12 is reached on some pair in every draw.
All inputs are finite; a program needn't handle non-finite values.
Results may differ from a plain program's by a relative error of at most 0.02.
Values may be sent and summed in bfloat16 or wider, within the bound.
A program may use at most 192 MiB of HBM per device.

v0:
```python
import jax
import jax.numpy as jnp
from jax import lax
from jax.sharding import PartitionSpec as P

LAT = 512
ROPE = 64
NOPE = 128
VH = 128
DK = 128
DV = 128
PAGE = 64
MAXP = 12


epsilon = 1e-06
masked_score = -1e30


def norm_rows(values):
    return values * lax.rsqrt(jnp.mean(values * values, axis=-1, keepdims=True) + epsilon)


def unit_rows(values):
    return values * lax.rsqrt(jnp.sum(values * values, axis=-1, keepdims=True) + epsilon)


def rotate(values, position):
    halfway = values.shape[-1] // 2
    frequency = jnp.exp(-jnp.log(10000.0) * jnp.arange(halfway, dtype=jnp.float32) / halfway)
    angles = position.astype(jnp.float32)[..., None] * frequency
    leading = values[..., :halfway]
    trailing = values[..., halfway:]
    return jnp.concatenate(
        [
            leading * jnp.cos(angles) - trailing * jnp.sin(angles),
            leading * jnp.sin(angles) + trailing * jnp.cos(angles),
        ],
        axis=-1,
    )


def make_latent(normed, latent_proj, position):
    projected = jnp.dot(normed, latent_proj, preferred_element_type=jnp.float32)
    return jnp.concatenate(
        [norm_rows(projected[:, :LAT]), rotate(projected[:, LAT:], position)], axis=-1
    ).astype(jnp.bfloat16)


def make_query(normed, query_proj, position):
    head_count = query_proj.shape[1] // (NOPE + ROPE)
    projected = jnp.dot(normed, query_proj, preferred_element_type=jnp.float32).reshape(
        normed.shape[0], head_count, NOPE + ROPE
    )
    return (
        projected[..., :NOPE].astype(jnp.bfloat16),
        rotate(projected[..., NOPE:], position[:, None]).astype(jnp.bfloat16),
    )


def absorb(q_nope, q_rope, key_expand):
    head_count = q_nope.shape[1]
    latent_query = jnp.einsum(
        "rhn,chn->rhc",
        q_nope,
        key_expand.reshape(LAT, head_count, NOPE),
        preferred_element_type=jnp.float32,
    )
    return jnp.concatenate([latent_query.astype(jnp.bfloat16), q_rope], axis=-1)


def partial_attend(queries, key_rows, live_mask):
    scores = jnp.einsum("rhc,kc->rhk", queries, key_rows, preferred_element_type=jnp.float32) * (
        NOPE + ROPE
    ) ** (-0.5)
    scores = jnp.where(live_mask[:, None, :], scores, masked_score)
    highest = jnp.max(scores, axis=-1)
    weights = jnp.where(live_mask[:, None, :], jnp.exp(scores - highest[..., None]), 0.0)
    totals = jnp.sum(weights, axis=-1)
    summed = jnp.einsum(
        "rhk,kc->rhc",
        weights.astype(jnp.bfloat16),
        key_rows[:, :LAT],
        preferred_element_type=jnp.float32,
    )
    return (highest, totals, summed)


def cache_mask(target, counts, lengths, offset, width):
    slot_live = jnp.arange(target.shape[1])[None, :] < counts[:, None]
    request = target // MAXP
    token_pos = (target % MAXP)[..., None] * PAGE + offset + jnp.arange(width)[None, None, :]
    owners = jnp.arange(lengths.shape[0])[:, None, None, None]
    live = (
        slot_live[None, :, :, None]
        & (request[None, :, :, None] == owners)
        & (token_pos[None] < lengths[:, None, None, None])
    )
    return live.reshape(lengths.shape[0], -1)


def shards(
    x_group,
    decode_input,
    prompt_len,
    latent_pages,
    slot_target,
    page_counts,
    kda_state,
    query_proj,
    latent_proj,
    key_expand,
    value_expand,
    mla_output,
    kda_inputs,
    kda_beta,
    decay_down,
    decay_up,
    gate_down,
    gate_up,
    decay_log,
    kda_output,
):
    seq_index = lax.axis_index("seq")
    grp_index = lax.axis_index("grp")
    head_local = key_expand.shape[1] // NOPE
    kh_local = decay_log.shape[0]
    model_width = x_group.shape[1]
    share_width = model_width // lax.axis_size("grp")
    column_start = grp_index * share_width
    states = lax.all_to_all(
        kda_state.astype(jnp.bfloat16), "seq", split_axis=0, concat_axis=2, tiled=True
    ).astype(kda_state.dtype)
    target = slot_target[:, 0, :]
    counts = page_counts[:, 0]
    sub_width = PAGE
    offset = 0
    arrived = lax.all_to_all(latent_pages, "seq", split_axis=1, concat_axis=0, tiled=True)
    cache_rows = arrived.reshape(-1, LAT + ROPE)
    cache_live = cache_mask(target, counts, prompt_len, offset, sub_width)
    rows_in = x_group.astype(jnp.float32)
    normed = norm_rows(rows_in).astype(jnp.bfloat16)
    group_rows = x_group.shape[0]
    position = seq_index * group_rows + jnp.arange(group_rows)
    q_nope, q_rope = make_query(normed, query_proj, position)
    own_latent = make_latent(normed, latent_proj, position)
    shard_rows = lax.all_gather(own_latent, "seq", axis=0, tiled=True)
    peak_old = jnp.full((group_rows, head_local), masked_score, jnp.float32)
    row_count = shard_rows.shape[0]
    k_nope = (
        jnp.dot(shard_rows[:, :LAT], key_expand, preferred_element_type=jnp.float32)
        .astype(jnp.bfloat16)
        .reshape(row_count, head_local, NOPE)
    )
    values = (
        jnp.dot(shard_rows[:, :LAT], value_expand, preferred_element_type=jnp.float32)
        .astype(jnp.bfloat16)
        .reshape(row_count, head_local, VH)
    )
    scores = jnp.einsum("qhn,khn->qhk", q_nope, k_nope, preferred_element_type=jnp.float32)
    scores = (
        scores
        + jnp.einsum("qhr,kr->qhk", q_rope, shard_rows[:, LAT:], preferred_element_type=jnp.float32)
    ) * (NOPE + ROPE) ** (-0.5)
    key_pos = jnp.arange(row_count)
    live = key_pos[None, None, :] <= position[:, None, None]
    scores = jnp.where(live, scores, masked_score)
    new_peak = jnp.maximum(peak_old, jnp.max(scores, axis=-1))
    weights = jnp.where(live, jnp.exp(scores - new_peak[..., None]), 0.0)
    totals_new = jnp.sum(weights, axis=-1)
    summed_new = jnp.einsum(
        "qhk,khv->qhv", weights.astype(jnp.bfloat16), values, preferred_element_type=jnp.float32
    )
    heads_out = (
        (summed_new / totals_new[..., None])
        .astype(jnp.bfloat16)
        .reshape(group_rows, head_local * VH)
    )
    prefill_part = jnp.dot(heads_out, mla_output, preferred_element_type=jnp.float32)
    attended = lax.psum_scatter(
        prefill_part.astype(jnp.bfloat16), "grp", scatter_dimension=1, tiled=True
    ).astype(jnp.float32)
    prefill_out = (
        lax.dynamic_slice_in_dim(rows_in, column_start, share_width, 1) + attended
    ).astype(jnp.bfloat16)
    steps_total = decode_input.shape[0]
    req_local = decode_input.shape[1]
    dec_rows = decode_input.astype(jnp.float32)
    dec_normed = norm_rows(dec_rows).astype(jnp.bfloat16)
    fresh_list = []
    results = []
    for step_index in range(steps_total):
        place = prompt_len + step_index
        q_nope_now, q_rope_now = make_query(dec_normed[step_index], query_proj, place)
        latent_query = absorb(q_nope_now, q_rope_now, key_expand)
        fresh_list.append(make_latent(dec_normed[step_index], latent_proj, place))
        fresh_keys = jnp.concatenate(fresh_list, axis=0)
        fresh_live = (jnp.arange(fresh_keys.shape[0]) % req_local)[None, :] == jnp.arange(
            req_local
        )[:, None]
        all_keys = jnp.concatenate([cache_rows, fresh_keys], axis=0)
        live_now = jnp.concatenate([cache_live, fresh_live], axis=1)
        peak_now, totals_now, summed_now = partial_attend(latent_query, all_keys, live_now)
        latent_out = (summed_now / totals_now[..., None]).astype(jnp.bfloat16)
        head_values = jnp.einsum(
            "rhc,chv->rhv",
            latent_out,
            value_expand.reshape(LAT, head_local, VH),
            preferred_element_type=jnp.float32,
        ).astype(jnp.bfloat16)
        mla_part = jnp.dot(
            head_values.reshape(req_local, head_local * VH),
            mla_output,
            preferred_element_type=jnp.float32,
        )
        mla_total = lax.psum(mla_part.astype(jnp.bfloat16), "grp").astype(jnp.float32)
        hidden = dec_rows[step_index] + mla_total
        kda_in = norm_rows(hidden).astype(jnp.bfloat16)
        hidden_share = lax.dynamic_slice_in_dim(hidden, column_start, share_width, 1)
        projected = jnp.dot(
            kda_in, kda_inputs.reshape(model_width, -1), preferred_element_type=jnp.float32
        ).reshape(req_local, 3, kh_local, DK)
        queries_kda = unit_rows(projected[:, 0]) * DK ** (-0.5)
        keys_kda = unit_rows(projected[:, 1])
        values_kda = projected[:, 2]
        write_rate = jax.nn.sigmoid(jnp.dot(kda_in, kda_beta, preferred_element_type=jnp.float32))
        decay_low = jnp.dot(kda_in, decay_down, preferred_element_type=jnp.float32).astype(
            jnp.bfloat16
        )
        decays = jnp.exp(
            -jnp.exp(decay_log)[None, :, None]
            * jax.nn.softplus(
                jnp.dot(decay_low, decay_up, preferred_element_type=jnp.float32).reshape(
                    req_local, kh_local, DK
                )
            )
        )
        gate_low = jnp.dot(kda_in, gate_down, preferred_element_type=jnp.float32).astype(
            jnp.bfloat16
        )
        out_gate = jax.nn.sigmoid(
            jnp.dot(gate_low, gate_up, preferred_element_type=jnp.float32).reshape(
                req_local, kh_local, DV
            )
        )
        states = states * decays[:, :, None, :]
        errors = values_kda - jnp.sum(states * keys_kda[:, :, None, :], axis=-1)
        states = states + write_rate[..., None, None] * errors[..., None] * keys_kda[:, :, None, :]
        readout = jnp.sum(states * queries_kda[:, :, None, :], axis=-1)
        blended = (
            (norm_rows(readout) * out_gate).astype(jnp.bfloat16).reshape(req_local, kh_local * DV)
        )
        kda_part = jnp.dot(blended, kda_output, preferred_element_type=jnp.float32)
        kda_share = lax.psum_scatter(
            kda_part.astype(jnp.bfloat16), "grp", scatter_dimension=1, tiled=True
        ).astype(jnp.float32)
        results.append((hidden_share + kda_share).astype(jnp.bfloat16))
    return (prefill_out, jnp.stack(results))


def solution(mesh):
    in_specs = (
        P("seq", None),
        P(None, "seq", None),
        P("seq"),
        P("seq", None, None, None, None),
        P(None, "seq", None),
        P(None, "seq"),
        P(None, "grp", "seq", None),
        P(None, "grp"),
        P(),
        P(None, "grp"),
        P(None, "grp"),
        P("grp", None),
        P(None, None, "grp"),
        P(None, "grp"),
        P(),
        P(None, "grp"),
        P(),
        P(None, "grp"),
        P("grp"),
        P("grp", None),
    )
    out_specs = (P("seq", "grp"), P(None, "seq", "grp"))
    return jax.shard_map(shards, mesh=mesh, in_specs=in_specs, out_specs=out_specs, check_vma=False)
```

profile of v0, /device:TPU:0, one launch (start us, length us, event | category | flops | bytes accessed | tf_op | source)
XLA Modules:
  0.0 498.3 jit_solution(10147834125611707913)
XLA Ops:
  8.0 7.6 %all-to-all-start = ((bf16[1,8,12,64,576]{4,3,2,0,1:T(8,128)(2,1)}), bf16[1,8,12,64,576]{4,3,2,0,1:T(8,128)(2,1)}, u32[]{:S(2)}, u32[]{:S(2)}) async-start(bf16[1,8,12,64,576]{4,3,2,0,1:T(8,128)(2,1)} %bitcast.383), calls=%async_computation.1 | async-start | bytes 15728640 | tf_op jit(solution)/shard_map/all_to_all | solution.py:138
  15.6 2.4 copy.278
  18.0 1.6 multiply_reduce_fusion.5
  19.6 2.1 fusion.92
  27.9 9.8 %copy.287 = bf16[2304,1536]{0,1:T(8,128)(2,1)} copy(bf16[2304,1536]{1,0:T(8,128)(2,1)} %param.27) | data formatting | bytes 14155776 | tf_op args[7]
  37.8 5.1 %fusion.139 = f32[8,8,192]{2,0,1:T(8,128)S(1)} fusion(bf16[8,192,2304]{2,1,0:T(8,128)(2,1)} %bitcast.374, bf16[3,8,2304]{2,1,0:T(8,128)(2,1)S(1)} %multiply_convert_fusion.4), kind=kOutput, calls=%fused_computation.208 | convolution fusion | flops 56623104 | bytes 7163904 | tf_op jit(solution)/shard_map/dot_general | solution.py:52
  42.8 1.9 fusion.143
  44.8 1.9 fusion.135
  53.3 18.7 %copy.297 = bf16[2304,3,1024]{0,2,1:T(8,128)(2,1)} copy(bf16[2304,3,1024]{2,0,1:T(8,128)(2,1)} %param.32) | data formatting | bytes 28311552 | tf_op args[12]
  72.0 4.0 convert_element_type.249
  78.9 6.0 %fusion.91 = f32[256,1536]{0,1:T(8,128)S(1)} fusion(bf16[2304,1536]{1,0:T(8,128)(2,1)} %param.27, f32[256]{0:T(256)S(1)} %copy-done.41, bf16[256,2304]{0,1:T(8,128)(2,1)S(1)} %copy-done.5), kind=kOutput, calls=%fused_computation.134 | convolution fusion | flops 1813708800 | bytes 9831424 | tf_op jit(solution)/shard_map/dot_general | solution.py:52
  89.2 95.4 %all-gather.2.cloned.1.call-done = bf16[2048,576]{0,1:T(8,128)(2,1)} async-done(((bf16[256,576]{0,1:T(8,128)(2,1)}), bf16[2048,576]{0,1:T(8,128)(2,1)}) %all-gather.2.cloned.1.call-update) | async-done | bytes 2359312 | tf_op jit(solution)/shard_map/all_gather | solution.py:147
  184.6 4.1 convolution_convert_fusion.1
  188.7 8.1 %fusion.110 = f32[8,2048,256]{2,1,0:T(8,128)} fusion(bf16[2048,8,128]{0,2,1:T(8,128)(2,1)S(1)} %bitcast.384, f32[256,8,192]{0,2,1:T(8,128)S(1)} %bitcast.389), kind=kOutput, calls=%fused_computation.146 | convolution fusion | flops 1073741824 | bytes 21495808 | tf_op jit(solution)/shard_map/qhn,khn->qhk/dot_general | solution.py:160
  196.8 11.2 %fusion.187 = (f32[256,8]{0,1:T(8,128)S(1)}, f32[256,8,2048]{0,2,1:T(8,128)}) fusion(bf16[2048,576]{0,1:T(8,128)(2,1)S(1)} %copy-done.36, bf16[256,8,32]{0,2,1:T(8,128)(2,1)S(1)} %copy-done.20, bf16[256,8,32]{0,2,1:T(8,128)(2,1)S(1)} %get-tuple-element.21, f32[8,2048,256]{2,1,0:T(8,128)} %fusion.110, pred[256,2048]{0,1:T(8,128)(4,1)S(1)} %iota_compare_fusion), kind=kOutput, calls=%fused_computation.344 | convolution fusion | flops 554170368 | bytes 34611200 | tf_op jit(solution)/shard_map/qhr,kr->qhk/dot_general | solution.py:163
  208.1 4.4 convolution_convert_fusion.2
  212.5 8.6 %fusion.5 = f32[256,8]{0,1:T(8,128)S(1)} fusion(f32[256,8,2048]{0,2,1:T(8,128)} %get-tuple-element.77, f32[256,8]{0,1:T(8,128)S(1)} %broadcast_maximum_fusion, pred[256,2048]{0,1:T(8,128)(4,1)S(1)} %iota_compare_fusion), kind=kLoop, calls=%fused_computation.7 | loop fusion | flops 12580864 | bytes 17317888 | tf_op jit(solution)/shard_map/reduce_sum | solution.py:170
  221.1 10.9 %divide_convert_fusion = bf16[256,8,128]{0,2,1:T(8,128)(2,1)} fusion(bf16[2048,8,128]{0,2,1:T(8,128)(2,1)} %bitcast.395, f32[256,8,2048]{0,2,1:T(8,128)} %get-tuple-element.77, f32[256,8]{0,1:T(8,128)S(1)} %broadcast_maximum_fusion, pred[256,2048]{0,1:T(8,128)(4,1)S(1)} %iota_compare_fusion, f32[256,8]{0,1:T(8,128)S(1)} %fusion.5), kind=kOutput, calls=%fused_computation.133 | convolution fusion | flops 1086849024 | bytes 22036480 | tf_op jit(solution)/shard_map/qhk,khv->qhv/dot_general | solution.py:171
  232.0 7.5 %all-to-all-start.1 = ((bf16[64,8,16,128]{3,2,1,0:T(8,128)(2,1)}), bf16[64,8,16,128]{3,2,1,0:T(8,128)(2,1)S(1)}, u32[]{:S(2)}, u32[]{:S(2)}) async-start(bf16[64,8,16,128]{3,2,1,0:T(8,128)(2,1)} %convert_element_type.249), calls=%async_computation.2 | async-start | bytes 4194304 | tf_op jit(solution)/shard_map/all_to_all | solution.py:131
  239.5 10.7 %copy.290 = bf16[6144,576]{0,1:T(8,128)(2,1)} copy(bf16[6144,576]{1,0:T(8,128)(2,1)} %bitcast.21) | data formatting | bytes 14155776 | tf_op jit(solution)/shard_map/reshape | solution.py:139
  250.2 11.3 %concatenate.65 = bf16[6160,576]{0,1:T(8,128)(2,1)} concatenate(bf16[6144,576]{0,1:T(8,128)(2,1)} %copy.290, bf16[8,576]{0,1:T(8,128)(2,1)S(1)} %copy.291, bf16[8,576]{0,1:T(8,128)(2,1)S(1)} %copy.306), dimensions={0} | concatenate | bytes 14192640 | tf_op jit(solution)/shard_map/concatenate | solution.py:201
  261.5 4.8 fusion.16
  269.9 2.0 fusion.82
  272.0 4.2 convolution_convert_fusion.6
  276.2 5.1 %fusion.78 = bf16[8,8,512]{2,1,0:T(8,128)(2,1)S(1)} fusion(bf16[6144,576]{0,1:T(8,128)(2,1)} %copy.290, bf16[8,576]{0,1:T(8,128)(2,1)S(1)} %copy.291, bf16[8,8,6152]{2,1,0:T(8,128)(2,1)} %get-tuple-element.81, f32[8,8]{1,0:T(8,128)S(1)} %get-tuple-element.80), kind=kOutput, calls=%fused_computation.121 | convolution fusion | flops 415842304 | bytes 7940352 | tf_op jit(solution)/shard_map/rhk,kc->rhc/dot_general | solution.py:80
  281.3 4.2 convolution_convert_fusion.8
  285.5 11.3 %concatenate.69 = bf16[6168,576]{0,1:T(8,128)(2,1)} concatenate(bf16[6144,576]{0,1:T(8,128)(2,1)} %copy.290, bf16[8,576]{0,1:T(8,128)(2,1)S(1)} %copy.291, bf16[8,576]{0,1:T(8,128)(2,1)S(1)} %copy.306, bf16[8,576]{0,1:T(8,128)(2,1)S(1)} %copy.321), dimensions={0} | concatenate | bytes 14211072 | tf_op jit(solution)/shard_map/concatenate | solution.py:201
  296.9 4.8 fusion.15
  302.3 2.0 fusion.84
  304.3 4.3 convolution_convert_fusion.4
  308.7 5.3 %convolution_convert_fusion = bf16[256,2304]{0,1:T(8,128)(2,1)} fusion(bf16[256,1024]{0,1:T(8,128)(2,1)S(1)} %bitcast.396, bf16[1024,2304]{1,0:T(8,128)(2,1)} %param.31), kind=kOutput, calls=%fused_computation.54 | convolution fusion | flops 1208549376 | bytes 6422528 | tf_op jit(solution)/shard_map/dot_general | solution.py:179
  314.3 25.8 %all-reduce.3.cloned.1.call-done = (bf16[8,2304]{1,0:T(8,128)(2,1)}, bf16[8,2304]{1,0:T(8,128)(2,1)}, bf16[8,2304]{1,0:T(8,128)(2,1)}) async-done(((bf16[8,2304]{1,0:T(8,128)(2,1)}, bf16[8,2304]{1,0:T(8,128)(2,1)}, bf16[8,2304]{1,0:T(8,128)(2,1)}), (bf16[8,2304]{1,0:T(8,128)(2,1)}, bf16[8,2304]{1,0:T(8,128)(2,1)}, bf16[8,2304]{1,0:T(8,128)(2,1)})) %all-reduce.3.cloned.1.call-update) | async-done | bytes 110608 | tf_op jit(solution)/shard_map/psum | solution.py:216
  341.8 6.9 %fusion.133 = f32[8,3,8,128]{3,0,2,1:T(8,128)S(1)} fusion(bf16[3,8,128,2304]{3,2,1,0:T(8,128)(2,1)} %bitcast.371, bf16[8,2304]{1,0:T(8,128)(2,1)S(1)} %multiply_convert_fusion.7), kind=kOutput, calls=%fused_computation.202 | convolution fusion | flops 113246208 | bytes 14290944 | tf_op jit(solution)/shard_map/dot_general | solution.py:220
  349.0 7.5 %fusion.131 = f32[8,3,8,128]{3,0,2,1:T(8,128)S(1)} fusion(bf16[3,8,128,2304]{3,2,1,0:T(8,128)(2,1)} %bitcast.372, bf16[8,2304]{1,0:T(8,128)(2,1)S(1)} %multiply_convert_fusion.6), kind=kOutput, calls=%fused_computation.200 | convolution fusion | flops 113246208 | bytes 14290944 | tf_op jit(solution)/shard_map/dot_general | solution.py:220
  365.2 7.0 %fusion.129 = f32[8,3,8,128]{3,0,2,1:T(8,128)S(1)} fusion(bf16[3,8,128,2304]{3,2,1,0:T(8,128)(2,1)} %bitcast.373, bf16[8,2304]{1,0:T(8,128)(2,1)S(1)} %multiply_convert_fusion.5), kind=kOutput, calls=%fused_computation.198 | convolution fusion | flops 113246208 | bytes 14290944 | tf_op jit(solution)/shard_map/dot_general | solution.py:220
  374.9 1.9 fusion.38
  377.1 3.2 multiply_reduce_fusion.3
  381.5 7.0 %multiply_reduce_fusion.2 = (f32[8,8,8,16]{3,1,0,2:T(8,128)S(1)}, f32[8,8,8,16]{3,1,0,2:T(8,128)}) fusion(bf16[8,8,8,16,128]{4,3,2,1,0:T(8,128)(2,1)S(1)} %bitcast.379, f32[8,8,128]{2,1,0:T(8,128)} %copy.314, f32[8,8,8,16]{3,1,0,2:T(8,128)S(1)} %fusion.115, f32[8,8,128]{2,1,0:T(8,128)} %copy.312, f32[8,8,128]{2,1,0:T(8,128)} %copy.311, ...), kind=kLoop, calls=%fused_computation.49 | loop fusion | flops 12566528 | bytes 2457600 | tf_op jit(solution)/shard_map/reduce_sum | solution.py:249
  390.8 1.7 reduce_sum.278
  393.6 3.8 convolution_convert_fusion.5
  397.4 1.8 copy.348
  403.7 7.2 %multiply_reduce_fusion.4 = (f32[8,8,8,16]{3,1,0,2:T(8,128)S(1)}, f32[8,8,8,16]{3,1,0,2:T(8,128)S(1)}) fusion(bf16[8,8,8,16,128]{4,3,2,1,0:T(8,128)(2,1)S(1)} %bitcast.380, f32[8,8,128]{2,1,0:T(8,128)S(1)} %copy.300, f32[8,8,8,16]{3,1,0,2:T(8,128)S(1)} %fusion.116, f32[8,8,128]{2,1,0:T(8,128)S(1)} %copy.298, f32[8,8,128]{2,1,0:T(8,128)} %copy.296, ...), kind=kLoop, calls=%fused_computation.52 | loop fusion | flops 14663680 | bytes 2523136 | tf_op jit(solution)/shard_map/reduce_sum | solution.py:249
  414.5 3.3 convolution_convert_fusion.7
  419.3 3.4 convolution_convert_fusion.3
  423.9 2.0 add_convert_fusion
  425.9 12.1 %reduce-scatter.15.cloned.1.call-done = bf16[576,8]{1,0:T(8,128)(2,1)} async-done(((bf16[2304,8]{1,0:T(8,128)(2,1)}), bf16[576,8]{1,0:T(8,128)(2,1)}) %reduce-scatter.15.cloned.1.call-update) | async-done | bytes 9232
  438.9 23.5 %reduce-scatter.13.cloned.1.call-done = bf16[576,8]{1,0:T(8,128)(2,1)} async-done(((bf16[2304,8]{1,0:T(8,128)(2,1)}), bf16[576,8]{1,0:T(8,128)(2,1)}) %reduce-scatter.13.cloned.1.call-update) | async-done | bytes 9232
  463.5 23.5 %reduce-scatter.17.cloned.1.call-done = bf16[576,8]{1,0:T(8,128)(2,1)} async-done(((bf16[2304,8]{1,0:T(8,128)(2,1)}), bf16[576,8]{1,0:T(8,128)(2,1)}) %reduce-scatter.17.cloned.1.call-update) | async-done | bytes 9232
  (246 shorter events, 58.3 us)
Async XLA Ops:
  8.0 11.6 %copy-start = (bf16[2304,576]{0,1:T(8,128)(2,1)S(1)}, bf16[2304,576]{0,1:T(8,128)(2,1)}, u32[]{:S(2)}) copy-start(bf16[2304,576]{0,1:T(8,128)(2,1)} %param.28) | copy-start | bytes 7962628
  8.0 224.0 %all-to-all-start = ((bf16[1,8,12,64,576]{4,3,2,0,1:T(8,128)(2,1)}), bf16[1,8,12,64,576]{4,3,2,0,1:T(8,128)(2,1)}, u32[]{:S(2)}, u32[]{:S(2)}) async-start(bf16[1,8,12,64,576]{4,3,2,0,1:T(8,128)(2,1)} %bitcast.383), calls=%async_computation.1 | async-start | bytes 15728640 | tf_op jit(solution)/shard_map/all_to_all | solution.py:138
  15.6 169.0 %all-gather.2.cloned.1.call-start = ((), (), s32[]{:S(2)}) async-start(), calls=%async_computation.6 | async-start | bytes 2654208 | tf_op jit(solution)/shard_map/all_gather | solution.py:147
  37.8 5.1 %copy-start.2 = (bf16[2304,1536]{0,1:T(8,128)(2,1)S(1)}, bf16[2304,1536]{0,1:T(8,128)(2,1)}, u32[]{:S(2)}) copy-start(bf16[2304,1536]{0,1:T(8,128)(2,1)} %copy.287) | copy-start | bytes 21233668
  44.8 4.2 copy-start.38
  44.8 5.4 %copy-start.37 = (s32[8,1,12]{2,1,0:T(1,128)S(1)}, s32[8,1,12]{2,1,0:T(1,128)}, u32[]{:S(2)}) copy-start(s32[8,1,12]{2,1,0:T(1,128)} %param.24) | copy-start | bytes 1156
  44.8 5.4 %copy-start.42 = (s32[8,1]{0,1:T(1,128)S(1)}, s32[8,1]{0,1:T(1,128)}, u32[]{:S(2)}) copy-start(s32[8,1]{0,1:T(1,128)} %param.25) | copy-start | bytes 100
  46.8 5.4 %copy-start.7 = (bf16[512,1024]{1,0:T(8,128)(2,1)S(1)}, bf16[512,1024]{1,0:T(8,128)(2,1)}, u32[]{:S(2)}) copy-start(bf16[512,1024]{1,0:T(8,128)(2,1)} %param.29) | copy-start | bytes 3145732
  72.0 6.8 %copy-start.43 = (f32[8]{0:T(128)S(1)}, f32[8]{0:T(128)}, u32[]{:S(2)}) copy-start(f32[8]{0:T(128)} %param.38) | copy-start | bytes 100
  72.0 6.8 %copy-start.41 = (f32[256]{0:T(256)S(1)}, f32[256]{0:T(256)}, u32[]{:S(2)}) copy-start(f32[256]{0:T(256)} %copy-done.40) | copy-start | bytes 3076
  78.8 7.3 %copy-start.31 = (f32[256,32]{0,1:T(8,128)S(1)}, f32[256,32]{0,1:T(8,128)}, u32[]{:S(2)}) copy-start(f32[256,32]{0,1:T(8,128)} %get-tuple-element.49) | copy-start | bytes 98308
  78.8 7.3 %copy-start.32 = (f32[256,32]{0,1:T(8,128)S(1)}, f32[256,32]{0,1:T(8,128)}, u32[]{:S(2)}) copy-start(f32[256,32]{0,1:T(8,128)} %get-tuple-element.50) | copy-start | bytes 98308
  78.8 8.0 %copy-start.39 = (s32[256]{0:T(256)S(1)}, s32[256]{0:T(256)}, u32[]{:S(2)}) copy-start(s32[256]{0:T(256)} %iota_add_fusion.1) | copy-start | bytes 3076
  78.8 8.4 %copy-start.30 = (pred[8,6144]{1,0:T(8,128)(4,1)S(1)}, pred[8,6144]{1,0:T(8,128)(4,1)}, u32[]{:S(2)}) copy-start(pred[8,6144]{1,0:T(8,128)(4,1)} %and.82) | copy-start | bytes 147460
  78.9 8.4 %copy-start.33 = (s32[6144]{0:T(1024)S(1)}, s32[6144]{0:T(1024)}, u32[]{:S(2)}) copy-start(s32[6144]{0:T(1024)} %add.375) | copy-start | bytes 73732
  184.6 4.1 copy-start.15
  188.7 8.1 %copy-start.20 = (bf16[256,8,32]{0,2,1:T(8,128)(2,1)S(1)}, bf16[256,8,32]{0,2,1:T(8,128)(2,1)}, u32[]{:S(2)}) copy-start(bf16[256,8,32]{0,2,1:T(8,128)(2,1)} %get-tuple-element.22) | copy-start | bytes 393220
  188.7 8.1 %copy-start.36 = (bf16[2048,576]{0,1:T(8,128)(2,1)S(1)}, bf16[2048,576]{0,1:T(8,128)(2,1)}, u32[]{:S(2)}) copy-start(bf16[2048,576]{0,1:T(8,128)(2,1)} %all-gather.2.cloned.1.call-done) | copy-start | bytes 7077892
  196.8 11.2 %copy-start.6 = (bf16[512,1024]{1,0:T(8,128)(2,1)S(1)}, bf16[512,1024]{1,0:T(8,128)(2,1)}, u32[]{:S(2)}) copy-start(bf16[512,1024]{1,0:T(8,128)(2,1)} %param.30) | copy-start | bytes 3145732
  232.0 142.9 %all-to-all-start.1 = ((bf16[64,8,16,128]{3,2,1,0:T(8,128)(2,1)}), bf16[64,8,16,128]{3,2,1,0:T(8,128)(2,1)S(1)}, u32[]{:S(2)}, u32[]{:S(2)}) async-start(bf16[64,8,16,128]{3,2,1,0:T(8,128)(2,1)} %convert_element_type.249), calls=%async_computation.2 | async-start | bytes 4194304 | tf_op jit(solution)/shard_map/all_to_all | solution.py:131
  239.5 100.6 %all-reduce.3.cloned.1.call-start = ((), (), s32[]{:S(2)}) async-start(), calls=%async_computation.11 | async-start | bytes 221184 | tf_op jit(solution)/shard_map/psum | solution.py:216
  250.2 11.3 %copy-start.22 = (bf16[8,8,576]{2,0,1:T(8,128)(2,1)S(1)}, bf16[8,8,576]{2,0,1:T(8,128)(2,1)}, u32[]{:S(2)}) copy-start(bf16[8,8,576]{2,0,1:T(8,128)(2,1)} %pad_maximum_fusion.3) | copy-start | bytes 221188
  250.2 11.3 %copy-start.29 = (pred[8,6160]{1,0:T(8,128)(4,1)S(1)}, pred[8,6160]{1,0:T(8,128)(4,1)}, u32[]{:S(2)}) copy-start(pred[8,6160]{1,0:T(8,128)(4,1)} %pad_add_fusion.1) | copy-start | bytes 147844
  261.5 5.4 %copy-start.3 = (bf16[6144,576]{0,1:T(8,128)(2,1)S(1)}, bf16[6144,576]{0,1:T(8,128)(2,1)}, u32[]{:S(2)}) copy-start(bf16[6144,576]{0,1:T(8,128)(2,1)} %copy.290) | copy-start | bytes 21233668
  261.5 5.4 %copy-start.34 = (bf16[8,8,576]{2,0,1:T(8,128)(2,1)S(1)}, bf16[8,8,576]{2,0,1:T(8,128)(2,1)}, u32[]{:S(2)}) copy-start(bf16[8,8,576]{2,0,1:T(8,128)(2,1)} %pad_maximum_fusion.2) | copy-start | bytes 221188
  261.5 5.4 %copy-start.35 = (pred[8,6152]{1,0:T(8,128)(4,1)S(1)}, pred[8,6152]{1,0:T(8,128)(4,1)}, u32[]{:S(2)}) copy-start(pred[8,6152]{1,0:T(8,128)(4,1)} %pad_add_fusion) | copy-start | bytes 147652
  266.3 3.6 slice-start
  285.5 11.3 %copy-start.21 = (bf16[8,8,576]{2,0,1:T(8,128)(2,1)S(1)}, bf16[8,8,576]{2,0,1:T(8,128)(2,1)}, u32[]{:S(2)}) copy-start(bf16[8,8,576]{2,0,1:T(8,128)(2,1)} %pad_maximum_fusion.4) | copy-start | bytes 221188
  285.5 11.3 %copy-start.28 = (pred[8,6168]{1,0:T(8,128)(4,1)S(1)}, pred[8,6168]{1,0:T(8,128)(4,1)}, u32[]{:S(2)}) copy-start(pred[8,6168]{1,0:T(8,128)(4,1)} %pad_add_fusion.2) | copy-start | bytes 148036
  296.9 5.4 %copy-start.4 = (bf16[6168,576]{0,1:T(8,128)(2,1)S(1)}, bf16[6168,576]{0,1:T(8,128)(2,1)}, u32[]{:S(2)}) copy-start(bf16[6168,576]{0,1:T(8,128)(2,1)} %concatenate.69) | copy-start | bytes 21316612
  304.3 4.4 copy-start.44
  308.6 115.3 %reduce-scatter.11.cloned.1.call-start = ((), (), s32[]{:S(2)}) async-start(), calls=%async_computation.7 | async-start | bytes 1474560 | tf_op jit(solution)/shard_map/reduce_scatter | solution.py:180
  314.0 123.9 %reduce-scatter.15.cloned.1.call-start = ((), (), s32[]{:S(2)}) async-start(), calls=%async_computation.9 | async-start | bytes 737280
  341.7 7.0 %copy-start.24 = (f32[8,2304]{1,0:T(8,128)}, f32[8,2304]{1,0:T(8,128)S(1)}, u32[]{:S(2)}) copy-start(f32[8,2304]{1,0:T(8,128)S(1)} %get-tuple-element.28) | copy-start | bytes 221188
  341.7 7.2 %copy-start.23 = (f32[8,2304]{1,0:T(8,128)}, f32[8,2304]{1,0:T(8,128)S(1)}, u32[]{:S(2)}) copy-start(f32[8,2304]{1,0:T(8,128)S(1)} %get-tuple-element.16) | copy-start | bytes 221188
  349.0 25.8 %copy-start.18 = (bf16[8,2304]{1,0:T(8,128)(2,1)}, bf16[8,2304]{1,0:T(8,128)(2,1)S(1)}, u32[]{:S(2)}) copy-start(bf16[8,2304]{1,0:T(8,128)(2,1)S(1)} %multiply_convert_fusion.6) | copy-start | bytes 110596
  349.0 9.5 %copy-start.8 = (bf16[2304,128]{1,0:T(8,128)(2,1)S(1)}, bf16[2304,128]{1,0:T(8,128)(2,1)}, u32[]{:S(2)}) copy-start(bf16[2304,128]{1,0:T(8,128)(2,1)} %param.34) | copy-start | bytes 1769476
  349.0 9.5 %copy-start.11 = (bf16[128,1024]{1,0:T(8,128)(2,1)S(1)}, bf16[128,1024]{1,0:T(8,128)(2,1)}, u32[]{:S(2)}) copy-start(bf16[128,1024]{1,0:T(8,128)(2,1)} %param.35) | copy-start | bytes 786436
  365.2 8.5 %copy-start.17 = (bf16[8,2304]{1,0:T(8,128)(2,1)}, bf16[8,2304]{1,0:T(8,128)(2,1)S(1)}, u32[]{:S(2)}) copy-start(bf16[8,2304]{1,0:T(8,128)(2,1)S(1)} %multiply_convert_fusion.5) | copy-start | bytes 110596
  365.2 9.4 %copy-start.25 = (bf16[2304,8]{0,1:T(8,128)(2,1)S(1)}, bf16[2304,8]{0,1:T(8,128)(2,1)}, u32[]{:S(2)}) copy-start(bf16[2304,8]{0,1:T(8,128)(2,1)} %param.33) | copy-start | bytes 110596
  374.9 6.5 %copy-start.26 = (f32[8,8,128]{2,1,0:T(8,128)S(1)}, f32[8,8,128]{2,1,0:T(8,128)}, u32[]{:S(2)}) copy-start(f32[8,8,128]{2,1,0:T(8,128)} %copy.327) | copy-start | bytes 98308
  374.9 6.5 %copy-start.27 = (f32[8,8,128]{2,1,0:T(8,128)S(1)}, f32[8,8,128]{2,1,0:T(8,128)}, u32[]{:S(2)}) copy-start(f32[8,8,128]{2,1,0:T(8,128)} %copy.326) | copy-start | bytes 98308
  377.1 15.5 %copy-start.9 = (bf16[2304,128]{1,0:T(8,128)(2,1)S(1)}, bf16[2304,128]{1,0:T(8,128)(2,1)}, u32[]{:S(2)}) copy-start(bf16[2304,128]{1,0:T(8,128)(2,1)} %param.36) | copy-start | bytes 1769476
  377.1 16.5 %copy-start.12 = (bf16[128,1024]{1,0:T(8,128)(2,1)S(1)}, bf16[128,1024]{1,0:T(8,128)(2,1)}, u32[]{:S(2)}) copy-start(bf16[128,1024]{1,0:T(8,128)(2,1)} %param.37) | copy-start | bytes 786436
  414.4 4.9 copy-start.13
  414.5 48.0 %reduce-scatter.13.cloned.1.call-start = ((), (), s32[]{:S(2)}) async-start(), calls=%async_computation.8 | async-start | bytes 737280
  419.3 71.1 %copy-start.1 = (bf16[2304,576]{0,1:T(8,128)(2,1)S(1)}, bf16[2304,576]{0,1:T(8,128)(2,1)}, u32[]{:S(2)}) copy-start(bf16[2304,576]{0,1:T(8,128)(2,1)} %param.28) | copy-start | bytes 7962628
  419.3 67.7 %reduce-scatter.17.cloned.1.call-start = ((), (), s32[]{:S(2)}) async-start(), calls=%async_computation.10 | async-start | bytes 737280
  (7 other events, 14.5 us)
Sparse Core Ops, SparseCore 0:
  23.7 160.9 all-gather.1
Sparse Core Ops, SparseCore 1:
  308.7 31.3 all-reduce.2
  342.7 27.0 reduce-scatter.10
  414.6 23.3 reduce-scatter.14
  440.5 22.0 reduce-scatter.12
  465.0 22.0 reduce-scatter.16
where the time goes:
time: 508 us; the launch traced here: 498 us
  waiting for transfers between devices  181 us (36%)
  matrix products  134 us (26%)
  local copies, waits for them, and re-layouts  89.5 us (18%)
  other arithmetic  62 us (12%)
  between operations  17 us (3%)
  starting transfers between devices  15.5 us (3%)
    all_gather x1, waiting for transfers between devices, shards(): shard_rows = lax.all_gather(own_latent, 'seq', axis=0, tiled=True)  95.4 us
    unnamed x9, waiting for transfers between devices  59.3 us
    unnamed x103, local copies, waits for them, and re-layouts  40 us
    psum x1, waiting for transfers between devices, shards(): lax.psum(mla_part.astype(jnp.bfloat16), 'grp').astype(jnp.float32)  25.8 us
    concatenate x2, local copies, waits for them, and re-layouts, shards(): all_keys = jnp.concatenate([cache_rows, fresh_keys], axis=0)  22.6 us
    dot_general x3, matrix products, shards(): jnp.dot(kda_in, kda_inputs.reshape(model_width, -1), preferred_element_ty...  21.4 us
    dot_general x4, matrix products, make_query(): jnp.dot(normed, query_proj, preferred_element_type=jnp.float32)  14.9 us
    reduce_sum x2, other arithmetic, shards(): readout = jnp.sum(states * queries_kda[:, :, None, :], axis=-1)  14.2 us
  transfers between devices with their start and end apart: 8, of which 5 were waited for; matrix products, arithmetic and copies ran while one was open for 56% of the time, Pallas kernels for 0%

commit v1 on v0

v1 whole, which is shorter than its diff:
```python
import jax
import jax.numpy as jnp
from jax import lax
from jax.experimental import pallas as pl
from jax.experimental.pallas import tpu as pltpu
from jax.sharding import PartitionSpec as P

LAT = 512
ROPE = 64
NOPE = 128
VH = 128
DK = 128
DV = 128
PAGE = 64
MAXP = 12


epsilon = 1e-06
masked_score = -1e30


def norm_rows(values):
    return values * lax.rsqrt(jnp.mean(values * values, axis=-1, keepdims=True) + epsilon)


def unit_rows(values):
    return values * lax.rsqrt(jnp.sum(values * values, axis=-1, keepdims=True) + epsilon)


def rotate(values, position):
    halfway = values.shape[-1] // 2
    frequency = jnp.exp(-jnp.log(10000.0) * jnp.arange(halfway, dtype=jnp.float32) / halfway)
    angles = position.astype(jnp.float32)[..., None] * frequency
    leading = values[..., :halfway]
    trailing = values[..., halfway:]
    return jnp.concatenate(
        [
            leading * jnp.cos(angles) - trailing * jnp.sin(angles),
            leading * jnp.sin(angles) + trailing * jnp.cos(angles),
        ],
        axis=-1,
    )


def make_latent(normed, latent_proj, position):
    projected = jnp.dot(normed, latent_proj, preferred_element_type=jnp.float32)
    return jnp.concatenate(
        [norm_rows(projected[:, :LAT]), rotate(projected[:, LAT:], position)], axis=-1
    ).astype(jnp.bfloat16)


def make_query(normed, query_proj, position):
    head_count = query_proj.shape[1] // (NOPE + ROPE)
    projected = jnp.dot(normed, query_proj, preferred_element_type=jnp.float32).reshape(
        normed.shape[0], head_count, NOPE + ROPE
    )
    return (
        projected[..., :NOPE].astype(jnp.bfloat16),
        rotate(projected[..., NOPE:], position[:, None]).astype(jnp.bfloat16),
    )


def prefill_body(place_ref, query_ref, rows_ref, key_ref, value_ref, out_ref, peak, total, mixed):
    pair, group_rows, _ = query_ref.shape
    nt = (((1,), (1,)), ((), ()))
    factor = (NOPE + ROPE) ** (-0.5) * 1.4426950408889634
    own = place_ref[0]

    def chunk(index, first):
        rows = rows_ref[pl.ds(pl.multiple_of(index * group_rows, group_rows), group_rows), :]
        latent = rows[:, :LAT]
        keys = jnp.dot(latent, key_ref[...], preferred_element_type=jnp.float32)
        keys = keys.astype(jnp.bfloat16)
        values = lax.dot_general(value_ref[...], latent, nt, preferred_element_type=jnp.float32)
        values = values.astype(jnp.bfloat16)
        for h in range(pair):
            full = jnp.concatenate([keys[:, h * NOPE : (h + 1) * NOPE], rows[:, LAT:]], axis=1)
            scores = lax.dot_general(full, query_ref[h], nt, preferred_element_type=jnp.float32)
            if first:
                key_at = lax.broadcasted_iota(jnp.int32, scores.shape, 0)
                query_at = lax.broadcasted_iota(jnp.int32, scores.shape, 1)
                scores = jnp.where(key_at <= query_at, scores, masked_score)
            top = jnp.max(scores, axis=0, keepdims=True)
            if not first:
                top = jnp.maximum(top, peak[h])
            weights = jnp.exp2((scores - top) * factor)
            summed = jnp.sum(weights, axis=0, keepdims=True)
            added = jnp.dot(
                values[h * VH : (h + 1) * VH],
                weights.astype(jnp.bfloat16),
                preferred_element_type=jnp.float32,
            )
            if first:
                total[h] = summed
                mixed[h] = added
            else:
                shrink = jnp.exp2((peak[h] - top) * factor)
                total[h] = total[h] * shrink + summed
                mixed[h] = mixed[h] * shrink + added
            peak[h] = top

    chunk(own, True)

    @pl.loop(0, own)
    def _(index):
        chunk(index, False)

    for h in range(pair):
        out_ref[:, h * VH : (h + 1) * VH] = (mixed[h] / total[h]).T.astype(out_ref.dtype)


def prefill_attend(seq_index, queries, rows, key_expand, value_expand):
    heads, group_rows, _ = queries.shape
    pair = 2
    row_count = rows.shape[0]
    return pl.pallas_call(
        prefill_body,
        out_shape=jax.ShapeDtypeStruct((group_rows, heads * VH), jnp.bfloat16),
        grid_spec=pltpu.PrefetchScalarGridSpec(
            num_scalar_prefetch=1,
            grid=(heads // pair,),
            in_specs=[
                pl.BlockSpec((pair, group_rows, NOPE + ROPE), lambda h, p: (h, 0, 0)),
                pl.BlockSpec((row_count, LAT + ROPE), lambda h, p: (0, 0)),
                pl.BlockSpec((LAT, pair * NOPE), lambda h, p: (0, h)),
                pl.BlockSpec((pair * VH, LAT), lambda h, p: (h, 0)),
            ],
            out_specs=pl.BlockSpec((group_rows, pair * VH), lambda h, p: (0, h)),
            scratch_shapes=[
                pltpu.VMEM((pair, 1, group_rows), jnp.float32),
                pltpu.VMEM((pair, 1, group_rows), jnp.float32),
                pltpu.VMEM((pair, VH, group_rows), jnp.float32),
            ],
        ),
        compiler_params=pltpu.CompilerParams(vmem_limit_bytes=40 * 1024 * 1024),
        cost_estimate=pl.CostEstimate(
            flops=2 * heads * group_rows * row_count * 4 * NOPE,
            bytes_accessed=row_count * (LAT + ROPE) * 4,
            transcendentals=heads * group_rows * row_count,
        ),
        name="prefill_attend",
    )(seq_index.reshape(1).astype(jnp.int32), queries, rows, key_expand, value_expand.T)


def shards(
    x_group,
    decode_input,
    prompt_len,
    latent_pages,
    slot_target,
    page_counts,
    kda_state,
    query_proj,
    latent_proj,
    key_expand,
    value_expand,
    mla_output,
    kda_inputs,
    kda_beta,
    decay_down,
    decay_up,
    gate_down,
    gate_up,
    decay_log,
    kda_output,
):
    f32, bf16 = jnp.float32, jnp.bfloat16
    seq_index = lax.axis_index("seq")
    grp_index = lax.axis_index("grp")
    owners = lax.axis_size("seq")
    heads = key_expand.shape[1] // NOPE
    kheads = decay_log.shape[0]
    width = x_group.shape[1]
    share = width // lax.axis_size("grp")
    col = grp_index * share
    scale = (NOPE + ROPE) ** (-0.5)
    steps, reqs, _ = decode_input.shape
    cap = slot_target.shape[2]
    n = steps * reqs

    dec_own = decode_input.reshape(n, width)
    dec_all = lax.all_gather(dec_own, "seq", axis=0, tiled=True)
    ints = jnp.concatenate([prompt_len, page_counts[:, 0], slot_target.reshape(-1)])
    ints = lax.all_gather(ints, "seq", axis=0)
    lens_all = ints[:, :reqs]
    counts = lax.dynamic_slice_in_dim(ints, reqs + seq_index, 1, 1)
    targets = lax.dynamic_slice_in_dim(ints, reqs + owners + seq_index * cap, cap, 1)

    states = lax.all_to_all(
        kda_state.astype(bf16), "seq", split_axis=0, concat_axis=2, tiled=True
    )

    group_rows = x_group.shape[0]
    rows_share = group_rows // lax.axis_size("grp")
    x_normed = norm_rows(x_group.astype(f32)).astype(bf16)
    own_normed = norm_rows(dec_own.astype(f32)).astype(bf16)
    own_place = (prompt_len[None, :] + jnp.arange(steps)[:, None]).reshape(n)
    share_normed = lax.dynamic_slice_in_dim(x_normed, grp_index * rows_share, rows_share, 0)
    share_place = seq_index * group_rows + grp_index * rows_share + jnp.arange(rows_share)
    latents = make_latent(
        jnp.concatenate([share_normed, own_normed]),
        latent_proj,
        jnp.concatenate([share_place, own_place]),
    )
    fresh = latents[rows_share:]
    shard_rows = lax.all_gather(latents[:rows_share], ("seq", "grp"), axis=0, tiled=True)

    dec_normed = norm_rows(dec_all.astype(f32)).astype(bf16)
    dec_place = (lens_all[:, None, :] + jnp.arange(steps)[None, :, None]).reshape(owners * n)
    dq_nope, dq_rope = make_query(dec_normed, query_proj, dec_place)
    latent_query = jnp.einsum(
        "rhn,chn->rhc", dq_nope, key_expand.reshape(LAT, heads, NOPE), preferred_element_type=f32
    ).astype(bf16)
    qc = jnp.concatenate([latent_query, dq_rope], axis=-1).reshape(owners, n * heads, LAT + ROPE)
    pages = latent_pages.reshape(owners, cap * PAGE, LAT + ROPE)
    slot_live = jnp.arange(cap)[None, :] < counts
    token = (targets % MAXP)[..., None] * PAGE + jnp.arange(PAGE)
    live = (
        slot_live[:, None, :, None]
        & ((targets // MAXP)[:, None, :, None] == jnp.arange(reqs)[None, :, None, None])
        & (token[:, None] < lens_all[:, :, None, None])
    ).reshape(owners, 1, reqs, 1, cap * PAGE)
    scores = jnp.einsum("oqc,okc->oqk", qc, pages, preferred_element_type=f32) * scale
    scores = scores.reshape(owners, steps, reqs, heads, cap * PAGE)
    scores = jnp.where(live, scores, masked_score)
    highest = jnp.max(scores, axis=-1, keepdims=True)
    weights = jnp.where(live, jnp.exp(scores - highest), 0.0)
    totals = jnp.sum(weights, axis=-1)
    summed = jnp.einsum(
        "oqk,okc->oqc",
        weights.astype(bf16).reshape(owners, n * heads, cap * PAGE),
        pages[:, :, :LAT],
        preferred_element_type=f32,
    ).reshape(owners * n, heads, LAT)
    safe = jnp.maximum(totals, 1e-30)
    part = (summed / safe.reshape(owners * n, heads, 1)).astype(bf16)
    part = jnp.einsum(
        "rhc,chv->rhv", part, value_expand.reshape(LAT, heads, VH), preferred_element_type=f32
    ).astype(bf16)
    lse = jnp.where(totals > 0, highest[..., 0] + jnp.log(safe), masked_score).reshape(
        owners, n, heads
    )
    lse_hi = lax.reduce_precision(lse, 8, 7)
    lse_lo = lse - lse_hi
    sent = jnp.concatenate(
        [part.reshape(owners, n, heads * VH), lse_hi.astype(bf16), lse_lo.astype(bf16)], axis=-1
    )
    came = lax.all_to_all(sent, "seq", split_axis=0, concat_axis=0, tiled=True)

    position = seq_index * group_rows + jnp.arange(group_rows)
    q_nope, q_rope = make_query(x_normed, query_proj, position)
    queries = jnp.concatenate([q_nope, q_rope], axis=-1).transpose(1, 0, 2)
    heads_out = prefill_attend(seq_index, queries, shard_rows, key_expand, value_expand)
    prefill_part = jnp.dot(heads_out, mla_output, preferred_element_type=f32)
    attended = lax.psum_scatter(
        prefill_part.astype(bf16), "grp", scatter_dimension=1, tiled=True
    ).astype(f32)
    prefill_out = (
        lax.dynamic_slice_in_dim(x_group, col, share, 1).astype(f32) + attended
    ).astype(bf16)

    own_nope = lax.dynamic_slice_in_dim(dq_nope, seq_index * n, n, 0)
    own_rope = lax.dynamic_slice_in_dim(dq_rope, seq_index * n, n, 0)
    fresh_k = jnp.dot(fresh[:, :LAT], key_expand, preferred_element_type=f32).astype(bf16)
    fresh_v = jnp.dot(fresh[:, :LAT], value_expand, preferred_element_type=f32).astype(bf16)
    fresh_scores = (
        jnp.einsum(
            "qhn,khn->hqk", own_nope, fresh_k.reshape(n, heads, NOPE), preferred_element_type=f32
        )
        + jnp.einsum("qhr,kr->hqk", own_rope, fresh[:, LAT:], preferred_element_type=f32)
    ) * scale
    at = jnp.arange(n)
    fresh_live = (
        (at[:, None] % reqs == at[None, :] % reqs) & (at[None, :] // reqs <= at[:, None] // reqs)
    )[None]
    fresh_scores = jnp.where(fresh_live, fresh_scores, masked_score)
    lse_came = came[..., heads * VH :].astype(f32)
    lse_came = (lse_came[..., :heads] + lse_came[..., heads:]).transpose(0, 2, 1)
    top = jnp.maximum(jnp.max(fresh_scores, axis=-1), jnp.max(lse_came, axis=0))
    fresh_w = jnp.where(fresh_live, jnp.exp(fresh_scores - top[..., None]), 0.0)
    came_w = jnp.exp(lse_came - top[None])
    total = jnp.sum(fresh_w, axis=-1) + jnp.sum(came_w, axis=0)
    mixed = jnp.einsum(
        "hqk,khv->qhv",
        fresh_w.astype(bf16),
        fresh_v.reshape(n, heads, VH),
        preferred_element_type=f32,
    )
    parts = came[..., : heads * VH].astype(f32).reshape(owners, n, heads, VH)
    mixed = mixed + jnp.sum(parts * came_w.transpose(0, 2, 1)[..., None], axis=0)
    head_values = (mixed / total.T[..., None]).astype(bf16).reshape(n, heads * VH)
    mla_part = jnp.dot(head_values, mla_output, preferred_element_type=f32)
    hidden = dec_own.astype(f32) + lax.psum(mla_part.astype(bf16), "grp").astype(f32)

    kda_in = norm_rows(hidden).astype(bf16)
    projected = jnp.dot(
        kda_in, kda_inputs.reshape(width, -1), preferred_element_type=f32
    ).reshape(n, 3, kheads, DK)
    split = (steps, reqs, kheads, DK)
    queries_kda = (unit_rows(projected[:, 0]) * DK ** (-0.5)).reshape(split)
    keys_kda = unit_rows(projected[:, 1]).reshape(split)
    values_kda = projected[:, 2].reshape(split)
    beta = jax.nn.sigmoid(jnp.dot(kda_in, kda_beta, preferred_element_type=f32))
    beta = beta.reshape(steps, reqs, kheads, 1)
    decay_low = jnp.dot(kda_in, decay_down, preferred_element_type=f32).astype(bf16)
    decays = jnp.exp(
        -jnp.exp(decay_log)[None, :, None]
        * jax.nn.softplus(
            jnp.dot(decay_low, decay_up, preferred_element_type=f32).reshape(n, kheads, DK)
        )
    ).reshape(split)
    gate_low = jnp.dot(kda_in, gate_down, preferred_element_type=f32).astype(bf16)
    out_gate = jax.nn.sigmoid(
        jnp.dot(gate_low, gate_up, preferred_element_type=f32).reshape(n, kheads, DV)
    )
    decayed = decays[0]
    looks = []
    for t in range(steps):
        if t:
            decayed = decayed * decays[t]
        looks += [keys_kda[t] * decayed, queries_kda[t] * decayed]
    seen = jnp.einsum(
        "rhxk,rhvk->rhxv",
        jnp.stack(looks, axis=2).astype(bf16),
        states,
        preferred_element_type=f32,
    )
    written = []
    reads = []
    for t in range(steps):
        if t:
            written = [(e, k * decays[t]) for e, k in written]
        err = values_kda[t] - seen[:, :, 2 * t]
        for e, k in written:
            err = err - e * jnp.sum(k * keys_kda[t], axis=-1, keepdims=True)
        written.append((beta[t] * err, keys_kda[t]))
        read = seen[:, :, 2 * t + 1]
        for e, k in written:
            read = read + e * jnp.sum(k * queries_kda[t], axis=-1, keepdims=True)
        reads.append(read)
    readout = jnp.stack(reads).reshape(n, kheads, DV)
    blended = (norm_rows(readout) * out_gate).astype(bf16).reshape(n, kheads * DV)
    kda_part = jnp.dot(blended, kda_output, preferred_element_type=f32)
    kda_share = lax.psum_scatter(
        kda_part.astype(bf16), "grp", scatter_dimension=1, tiled=True
    ).astype(f32)
    decode_out = (lax.dynamic_slice_in_dim(hidden, col, share, 1) + kda_share).astype(bf16)
    return (prefill_out, decode_out.reshape(steps, reqs, share))


def solution(mesh):
    in_specs = (
        P("seq", None),
        P(None, "seq", None),
        P("seq"),
        P("seq", None, None, None, None),
        P(None, "seq", None),
        P(None, "seq"),
        P(None, "grp", "seq", None),
        P(None, "grp"),
        P(),
        P(None, "grp"),
        P(None, "grp"),
        P("grp", None),
        P(None, None, "grp"),
        P(None, "grp"),
        P(),
        P(None, "grp"),
        P(),
        P(None, "grp"),
        P("grp"),
        P("grp", None),
    )
    out_specs = (P("seq", "grp"), P(None, "seq", "grp"))
    return jax.shard_map(shards, mesh=mesh, in_specs=in_specs, out_specs=out_specs, check_vma=False)
```

time: 508 us -> 279 us (0.55); the launches traced: 498 us -> 277 us
  waiting for transfers between devices: 181 us -> 56.5 us
  matrix products: 134 us -> 53.7 us
  blocking collectives: 0 us -> 45.3 us
  local copies, waits for them, and re-layouts: 89.5 us -> 56.2 us
  other arithmetic: 62 us -> 35.1 us
    all_gather x1, waiting for transfers between devices: 95.4 us -> 15.4 us  [shards(): lax.all_gather(latents[:rows_share], ('seq', 'grp'), axis=0, tiled=True)]
    dot_general x33 -> x17, matrix products: 114 us -> 39.9 us  [the longest x1 7.02 us: shards(): jnp.dot(kda_in, kda_inputs.reshape(width, -1), preferred_element_type=f32)]
    unnamed x9 -> x5, waiting for transfers between devices: 59.3 us -> 0.09 us
    reduce_scatter x1, waiting for transfers between devices: 0.03 us -> 41 us  [shards(): lax.psum_scatter(prefill_part.astype(bf16), 'grp', scatter_dimension=1, t...]
    all_gather x0 -> x1, blocking collectives: none -> 34.4 us  [shards(): dec_all = lax.all_gather(dec_own, 'seq', axis=0, tiled=True)]
    psum x1, waiting for transfers between devices: 25.8 us -> 0.01 us  [shards(): lax.psum(mla_part.astype(bf16), 'grp').astype(f32)]
    reduce_sum x5, other arithmetic: 28 us -> 3.85 us  [the longest x1 1.9 us: shards(): totals = jnp.sum(weights, axis=-1)]
    concatenate x5 -> x2, local copies, waits for them, and re-layouts: 23.1 us -> 3.02 us  [the longest x1 1.9 us: shards(): jnp.concatenate([part.reshape(owners, n, heads * VH), lse_hi.astype(bf16)...]
  transfers between devices with their start and end apart: 8 -> 6, of which waited for: 5 -> 2; matrix products, arithmetic and copies ran while one was open for 56% -> 32% of each run, Pallas kernels for 0% -> 1%
where the time goes in v1:
time: 279 us; the launch traced here: 277 us
  waiting for transfers between devices  56.5 us (20%)
  local copies, waits for them, and re-layouts  56.2 us (20%)
  matrix products  53.7 us (19%)
  blocking collectives  45.3 us (16%)
  other arithmetic  35.1 us (13%)
  between operations  16.6 us (6%)
  starting transfers between devices  10.5 us (4%)
  Pallas kernels  3.46 us (1%)
    reduce_scatter x1, waiting for transfers between devices, shards(): lax.psum_scatter(prefill_part.astype(bf16), 'grp', scatter_dimension=1, t...  41 us
    all_gather x1, blocking collectives, shards(): dec_all = lax.all_gather(dec_own, 'seq', axis=0, tiled=True)  34.4 us
    unnamed x74, local copies, waits for them, and re-layouts  32.8 us
    all_gather x1, waiting for transfers between devices, shards(): lax.all_gather(latents[:rows_share], ('seq', 'grp'), axis=0, tiled=True)  15.4 us
    dot_general x2, matrix products, make_query(): jnp.dot(normed, query_proj, preferred_element_type=jnp.float32)  12 us
    unnamed x1, blocking collectives  10.8 us
    dot_general x1, matrix products, shards(): jnp.dot(kda_in, kda_inputs.reshape(width, -1), preferred_element_type=f32)  7.02 us
    dot_general x1, matrix products, shards(): jnp.einsum('oqc,okc->oqk', qc, pages, preferred_element_type=f32) * scale  6.4 us
  transfers between devices with their start and end apart: 6, of which 2 were waited for; matrix products, arithmetic and copies ran while one was open for 32% of the time, Pallas kernels for 1%

profile of v1, /device:TPU:0, one launch (start us, length us, event | category | flops | bytes accessed | tf_op | source)
XLA Modules:
  0.0 277.3 jit_solution(16150370350815868816)
XLA Ops:
  8.0 34.4 %all_gather.13 = bf16[192,2304]{1,0:T(8,128)(2,1)S(1)} all-gather(bf16[24,2304]{1,0:T(8,128)(2,1)} %bitcast.276), channel_id=1, replica_groups=mesh['seq'=8,'grp'=4] {'seq'}, dimensions={0}, use_global_device_ids=true | all-gather | bytes 995328 | tf_op jit(solution)/shard_map/all_gather | solution.py:182
  42.7 5.6 %fusion.45 = f32[192,1536]{1,0:T(8,128)} fusion(bf16[2304,1536]{1,0:T(8,128)(2,1)} %param.27, bf16[192,2304]{1,0:T(8,128)(2,1)S(1)} %all_gather.13, f32[192]{0:T(256)S(1)} %add_rsqrt_fusion.4), kind=kOutput, calls=%fused_computation.64 | convolution fusion | flops 1360281600 | bytes 9143040 | tf_op jit(solution)/shard_map/dot_general | solution.py:54
  48.4 2.8 reshape.788
  51.1 2.8 %fusion.142 = (f32[192,8,32]{2,1,0:T(8,128)}, f32[192,8,32]{2,1,0:T(8,128)}) fusion(f32[192,8,192]{2,1,0:T(8,128)} %reshape.788), kind=kLoop, calls=%fused_computation.264 | loop fusion | bytes 786432 | tf_op jit(solution)/shard_map/slice | solution.py:34
  53.9 1.2 slice.222
  57.9 10.8 %all-reduce = s32[896]{0:T(1024)S(1)} all-reduce(s32[896]{0:T(1024)S(1)} %add_dynamic-update-slice_fusion), channel_id=2, replica_groups=mesh['seq'=8,'grp'=4] {'seq'}, use_global_device_ids=true, to_apply=%add | all-reduce | flops 896 | bytes 7168
  70.4 1.8 fusion.17
  74.7 6.4 %fusion.2 = (f32[8,192]{1,0:T(8,128)S(1)}, f32[8,192,768]{2,1,0:T(8,128)S(1)}) fusion(pred[8,192,768]{2,1,0:T(8,128)(4,1)S(1)} %bitcast.273, bf16[8,192,576]{2,1,0:T(8,128)(2,1)S(1)} %bitcast.278, bf16[8,768,576]{2,1,0:T(8,128)(2,1)} %bitcast.288), kind=kOutput, calls=%fused_computation.4 | convolution fusion | flops 1362491904 | bytes 14751744 | tf_op jit(solution)/shard_map/oqc,okc->oqk/dot_general | solution.py:223
  81.1 1.9 fusion.4
  83.0 6.4 %fusion = f32[8,192,512]{2,1,0:T(8,128)} fusion(bf16[8,768,576]{2,1,0:T(8,128)(2,1)} %bitcast.289, pred[8,192,768]{2,1,0:T(8,128)(4,1)S(1)} %bitcast.275, f32[8,192,768]{2,1,0:T(8,128)S(1)} %get-tuple-element.55, f32[8,192]{1,0:T(8,128)S(1)} %get-tuple-element.54), kind=kOutput, calls=%fused_computation | convolution fusion | flops 1213857792 | bytes 15341568 | tf_op jit(solution)/shard_map/oqk,okc->oqc/dot_general | solution.py:229
  90.1 4.2 %fusion.21 = bf16[192,8,128]{2,0,1:T(8,128)(2,1)S(1)} fusion(f32[192,8,512]{2,1,0:T(8,128)} %bitcast.290, f32[192,8]{0,1:T(8,128)S(1)} %copy.254, bf16[512,1024]{1,0:T(8,128)(2,1)} %param.30), kind=kOutput, calls=%fused_computation.29 | convolution fusion | flops 203096064 | bytes 4593664 | tf_op jit(solution)/shard_map/rhc,chv->rhv/dot_general | solution.py:237
  95.3 1.9 reshape.796
  97.2 1.4 select_n.115
  98.6 1.5 fusion.57
  100.2 1.9 concatenate.45
  102.1 4.3 %all-to-all-start = ((bf16[8,24,1040]{2,1,0:T(8,128)(2,1)}), bf16[8,24,1040]{2,1,0:T(8,128)(2,1)}, u32[]{:S(2)}, u32[]{:S(2)}) async-start(bf16[8,24,1040]{2,1,0:T(8,128)(2,1)} %concatenate.45), calls=%async_computation.1 | async-start | bytes 884736 | tf_op jit(solution)/shard_map/all_to_all | solution.py:248
  106.5 1.2 iota_add_fusion
  108.4 1.6 fusion.7
  110.0 2.5 fusion.8
  115.7 1.8 fusion.48
  120.6 3.9 %convert_element_type.175 = bf16[64,8,16,128]{3,2,1,0:T(8,128)(2,1)} convert(f32[64,8,16,128]{3,2,1,0:T(8,128)} %param.26) | non-fusion elementwise | flops 1048576 | bytes 6291456 | tf_op jit(solution)/shard_map/convert_element_type | solution.py:190
  126.1 5.7 %all-to-all-start.1 = ((bf16[64,8,16,128]{3,2,1,0:T(8,128)(2,1)}), bf16[64,8,16,128]{3,2,1,0:T(8,128)(2,1)S(1)}, u32[]{:S(2)}, u32[]{:S(2)}) async-start(bf16[64,8,16,128]{3,2,1,0:T(8,128)(2,1)} %convert_element_type.175), calls=%async_computation.2 | async-start | bytes 4194304 | tf_op jit(solution)/shard_map/all_to_all | solution.py:189
  133.1 1.2 mul.591
  134.3 1.3 mul.592
  137.1 3.7 %convolution_convert_fusion.2 = bf16[24,2304]{1,0:T(8,128)(2,1)} fusion(bf16[1024,2304]{1,0:T(8,128)(2,1)} %param.31, bf16[8,3,8,128]{3,2,1,0:T(8,128)(2,1)S(1)} %fusion.37), kind=kOutput, calls=%fused_computation.7 | convolution fusion | flops 113301504 | bytes 4878336 | tf_op jit(solution)/shard_map/dot_general | solution.py:292
  141.8 6.3 %fusion.148 = f32[256,1536]{0,1:T(8,128)S(1)} fusion(bf16[256,2304]{1,0:T(8,128)(2,1)} %fusion.8, bf16[2304,1536]{1,0:T(8,128)(2,1)} %param.27), kind=kOutput, calls=%fused_computation.270 | convolution fusion | flops 1811939328 | bytes 9830400 | tf_op jit(solution)/shard_map/dot_general | solution.py:54
  148.2 2.3 copy.246
  150.5 17.4 %copy.266 = bf16[2304,3,1024]{0,2,1:T(8,128)(2,1)} copy(bf16[2304,3,1024]{2,0,1:T(8,128)(2,1)} %param.32) | data formatting | bytes 28311552 | tf_op args[12]
  168.0 1.2 multiply_cosine_fusion
  169.2 1.3 copy.292
  170.5 1.3 copy.293
  172.1 1.9 subtract_convert_fusion
  174.0 1.3 maximum_bitcast_fusion.query_ref
  175.3 1.7 convert_add_fusion
  178.0 7.0 %fusion.55 = f32[24,3,8,128]{3,0,2,1:T(8,128)S(1)} fusion(bf16[3,8,128,2304]{3,2,1,0:T(8,128)(2,1)} %bitcast.268, bf16[24,2304]{1,0:T(8,128)(2,1)S(1)} %multiply_convert_fusion), kind=kOutput, calls=%fused_computation.95 | convolution fusion | flops 339738624 | bytes 14561280 | tf_op jit(solution)/shard_map/dot_general | solution.py:296
  185.2 1.5 convolution_bitcast_fusion
  189.5 1.2 fusion.53
  191.4 3.3 %convolution_convert_fusion.1 = bf16[24,2304]{1,0:T(8,128)(2,1)S(1)} fusion(bf16[1024,2304]{1,0:T(8,128)(2,1)} %param.39, bf16[24,128]{1,0:T(8,128)(2,1)S(1)} %convolution_convert_fusion.6, bf16[128,1024]{1,0:T(8,128)(2,1)S(1)} %copy-done.14, f32[3,8,8,128]{3,2,1,0:T(8,128)S(1)} %bitcast.281, f32[1,8,8,128]{3,1,2,0:T(8,128)S(1)} %get-tuple-element.26, ...), kind=kOutput, calls=%fused_computation.6 | convolution fusion | flops 119789568 | bytes 5294080 | tf_op jit(solution)/shard_map/dot_general | solution.py:343
  196.1 15.4 %all-gather.3.cloned.1.call-done.rows_ref = bf16[2048,576]{1,0:T(8,128)(2,1)} async-done(((bf16[64,576]{1,0:T(8,128)(2,1)}), bf16[2048,576]{1,0:T(8,128)(2,1)}) %all-gather.3.cloned.1.call-update) | async-done | bytes 2359312 | tf_op jit(solution)/shard_map/all_gather | solution.py:206
  211.5 1.2 copy-done.3
  212.8 1.3 copy-done.4
  214.0 1.2 copy-done.5
  215.3 1.7 copy-done.6
  217.0 3.5 %prefill_attend.1 = bf16[256,1024]{1,0:T(8,128)(2,1)S(1)} custom-call(s32[1]{0:T(128)} %bitcast.place_ref, bf16[8,256,192]{2,1,0:T(8,128)(2,1)S(1)} %copy-done.5, bf16[2048,576]{1,0:T(8,128)(2,1)S(1)} %copy-done.6, bf16[512,1024]{1,0:T(8,128)(2,1)S(1)} %copy-done.3, bf16[1024,512]{1,0:T(8,128)(2,1)S(1)} %bitcast.267), custom_call_target="tpu_custom_call" | custom-call | flops 4294967296 | bytes 4718592 | tf_op jit(solution)/shard_map/prefill_attend/pallas_call | solution.py:116
  220.5 3.0 %convolution_convert_fusion = bf16[256,2304]{0,1:T(8,128)(2,1)} fusion(bf16[256,1024]{1,0:T(8,128)(2,1)S(1)} %prefill_attend.1, bf16[1024,2304]{1,0:T(8,128)(2,1)S(1)} %bitcast.272), kind=kOutput, calls=%fused_computation.5 | convolution fusion | flops 1208549376 | bytes 6422528 | tf_op jit(solution)/shard_map/dot_general | solution.py:254
  225.9 1.6 fusion.111
  227.5 41.0 %reduce-scatter.5.cloned.1.call-done = bf16[256,576]{0,1:T(8,128)(2,1)} async-done(((bf16[256,2304]{0,1:T(8,128)(2,1)}), bf16[256,576]{0,1:T(8,128)(2,1)}) %reduce-scatter.5.cloned.1.call-update) | async-done | bytes 294928 | tf_op jit(solution)/shard_map/reduce_scatter | solution.py:255
  268.4 1.7 add_convert_fusion.2
  (172 shorter events, 28.9 us)
Async XLA Ops:
  8.0 107.7 %copy-start = (bf16[2304,576]{0,1:T(8,128)(2,1)S(1)}, bf16[2304,576]{0,1:T(8,128)(2,1)}, u32[]{:S(2)}) copy-start(bf16[2304,576]{0,1:T(8,128)(2,1)} %param.28) | copy-start | bytes 7962628
  8.0 61.9 %copy-start.22 = (f32[32]{0:T(128)}, f32[32]{0:T(128)S(1)}, u32[]{:S(2)}) copy-start(f32[32]{0:T(128)S(1)} %multiply_exponential_fusion) | copy-start | bytes 388
  48.3 7.4 %copy-start.24 = (s32[8,1,12]{2,1,0:T(1,128)S(1)}, s32[8,1,12]{2,1,0:T(1,128)}, u32[]{:S(2)}) copy-start(s32[8,1,12]{2,1,0:T(1,128)} %param.24) | copy-start | bytes 1156
  48.3 8.1 %copy-start.28 = (u32[32]{0:T(128)S(1)}, u32[32]{0:T(128)}, u32[]{:S(2)}) copy-start(u32[32]{0:T(128)} %constant.148) | copy-start | bytes 388
  48.3 9.4 %copy-start.25 = (s32[8]{0:T(128)S(1)}, s32[8]{0:T(128)}, u32[]{:S(2)}) copy-start(s32[8]{0:T(128)} %param.22) | copy-start | bytes 100
  48.3 9.4 %copy-start.26 = (s32[8,1]{0,1:T(1,128)S(1)}, s32[8,1]{0,1:T(1,128)}, u32[]{:S(2)}) copy-start(s32[8,1]{0,1:T(1,128)} %param.25) | copy-start | bytes 100
  55.1 17.1 %copy-start.8 = (bf16[192,8,128]{2,1,0:T(8,128)(2,1)}, bf16[192,8,128]{2,1,0:T(8,128)(2,1)S(1)}, u32[]{:S(2)}) copy-start(bf16[192,8,128]{2,1,0:T(8,128)(2,1)S(1)} %slice.222) | copy-start | bytes 1179652
  70.0 2.3 copy-start.9
  70.0 2.3 copy-start.10
  94.3 12.1 %copy-start.11 = (bf16[3,8,2304]{2,1,0:T(8,128)(2,1)S(1)}, bf16[3,8,2304]{2,1,0:T(8,128)(2,1)}, u32[]{:S(2)}) copy-start(bf16[3,8,2304]{2,1,0:T(8,128)(2,1)} %param.21) | copy-start | bytes 331780
  102.1 24.1 %all-to-all-start = ((bf16[8,24,1040]{2,1,0:T(8,128)(2,1)}), bf16[8,24,1040]{2,1,0:T(8,128)(2,1)}, u32[]{:S(2)}, u32[]{:S(2)}) async-start(bf16[8,24,1040]{2,1,0:T(8,128)(2,1)} %concatenate.45), calls=%async_computation.1 | async-start | bytes 884736 | tf_op jit(solution)/shard_map/all_to_all | solution.py:248
  114.6 3.2 %copy-start.2 = (bf16[512,1024]{1,0:T(8,128)(2,1)S(1)}, bf16[512,1024]{1,0:T(8,128)(2,1)}, u32[]{:S(2)}) copy-start(bf16[512,1024]{1,0:T(8,128)(2,1)} %key_ref.1) | copy-start | bytes 3145732
  114.6 3.7 %copy-start.7 = (bf16[512,1024]{1,0:T(8,128)(2,1)S(1)}, bf16[512,1024]{1,0:T(8,128)(2,1)}, u32[]{:S(2)}) copy-start(bf16[512,1024]{1,0:T(8,128)(2,1)} %param.30) | copy-start | bytes 3145732
  114.6 3.9 %copy-start.21 = (s32[3,8]{1,0:T(4,128)S(1)}, s32[3,8]{1,0:T(4,128)}, u32[]{:S(2)}) copy-start(s32[3,8]{1,0:T(4,128)} %iota_add_fusion) | copy-start | bytes 292
  117.6 0.7 copy-start.12
  120.6 4.0 %copy-start.23 = (f32[32]{0:T(128)S(1)}, f32[32]{0:T(128)}, u32[]{:S(2)}) copy-start(f32[32]{0:T(128)} %copy-done.22) | copy-start | bytes 388
  126.1 62.7 %all-to-all-start.1 = ((bf16[64,8,16,128]{3,2,1,0:T(8,128)(2,1)}), bf16[64,8,16,128]{3,2,1,0:T(8,128)(2,1)S(1)}, u32[]{:S(2)}, u32[]{:S(2)}) async-start(bf16[64,8,16,128]{3,2,1,0:T(8,128)(2,1)} %convert_element_type.175), calls=%async_computation.2 | async-start | bytes 4194304 | tf_op jit(solution)/shard_map/all_to_all | solution.py:189
  131.8 43.4 %all-reduce.3.cloned.1.call-start = ((), (), s32[]{:S(2)}) async-start(), calls=%async_computation.6 | async-start | bytes 221184 | tf_op jit(solution)/shard_map/psum | solution.py:293
  140.9 70.6 %all-gather.3.cloned.1.call-start = ((), (), s32[]{:S(2)}) async-start(), calls=%async_computation.4 | async-start | bytes 2703360 | tf_op jit(solution)/shard_map/all_gather | solution.py:206
  141.7 83.2 %reduce-scatter.7.cloned.1.call-start = ((), (), s32[]{:S(2)}) async-start(), calls=%async_computation.7 | async-start | bytes 737280
  150.5 17.4 %copy-start.27 = (f32[8]{0:T(128)S(1)}, f32[8]{0:T(128)}, u32[]{:S(2)}) copy-start(f32[8]{0:T(128)} %param.38) | copy-start | bytes 100
  178.0 9.6 %copy-start.15 = (bf16[2304,8]{0,1:T(8,128)(2,1)S(1)}, bf16[2304,8]{0,1:T(8,128)(2,1)}, u32[]{:S(2)}) copy-start(bf16[2304,8]{0,1:T(8,128)(2,1)} %param.33) | copy-start | bytes 110596
  178.0 10.6 %copy-start.13 = (bf16[2304,128]{1,0:T(8,128)(2,1)S(1)}, bf16[2304,128]{1,0:T(8,128)(2,1)}, u32[]{:S(2)}) copy-start(bf16[2304,128]{1,0:T(8,128)(2,1)} %param.36) | copy-start | bytes 1769476
  188.8 2.0 copy-start.17
  188.8 2.0 copy-start.20
  188.9 2.1 copy-start.16
  188.9 2.1 copy-start.18
  188.9 2.1 copy-start.19
  188.9 2.5 copy-start.14
  191.4 29.0 %slice-start = ((s8[4718592]{0:T(1024)(128)(4,1)}), s8[524288]{0:T(1024)(128)(4,1)S(1)}, s32[]{:S(2)}) async-start(s8[4718592]{0:T(1024)(128)(4,1)} %bitcast.271), calls=%async_computation.8 | async-start | bytes 1048576
  195.8 72.6 %reduce-scatter.5.cloned.1.call-start = ((), (), s32[]{:S(2)}) async-start(), calls=%async_computation.5 | async-start | bytes 1474560 | tf_op jit(solution)/shard_map/reduce_scatter | solution.py:255
  211.5 1.2 copy-start.3
  212.8 1.3 copy-start.4
  214.0 1.2 copy-start.5
  215.2 1.7 copy-start.6
  217.0 3.5 %slice-start.1 = ((s8[4718592]{0:T(1024)(128)(4,1)}), s8[4194304]{0:T(1024)(128)(4,1)S(1)}, s32[]{:S(2)}) async-start(s8[4718592]{0:T(1024)(128)(4,1)} %bitcast.271), calls=%async_computation.9 | async-start | bytes 8388608
  220.5 49.7 %copy-start.1 = (bf16[2304,576]{0,1:T(8,128)(2,1)S(1)}, bf16[2304,576]{0,1:T(8,128)(2,1)}, u32[]{:S(2)}) copy-start(bf16[2304,576]{0,1:T(8,128)(2,1)} %param.28) | copy-start | bytes 7962628
Sparse Core Ops, SparseCore 0:
  141.0 31.3 all-reduce.2
  195.9 23.5 reduce-scatter.6
  223.6 44.7 reduce-scatter.4
Sparse Core Ops, SparseCore 1:
  144.6 66.9 all-gather.2

commit v2 on v1

--- a/solution.py
+++ b/solution.py
@@ -1,3 +1,5 @@
+import functools
+
 import jax
 import jax.numpy as jnp
 from jax import lax
@@ -140,6 +142,177 @@
         ),
         name="prefill_attend",
     )(seq_index.reshape(1).astype(jnp.int32), queries, rows, key_expand, value_expand.T)
+
+
+def gather_body(owners, own_ref, all_ref, send_sem, recv_sem, local_sem):
+    me = lax.axis_index("seq")
+    rows = own_ref.shape[0]
+    barrier = pltpu.get_barrier_semaphore()
+    for step in range(1, owners):
+        peer = lax.rem(me + step, owners)
+        pl.semaphore_signal(
+            barrier, inc=1, device_id={"seq": peer}, device_id_type=pl.DeviceIdType.MESH
+        )
+    pl.semaphore_wait(barrier, owners - 1)
+    place = all_ref.at[pl.ds(pl.multiple_of(me * rows, rows), rows)]
+    copies = []
+    for step in range(1, owners):
+        peer = lax.rem(me + step, owners)
+        copies.append(
+            pltpu.make_async_remote_copy(
+                src_ref=own_ref,
+                dst_ref=place,
+                send_sem=send_sem.at[step],
+                recv_sem=recv_sem.at[step],
+                device_id={"seq": peer},
+                device_id_type=pl.DeviceIdType.MESH,
+            )
+        )
+        copies[-1].start()
+    local = pltpu.make_async_copy(own_ref, place, local_sem)
+    local.start()
+    local.wait()
+    for copy in copies:
+        copy.wait()
+
+
+def gather_rows(own, owners):
+    rows, width = own.shape
+    return pl.pallas_call(
+        functools.partial(gather_body, owners),
+        out_shape=jax.ShapeDtypeStruct((owners * rows, width), own.dtype),
+        in_specs=[pl.BlockSpec(memory_space=pltpu.VMEM)],
+        out_specs=pl.BlockSpec(memory_space=pltpu.VMEM),
+        scratch_shapes=[
+            pltpu.SemaphoreType.DMA((owners,)),
+            pltpu.SemaphoreType.DMA((owners,)),
+            pltpu.SemaphoreType.DMA,
+        ],
+        compiler_params=pltpu.CompilerParams(collective_id=0, has_side_effects=True),
+        name="gather_rows",
+    )(own)
+
+
+def query_body(rows_ref, weight_ref, key_ref, cos_ref, sin_ref, prefill_ref, decode_ref):
+    pair, group_rows, _ = prefill_ref.shape
+    owners, slab, _ = decode_ref.shape
+    each = slab // pair
+    nt = (((1,), (1,)), ((), ()))
+    projected = jnp.dot(rows_ref[...], weight_ref[...], preferred_element_type=jnp.float32)
+    for h in range(pair):
+        start = h * (NOPE + ROPE)
+        nope = projected[:, start : start + NOPE].astype(jnp.bfloat16)
+        rope = projected[:, start + NOPE : start + NOPE + ROPE]
+        turned = jnp.concatenate([rope[:, ROPE // 2 :], rope[:, : ROPE // 2]], axis=1)
+        rope = (rope * cos_ref[...] + turned * sin_ref[...]).astype(jnp.bfloat16)
+        prefill_ref[h] = jnp.concatenate([nope[:group_rows], rope[:group_rows]], axis=1)
+        latent = lax.dot_general(
+            nope[group_rows:],
+            key_ref[:, h * NOPE : (h + 1) * NOPE],
+            nt,
+            preferred_element_type=jnp.float32,
+        ).astype(jnp.bfloat16)
+        full = jnp.concatenate([latent, rope[group_rows:]], axis=1)
+        decode_ref[:, h * each : (h + 1) * each, :] = full.reshape(owners, each, LAT + ROPE)
+
+
+def make_queries(rows, group_rows, owners, query_proj, key_expand, cosine, sine):
+    pair = 2
+    total, width = rows.shape
+    heads = key_expand.shape[1] // NOPE
+    each = (total - group_rows) // owners
+    return pl.pallas_call(
+        query_body,
+        out_shape=(
+            jax.ShapeDtypeStruct((heads, group_rows, NOPE + ROPE), jnp.bfloat16),
+            jax.ShapeDtypeStruct((owners, heads * each, LAT + ROPE), jnp.bfloat16),
+        ),
+        grid=(heads // pair,),
+        in_specs=[
+            pl.BlockSpec((total, width), lambda h: (0, 0)),
+            pl.BlockSpec((width, pair * (NOPE + ROPE)), lambda h: (0, h)),
+            pl.BlockSpec((LAT, pair * NOPE), lambda h: (0, h)),
+            pl.BlockSpec((total, ROPE), lambda h: (0, 0)),
+            pl.BlockSpec((total, ROPE), lambda h: (0, 0)),
+        ],
+        out_specs=(
+            pl.BlockSpec((pair, group_rows, NOPE + ROPE), lambda h: (h, 0, 0)),
+            pl.BlockSpec((owners, pair * each, LAT + ROPE), lambda h: (0, h, 0)),
+        ),
+        compiler_params=pltpu.CompilerParams(vmem_limit_bytes=40 * 1024 * 1024),
+        cost_estimate=pl.CostEstimate(
+            flops=2 * total * width * query_proj.shape[1],
+            bytes_accessed=2 * width * (query_proj.shape[1] + total),
+            transcendentals=0,
+        ),
+        name="make_queries",
+    )(rows, query_proj, key_expand, cosine, sine)
+
+
+def page_body(reqs, query_ref, page_ref, holder_ref, value_ref, out_ref, parts, logs):
+    owner = pl.program_id(0)
+    heads, _, _ = parts.shape
+    rows = query_ref.shape[1]
+    each = rows // heads
+    keys = page_ref[0]
+    nt = (((1,), (1,)), ((), ()))
+    scores = lax.dot_general(query_ref[0], keys, nt, preferred_element_type=jnp.float32)
+    request = lax.rem(lax.broadcasted_iota(jnp.int32, (rows, 1), 0), reqs)
+    live = holder_ref[0] == request
+    scores = jnp.where(live, scores * (NOPE + ROPE) ** (-0.5), masked_score)
+    highest = jnp.max(scores, axis=1, keepdims=True)
+    weights = jnp.where(live, jnp.exp(scores - highest), 0.0)
+    totals = jnp.sum(weights, axis=1, keepdims=True)
+    safe = jnp.maximum(totals, 1e-30)
+    summed = jnp.dot(weights.astype(jnp.bfloat16), keys[:, :LAT], preferred_element_type=jnp.float32)
+    summed = (summed / safe).astype(jnp.bfloat16)
+    place = pl.ds(pl.multiple_of(owner * each, each), each)
+    parts[:, place, :] = summed.reshape(heads, each, LAT)
+    log = jnp.where(totals > 0, highest + jnp.log(safe), masked_score)
+    logs[:, place, :] = log.reshape(heads, each, 1)
+
+    @pl.when(owner == pl.num_programs(0) - 1)
+    def _():
+        lane = lax.broadcasted_iota(jnp.int32, (parts.shape[1], 128), 1)
+        tail = jnp.zeros((parts.shape[1], 128), jnp.float32)
+        for h in range(heads):
+            out_ref[:, h * VH : (h + 1) * VH] = jnp.dot(
+                parts[h], value_ref[:, h * VH : (h + 1) * VH], preferred_element_type=jnp.float32
+            ).astype(out_ref.dtype)
+            high = logs[h].astype(jnp.bfloat16).astype(jnp.float32)
+            tail = jnp.where(lane == h, high, tail)
+            tail = jnp.where(lane == heads + h, logs[h] - high, tail)
+        out_ref[:, heads * VH :] = tail.astype(out_ref.dtype)
+
+
+def attend_pages(reqs, queries, pages, holders, value_expand):
+    owners, rows, depth = queries.shape
+    heads = value_expand.shape[1] // VH
+    keys = pages.shape[1]
+    total = owners * rows // heads
+    return pl.pallas_call(
+        functools.partial(page_body, reqs),
+        out_shape=jax.ShapeDtypeStruct((total, heads * VH + 128), jnp.bfloat16),
+        grid=(owners,),
+        in_specs=[
+            pl.BlockSpec((1, rows, depth), lambda o: (o, 0, 0)),
+            pl.BlockSpec((1, keys, depth), lambda o: (o, 0, 0)),
+            pl.BlockSpec((1, 1, keys), lambda o: (o, 0, 0)),
+            pl.BlockSpec(value_expand.shape, lambda o: (0, 0)),
+        ],
+        out_specs=pl.BlockSpec((total, heads * VH + 128), lambda o: (0, 0)),
+        scratch_shapes=[
+            pltpu.VMEM((heads, total, LAT), jnp.bfloat16),
+            pltpu.VMEM((heads, total, 1), jnp.float32),
+        ],
+        compiler_params=pltpu.CompilerParams(vmem_limit_bytes=40 * 1024 * 1024),
+        cost_estimate=pl.CostEstimate(
+            flops=4 * owners * rows * keys * depth,
+            bytes_accessed=2 * owners * keys * depth,
+            transcendentals=owners * rows * keys,
+        ),
+        name="attend_pages",
+    )(queries, pages, holders, value_expand)
 
 
 def shards(
@@ -179,17 +352,6 @@
     n = steps * reqs
 
     dec_own = decode_input.reshape(n, width)
-    dec_all = lax.all_gather(dec_own, "seq", axis=0, tiled=True)
-    ints = jnp.concatenate([prompt_len, page_counts[:, 0], slot_target.reshape(-1)])
-    ints = lax.all_gather(ints, "seq", axis=0)
-    lens_all = ints[:, :reqs]
-    counts = lax.dynamic_slice_in_dim(ints, reqs + seq_index, 1, 1)
-    targets = lax.dynamic_slice_in_dim(ints, reqs + owners + seq_index * cap, cap, 1)
-
-    states = lax.all_to_all(
-        kda_state.astype(bf16), "seq", split_axis=0, concat_axis=2, tiled=True
-    )
-
     group_rows = x_group.shape[0]
     rows_share = group_rows // lax.axis_size("grp")
     x_normed = norm_rows(x_group.astype(f32)).astype(bf16)
@@ -205,53 +367,59 @@
     fresh = latents[rows_share:]
     shard_rows = lax.all_gather(latents[:rows_share], ("seq", "grp"), axis=0, tiled=True)
 
-    dec_normed = norm_rows(dec_all.astype(f32)).astype(bf16)
-    dec_place = (lens_all[:, None, :] + jnp.arange(steps)[None, :, None]).reshape(owners * n)
-    dq_nope, dq_rope = make_query(dec_normed, query_proj, dec_place)
-    latent_query = jnp.einsum(
-        "rhn,chn->rhc", dq_nope, key_expand.reshape(LAT, heads, NOPE), preferred_element_type=f32
+    each = -(-(n + 1) // 16) * 16
+    numbers = jnp.concatenate(
+        [prompt_len // PAGE, prompt_len % PAGE, page_counts[:, 0], slot_target.reshape(-1)]
     ).astype(bf16)
-    qc = jnp.concatenate([latent_query, dq_rope], axis=-1).reshape(owners, n * heads, LAT + ROPE)
+    numbers = jnp.pad(numbers, (0, width - numbers.shape[0]))[None]
+    payload = jnp.concatenate(
+        [own_normed, numbers, jnp.zeros((each - n - 1, width), bf16)], axis=0
+    )
+    payload, latents = lax.optimization_barrier((payload, latents))
+    dec_all = gather_rows(payload, owners)
+    numbers = dec_all.reshape(owners, each, width)[:, n, : 2 * reqs + owners + owners * cap]
+    ints = numbers.astype(jnp.int32)
+    lens_all = ints[:, :reqs] * PAGE + ints[:, reqs : 2 * reqs]
+    counts = lax.dynamic_slice_in_dim(ints, 2 * reqs + seq_index, 1, 1)
+    targets = lax.dynamic_slice_in_dim(ints, 2 * reqs + owners + seq_index * cap, cap, 1)
+
+    states = lax.all_to_all(
+        kda_state.astype(bf16), "seq", split_axis=0, concat_axis=2, tiled=True
+    )
+
+    position = seq_index * group_rows + jnp.arange(group_rows)
+    dec_place = (lens_all[:, None, :] + jnp.arange(each // reqs)[None, :, None]).reshape(-1)
+    place = jnp.concatenate([position, dec_place]).astype(f32)
+    half = ROPE // 2
+    angles = place[:, None] * jnp.exp(-jnp.log(10000.0) * jnp.arange(half, dtype=f32) / half)
+    cosine, sine = jnp.cos(angles), jnp.sin(angles)
+    queries, qc = make_queries(
+        jnp.concatenate([x_normed, dec_all]),
+        group_rows,
+        owners,
+        query_proj,
+        key_expand,
+        jnp.concatenate([cosine, cosine], axis=1),
+        jnp.concatenate([-sine, sine], axis=1),
+    )
+
     pages = latent_pages.reshape(owners, cap * PAGE, LAT + ROPE)
-    slot_live = jnp.arange(cap)[None, :] < counts
     token = (targets % MAXP)[..., None] * PAGE + jnp.arange(PAGE)
-    live = (
-        slot_live[:, None, :, None]
-        & ((targets // MAXP)[:, None, :, None] == jnp.arange(reqs)[None, :, None, None])
-        & (token[:, None] < lens_all[:, :, None, None])
-    ).reshape(owners, 1, reqs, 1, cap * PAGE)
-    scores = jnp.einsum("oqc,okc->oqk", qc, pages, preferred_element_type=f32) * scale
-    scores = scores.reshape(owners, steps, reqs, heads, cap * PAGE)
-    scores = jnp.where(live, scores, masked_score)
-    highest = jnp.max(scores, axis=-1, keepdims=True)
-    weights = jnp.where(live, jnp.exp(scores - highest), 0.0)
-    totals = jnp.sum(weights, axis=-1)
-    summed = jnp.einsum(
-        "oqk,okc->oqc",
-        weights.astype(bf16).reshape(owners, n * heads, cap * PAGE),
-        pages[:, :, :LAT],
-        preferred_element_type=f32,
-    ).reshape(owners * n, heads, LAT)
-    safe = jnp.maximum(totals, 1e-30)
-    part = (summed / safe.reshape(owners * n, heads, 1)).astype(bf16)
-    part = jnp.einsum(
-        "rhc,chv->rhv", part, value_expand.reshape(LAT, heads, VH), preferred_element_type=f32
-    ).astype(bf16)
-    lse = jnp.where(totals > 0, highest[..., 0] + jnp.log(safe), masked_score).reshape(
-        owners, n, heads
-    )
-    lse_hi = lax.reduce_precision(lse, 8, 7)
-    lse_lo = lse - lse_hi
-    sent = jnp.concatenate(
-        [part.reshape(owners, n, heads * VH), lse_hi.astype(bf16), lse_lo.astype(bf16)], axis=-1
-    )
-    came = lax.all_to_all(sent, "seq", split_axis=0, concat_axis=0, tiled=True)
-
-    position = seq_index * group_rows + jnp.arange(group_rows)
-    q_nope, q_rope = make_query(x_normed, query_proj, position)
-    queries = jnp.concatenate([q_nope, q_rope], axis=-1).transpose(1, 0, 2)
+    holder = targets // MAXP
+    length = jnp.sum(
+        jnp.where(holder[..., None] == jnp.arange(reqs), lens_all[:, None, :], 0), axis=-1
+    )
+    live = (jnp.arange(cap)[None, :] < counts)[..., None] & (token < length[..., None])
+    holders = jnp.where(live, holder[..., None], -1).reshape(owners, 1, cap * PAGE)
+    sent = attend_pages(reqs, qc, pages, holders, value_expand)
+    sent, shard_rows = lax.optimization_barrier((sent, shard_rows))
+    came = lax.all_to_all(
+        sent.reshape(owners, each, -1), "seq", split_axis=0, concat_axis=0, tiled=True
+    )
+
     heads_out = prefill_attend(seq_index, queries, shard_rows, key_expand, value_expand)
     prefill_part = jnp.dot(heads_out, mla_output, preferred_element_type=f32)
+    came, prefill_part = lax.optimization_barrier((came, prefill_part))
     attended = lax.psum_scatter(
         prefill_part.astype(bf16), "grp", scatter_dimension=1, tiled=True
     ).astype(f32)
@@ -259,22 +427,17 @@
         lax.dynamic_slice_in_dim(x_group, col, share, 1).astype(f32) + attended
     ).astype(bf16)
 
-    own_nope = lax.dynamic_slice_in_dim(dq_nope, seq_index * n, n, 0)
-    own_rope = lax.dynamic_slice_in_dim(dq_rope, seq_index * n, n, 0)
-    fresh_k = jnp.dot(fresh[:, :LAT], key_expand, preferred_element_type=f32).astype(bf16)
+    came = came[:, :n]
+    own_query = lax.dynamic_index_in_dim(qc, seq_index, 0, keepdims=False)
+    own_query = own_query.reshape(heads, each, LAT + ROPE)[:, :n]
     fresh_v = jnp.dot(fresh[:, :LAT], value_expand, preferred_element_type=f32).astype(bf16)
-    fresh_scores = (
-        jnp.einsum(
-            "qhn,khn->hqk", own_nope, fresh_k.reshape(n, heads, NOPE), preferred_element_type=f32
-        )
-        + jnp.einsum("qhr,kr->hqk", own_rope, fresh[:, LAT:], preferred_element_type=f32)
-    ) * scale
+    fresh_scores = jnp.einsum("hqc,kc->hqk", own_query, fresh, preferred_element_type=f32) * scale
     at = jnp.arange(n)
     fresh_live = (
         (at[:, None] % reqs == at[None, :] % reqs) & (at[None, :] // reqs <= at[:, None] // reqs)
     )[None]
     fresh_scores = jnp.where(fresh_live, fresh_scores, masked_score)
-    lse_came = came[..., heads * VH :].astype(f32)
+    lse_came = came[..., heads * VH :].astype(f32)[..., : 2 * heads]
     lse_came = (lse_came[..., :heads] + lse_came[..., heads:]).transpose(0, 2, 1)
     top = jnp.maximum(jnp.max(fresh_scores, axis=-1), jnp.max(lse_came, axis=0))
     fresh_w = jnp.where(fresh_live, jnp.exp(fresh_scores - top[..., None]), 0.0)

time: 279 us -> 265 us (0.950)
  waiting for transfers between devices: 56.5 us -> 107 us
  Pallas kernels: 3.46 us -> 50.8 us
  blocking collectives: 45.3 us -> 0 us
  matrix products: 53.7 us -> 21.8 us
  local copies, waits for them, and re-layouts: 56.2 us -> 39.5 us
  other arithmetic: 35.1 us -> 21 us
    pallas_call x0 -> x3, Pallas kernels: none -> 47.3 us  [the longest x1 28.7 us: gather_rows(): pl.pallas_call(functools.partial(gather_body, owners), out_shape=jax.Shap...]
    unnamed x5 -> x6, waiting for transfers between devices: 0.09 us -> 46.8 us
    reduce_scatter x1 -> x0, waiting for transfers between devices: 41 us -> none  [shards(): lax.psum_scatter(prefill_part.astype(bf16), 'grp', scatter_dimension=1, t...]
    all_gather x1 -> x0, blocking collectives: 34.4 us -> none  [shards(): dec_all = lax.all_gather(dec_own, 'seq', axis=0, tiled=True)]
    dot_general x9 -> x1, matrix products: 31.4 us -> 1.14 us  [shards(): jnp.einsum('hqc,kc->hqk', own_query, fresh, preferred_element_type=f32)]
    psum x1, waiting for transfers between devices: 0.01 us -> 20.1 us  [shards(): lax.psum(mla_part.astype(bf16), 'grp').astype(f32)]
    all_to_all x1, waiting for transfers between devices: 0.01 us -> 12.4 us  [shards(): lax.all_to_all(sent.reshape(owners, each, -1), 'seq', split_axis=0, conca...]
    all_to_all x1, waiting for transfers between devices: 0.01 us -> 10.9 us  [shards(): lax.all_to_all(kda_state.astype(bf16), 'seq', split_axis=0, concat_axis=2...]
  transfers between devices with their start and end apart: 6 -> 6, of which waited for: 2 -> 6; matrix products, arithmetic and copies ran while one was open for 32% -> 17% of each run, Pallas kernels for 1% -> 19%
where the time goes in v2:
time: 265 us; the launch traced here: 264 us
  waiting for transfers between devices  107 us (40%)
  Pallas kernels  50.8 us (19%)
  local copies, waits for them, and re-layouts  39.5 us (15%)
  matrix products  21.8 us (8%)
  other arithmetic  21 us (8%)
  between operations  14.5 us (5%)
  starting transfers between devices  8.99 us (3%)
    unnamed x6, waiting for transfers between devices  46.8 us
    unnamed x57, local copies, waits for them, and re-layouts  31.5 us
    pallas_call x1, Pallas kernels, gather_rows(): pl.pallas_call(functools.partial(gather_body, owners), out_shape=jax.Shap...  28.7 us
    psum x1, waiting for transfers between devices, shards(): lax.psum(mla_part.astype(bf16), 'grp').astype(f32)  20.1 us
    all_gather x1, waiting for transfers between devices, shards(): lax.all_gather(latents[:rows_share], ('seq', 'grp'), axis=0, tiled=True)  16.9 us
    all_to_all x1, waiting for transfers between devices, shards(): lax.all_to_all(sent.reshape(owners, each, -1), 'seq', split_axis=0, conca...  12.4 us
    all_to_all x1, waiting for transfers between devices, shards(): lax.all_to_all(kda_state.astype(bf16), 'seq', split_axis=0, concat_axis=2...  10.9 us
    pallas_call x1, Pallas kernels, attend_pages(): pl.pallas_call(functools.partial(page_body, reqs), out_shape=jax.ShapeDty...  9.37 us
  transfers between devices with their start and end apart: 6, of which 6 were waited for; matrix products, arithmetic and copies ran while one was open for 17% of the time, Pallas kernels for 19%

profile of v2, /device:TPU:0, one launch (start us, length us, event | category | flops | bytes accessed | tf_op | source)
XLA Modules:
  0.0 263.7 jit_solution(6732285053618265042)
XLA Ops:
  7.3 1.7 fusion
  9.0 2.6 fusion.1
  11.9 1.0 constant_dynamic-slice_fusion.1
  12.9 0.9 fusion.16
  14.6 0.7 slice.197
  15.6 0.8 maximum_maximum_fusion.own_ref
  16.4 28.7 %gather_rows.1 = bf16[256,2304]{1,0:T(8,128)(2,1)} custom-call(bf16[32,2304]{1,0:T(8,128)(2,1)} %maximum_maximum_fusion.own_ref), custom_call_target="tpu_custom_call" | custom-call | tf_op jit(solution)/shard_map/gather_rows/pallas_call | solution.py:181
  45.1 0.7 slice.196
  47.3 1.0 fusion.40
  48.6 1.6 pad_maximum_fusion.rows_ref
  50.3 9.2 %make_queries.1 = (bf16[8,256,192]{2,1,0:T(8,128)(2,1)S(1)}, bf16[8,256,576]{2,1,0:T(8,128)(2,1)S(1)}) custom-call(bf16[512,2304]{1,0:T(8,128)(2,1)S(1)} %pad_maximum_fusion.rows_ref, bf16[2304,1536]{1,0:T(8,128)(2,1)} %weight_ref.1, bf16[512,1024]{1,0:T(8,128)(2,1)S(1)} %copy-done.5, f32[512,64]{1,0:T(8,128)S(1)} %get-tuple-element.75.cos_ref, ...), custom_call_target="tpu_custom_call" | custom-call | flops 3623878656 | bytes 9437184 | tf_op jit(solution)/shard_map/make_queries/pallas_call | solution.py:224
  59.5 1.0 copy-done.7
  60.5 9.4 %attend_pages.1 = bf16[256,1152]{1,0:T(8,128)(2,1)} custom-call(bf16[8,256,576]{2,1,0:T(8,128)(2,1)S(1)} %get-tuple-element.10.query_ref, bf16[8,768,576]{2,1,0:T(8,128)(2,1)S(1)} %bitcast.258, s32[8,1,768]{2,1,0:T(1,128)S(1)} %and_select_fusion.holder_ref, bf16[512,1024]{1,0:T(8,128)(2,1)S(1)} %copy-done.2), custom_call_target="tpu_custom_call" | custom-call | flops 3623878656 | bytes 7077888 | tf_op jit(solution)/shard_map/attend_pages/pallas_call | solution.py:293
  69.9 1.5 copy-done.3
  71.4 16.9 %all-gather.2.cloned.1.call-done.rows_ref = bf16[2048,576]{1,0:T(8,128)(2,1)} async-done(((bf16[64,576]{1,0:T(8,128)(2,1)}), bf16[2048,576]{1,0:T(8,128)(2,1)}) %all-gather.2.cloned.1.call-update) | async-done | bytes 2359312 | tf_op jit(solution)/shard_map/all_gather | solution.py:368
  88.4 4.3 %all-to-all-start = ((bf16[8,32,1152]{2,1,0:T(8,128)(2,1)}), bf16[8,32,1152]{2,1,0:T(8,128)(2,1)S(1)}, u32[]{:S(2)}, u32[]{:S(2)}) async-start(bf16[8,32,1152]{2,1,0:T(8,128)(2,1)} %bitcast.8), calls=%async_computation | async-start | bytes 1179648 | tf_op jit(solution)/shard_map/all_to_all | solution.py:416
  92.6 3.9 %convert_element_type.125 = bf16[64,8,16,128]{3,2,1,0:T(8,128)(2,1)} convert(f32[64,8,16,128]{3,2,1,0:T(8,128)} %param.26) | non-fusion elementwise | flops 1048576 | bytes 6291456 | tf_op jit(solution)/shard_map/convert_element_type | solution.py:387
  96.6 12.4 %all-to-all-done = bf16[8,32,1152]{2,1,0:T(8,128)(2,1)S(1)} async-done(((bf16[8,32,1152]{2,1,0:T(8,128)(2,1)}), bf16[8,32,1152]{2,1,0:T(8,128)(2,1)S(1)}, u32[]{:S(2)}, u32[]{:S(2)}) %all-to-all-start) | async-done | bytes 589856 | tf_op jit(solution)/shard_map/all_to_all | solution.py:416
  109.0 4.4 %all-to-all-start.1 = ((bf16[64,8,16,128]{3,2,1,0:T(8,128)(2,1)}), bf16[64,8,16,128]{3,2,1,0:T(8,128)(2,1)}, u32[]{:S(2)}, u32[]{:S(2)}) async-start(bf16[64,8,16,128]{3,2,1,0:T(8,128)(2,1)} %convert_element_type.125), calls=%async_computation.1 | async-start | bytes 4194304 | tf_op jit(solution)/shard_map/all_to_all | solution.py:386
  113.4 0.5 copy.190
  114.0 1.0 constant_dynamic-slice_fusion
  115.3 1.1 fusion.111
  116.5 1.7 copy-done.4
  118.2 1.2 copy-done.6
  119.4 1.2 copy-done.8
  120.6 3.5 %prefill_attend.1 = bf16[256,1024]{1,0:T(8,128)(2,1)S(1)} custom-call(s32[1]{0:T(128)} %bitcast.9.place_ref, bf16[8,256,192]{2,1,0:T(8,128)(2,1)S(1)} %copy-done.8, bf16[2048,576]{1,0:T(8,128)(2,1)S(1)} %copy-done.4, bf16[512,1024]{1,0:T(8,128)(2,1)S(1)} %copy-done.6, bf16[1024,512]{1,0:T(8,128)(2,1)S(1)} %bitcast.255), custom_call_target="tpu_custom_call" | custom-call | flops 4294967296 | bytes 4718592 | tf_op jit(solution)/shard_map/prefill_attend/pallas_call | solution.py:118
  124.1 2.4 fusion.112
  126.5 0.9 slice_convert_fusion
  128.8 3.7 %convolution_convert_fusion.1 = bf16[24,2304]{1,0:T(8,128)(2,1)} fusion(bf16[1024,2304]{1,0:T(8,128)(2,1)} %param.31, bf16[8,3,8,128]{3,2,1,0:T(8,128)(2,1)S(1)} %fusion.12), kind=kOutput, calls=%fused_computation.1 | convolution fusion | flops 113301504 | bytes 4878336 | tf_op jit(solution)/shard_map/dot_general | solution.py:455
  132.8 17.4 %copy.199 = bf16[2304,3,1024]{0,2,1:T(8,128)(2,1)} copy(bf16[2304,3,1024]{2,0,1:T(8,128)(2,1)} %param.32) | data formatting | bytes 28311552 | tf_op args[12]
  150.2 10.9 %all-to-all-done.1 = bf16[64,8,16,128]{3,2,1,0:T(8,128)(2,1)} async-done(((bf16[64,8,16,128]{3,2,1,0:T(8,128)(2,1)}), bf16[64,8,16,128]{3,2,1,0:T(8,128)(2,1)}, u32[]{:S(2)}, u32[]{:S(2)}) %all-to-all-start.1) | async-done | bytes 2097184 | tf_op jit(solution)/shard_map/all_to_all | solution.py:386
  161.1 2.2 copy.205
  163.3 20.1 %all-reduce.3.cloned.1.call-done = bf16[24,2304]{1,0:T(8,128)(2,1)} async-done(((bf16[24,2304]{1,0:T(8,128)(2,1)}), bf16[24,2304]{1,0:T(8,128)(2,1)}) %all-reduce.3.cloned.1.call-update) | async-done | bytes 110608 | tf_op jit(solution)/shard_map/psum | solution.py:456
  183.4 1.7 fusion.20
  185.1 1.0 multiply_convert_fusion
  186.1 7.0 %fusion.27 = f32[24,3,8,128]{3,0,2,1:T(8,128)S(1)} fusion(bf16[3,8,128,2304]{3,2,1,0:T(8,128)(2,1)} %bitcast.259, bf16[24,2304]{1,0:T(8,128)(2,1)S(1)} %multiply_convert_fusion), kind=kOutput, calls=%fused_computation.55 | convolution fusion | flops 339738624 | bytes 14561280 | tf_op jit(solution)/shard_map/dot_general | solution.py:459
  193.4 1.3 convolution_bitcast_fusion
  195.1 1.2 fusion.25
  197.5 3.3 %convolution_convert_fusion = bf16[24,2304]{1,0:T(8,128)(2,1)S(1)} fusion(bf16[1024,2304]{1,0:T(8,128)(2,1)} %param.39, bf16[24,128]{1,0:T(8,128)(2,1)S(1)} %convolution_convert_fusion.3, bf16[128,1024]{1,0:T(8,128)(2,1)} %param.37, f32[3,8,8,128]{3,2,1,0:T(8,128)S(1)} %bitcast.266, f32[1,8,8,128]{3,1,2,0:T(8,128)S(1)} %get-tuple-element.46, ...), kind=kOutput, calls=%fused_computation | convolution fusion | flops 119789568 | bytes 5294080 | tf_op jit(solution)/shard_map/dot_general | solution.py:506
  200.8 1.1 copy.221
  202.0 2.5 copy.219
  204.5 21.1 %reduce-scatter.9.cloned.1.call-done = bf16[576,24]{1,0:T(8,128)(2,1)} async-done(((bf16[2304,24]{1,0:T(8,128)(2,1)}), bf16[576,24]{1,0:T(8,128)(2,1)}) %reduce-scatter.9.cloned.1.call-update) | async-done | bytes 27664
  225.6 1.0 copy.222
  226.6 1.6 fusion.76
  228.2 25.7 %reduce-scatter.7.cloned.1.call-done = bf16[576,256]{1,0:T(8,128)(2,1)} async-done(((bf16[2304,256]{1,0:T(8,128)(2,1)}), bf16[576,256]{1,0:T(8,128)(2,1)}) %reduce-scatter.7.cloned.1.call-update) | async-done | bytes 294928
  253.9 1.2 copy.220
  255.1 1.2 add_convert_fusion
  256.3 0.9 copy.215
  (141 shorter events, 6.9 us)
Async XLA Ops:
  7.2 5.7 %copy-start = (bf16[2304,576]{0,1:T(8,128)(2,1)S(1)}, bf16[2304,576]{0,1:T(8,128)(2,1)}, u32[]{:S(2)}) copy-start(bf16[2304,576]{0,1:T(8,128)(2,1)} %param.28) | copy-start | bytes 7962628
  7.2 4.4 %copy-start.12 = (bf16[3,8,2304]{2,1,0:T(8,128)(2,1)S(1)}, bf16[3,8,2304]{2,1,0:T(8,128)(2,1)}, u32[]{:S(2)}) copy-start(bf16[3,8,2304]{2,1,0:T(8,128)(2,1)} %param.21) | copy-start | bytes 331780
  7.2 81.2 %all-gather.2.cloned.1.call-start = ((), (), s32[]{:S(2)}) async-start(), calls=%async_computation.4 | async-start | bytes 2703360 | tf_op jit(solution)/shard_map/all_gather | solution.py:368
  11.6 2.5 copy-start.18
  11.7 3.6 %copy-start.17 = (s32[8,1,12]{2,1,0:T(1,128)S(1)}, s32[8,1,12]{2,1,0:T(1,128)}, u32[]{:S(2)}) copy-start(s32[8,1,12]{2,1,0:T(1,128)} %param.24) | copy-start | bytes 1156
  11.7 3.7 %copy-start.19 = (s32[8,1]{0,1:T(1,128)S(1)}, s32[8,1]{0,1:T(1,128)}, u32[]{:S(2)}) copy-start(s32[8,1]{0,1:T(1,128)} %param.25) | copy-start | bytes 100
  14.6 35.6 %copy-start.15 = (bf16[88,576]{1,0:T(8,128)(2,1)}, bf16[88,576]{1,0:T(8,128)(2,1)S(1)}, u32[]{:S(2)}) copy-start(bf16[88,576]{1,0:T(8,128)(2,1)S(1)} %pad_maximum_fusion.3) | copy-start | bytes 304132
  47.3 1.3 copy-start.9
  48.5 1.7 copy-start.5
  48.6 11.9 %slice-start = ((s8[7864320]{0:T(1024)(128)(4,1)}), s8[4194304]{0:T(1024)(128)(4,1)S(1)}, s32[]{:S(2)}) async-start(s8[7864320]{0:T(1024)(128)(4,1)} %bitcast.256), calls=%async_computation.8 | async-start | bytes 8388608
  50.2 10.3 %copy-start.2 = (bf16[512,1024]{1,0:T(8,128)(2,1)S(1)}, bf16[512,1024]{1,0:T(8,128)(2,1)}, u32[]{:S(2)}) copy-start(bf16[512,1024]{1,0:T(8,128)(2,1)} %value_ref.1) | copy-start | bytes 3145732
  50.3 10.3 %slice-start.1 = ((s8[7864320]{0:T(1024)(128)(4,1)}), s8[3670016]{0:T(1024)(128)(4,1)S(1)}, s32[]{:S(2)}) async-start(s8[7864320]{0:T(1024)(128)(4,1)} %bitcast.256), calls=%async_computation.9 | async-start | bytes 7340032
  59.5 1.0 copy-start.7
  69.9 1.5 copy-start.3
  88.4 20.6 %all-to-all-start = ((bf16[8,32,1152]{2,1,0:T(8,128)(2,1)}), bf16[8,32,1152]{2,1,0:T(8,128)(2,1)S(1)}, u32[]{:S(2)}, u32[]{:S(2)}) async-start(bf16[8,32,1152]{2,1,0:T(8,128)(2,1)} %bitcast.8), calls=%async_computation | async-start | bytes 1179648 | tf_op jit(solution)/shard_map/all_to_all | solution.py:416
  109.0 4.4 %copy-start.10 = (bf16[8,32,1152]{2,1,0:T(8,128)(2,1)}, bf16[8,32,1152]{2,1,0:T(8,128)(2,1)S(1)}, u32[]{:S(2)}) copy-start(bf16[8,32,1152]{2,1,0:T(8,128)(2,1)S(1)} %all-to-all-done) | copy-start | bytes 1769476
  109.0 52.2 %all-to-all-start.1 = ((bf16[64,8,16,128]{3,2,1,0:T(8,128)(2,1)}), bf16[64,8,16,128]{3,2,1,0:T(8,128)(2,1)}, u32[]{:S(2)}, u32[]{:S(2)}) async-start(bf16[64,8,16,128]{3,2,1,0:T(8,128)(2,1)} %convert_element_type.125), calls=%async_computation.1 | async-start | bytes 4194304 | tf_op jit(solution)/shard_map/all_to_all | solution.py:386
  113.3 70.0 %all-reduce.3.cloned.1.call-start = ((), (), s32[]{:S(2)}) async-start(), calls=%async_computation.5 | async-start | bytes 221184 | tf_op jit(solution)/shard_map/psum | solution.py:456
  113.4 10.7 %slice-start.2 = ((s8[4718592]{0:T(1024)(128)(4,1)}), s8[524288]{0:T(1024)(128)(4,1)S(1)}, s32[]{:S(2)}) async-start(s8[4718592]{0:T(1024)(128)(4,1)} %bitcast.263), calls=%async_computation.10 | async-start | bytes 1048576
  116.5 1.7 copy-start.4
  118.2 1.2 copy-start.6
  119.4 1.2 copy-start.8
  120.6 3.5 %slice-start.3 = ((s8[4718592]{0:T(1024)(128)(4,1)}), s8[4194304]{0:T(1024)(128)(4,1)S(1)}, s32[]{:S(2)}) async-start(s8[4718592]{0:T(1024)(128)(4,1)} %bitcast.263), calls=%async_computation.11 | async-start | bytes 8388608
  126.5 1.9 copy-start.11
  128.8 4.0 %copy-start.20 = (f32[8]{0:T(128)S(1)}, f32[8]{0:T(128)}, u32[]{:S(2)}) copy-start(f32[8]{0:T(128)} %param.38) | copy-start | bytes 100
  132.6 93.0 %reduce-scatter.9.cloned.1.call-start = ((), (), s32[]{:S(2)}) async-start(), calls=%async_computation.7 | async-start | bytes 737280
  186.1 7.3 %copy-start.14 = (bf16[2304,128]{1,0:T(8,128)(2,1)S(1)}, bf16[2304,128]{1,0:T(8,128)(2,1)}, u32[]{:S(2)}) copy-start(bf16[2304,128]{1,0:T(8,128)(2,1)} %param.34) | copy-start | bytes 1769476
  194.7 1.7 copy-start.16
  194.7 2.4 copy-start.13
  201.9 55.2 %copy-start.1 = (bf16[2304,576]{0,1:T(8,128)(2,1)S(1)}, bf16[2304,576]{0,1:T(8,128)(2,1)}, u32[]{:S(2)}) copy-start(bf16[2304,576]{0,1:T(8,128)(2,1)} %param.28) | copy-start | bytes 7962628
  201.9 52.0 %reduce-scatter.7.cloned.1.call-start = ((), (), s32[]{:S(2)}) async-start(), calls=%async_computation.6 | async-start | bytes 1474560
Sparse Core Ops, SparseCore 0:
  15.4 72.8 all-gather.1
  132.7 50.6 all-reduce.2
  202.0 23.5 reduce-scatter.8
  228.2 25.7 reduce-scatter.6

commit v3 on v2

--- a/solution.py
+++ b/solution.py
@@ -315,6 +315,280 @@
     )(queries, pages, holders, value_expand)
 
 
+def merge_body(reqs, count, came_ref, query_ref, fresh_ref, value_ref, weight_ref, out_ref):
+    owners, each, _ = came_ref.shape
+    heads = query_ref.shape[0]
+    pieces, _, share = out_ref.shape
+    nt = (((1,), (1,)), ((), ()))
+    fresh = fresh_ref[...]
+    values = jnp.dot(fresh[:, :LAT], value_ref[...], preferred_element_type=jnp.float32)
+    values = values.astype(jnp.bfloat16)
+    row = lax.broadcasted_iota(jnp.int32, (each, each), 0)
+    col = lax.broadcasted_iota(jnp.int32, (each, each), 1)
+    live = (lax.rem(row, reqs) == lax.rem(col, reqs)) & (col <= row) & (col < count)
+    logs = [came_ref[s, :, heads * VH :].astype(jnp.float32) for s in range(owners)]
+    results = []
+    for h in range(heads):
+        scores = lax.dot_general(query_ref[h], fresh, nt, preferred_element_type=jnp.float32)
+        scores = jnp.where(live, scores * (NOPE + ROPE) ** (-0.5), masked_score)
+        log = [g[:, h : h + 1] + g[:, heads + h : heads + h + 1] for g in logs]
+        top = jnp.max(scores, axis=1, keepdims=True)
+        for one in log:
+            top = jnp.maximum(top, one)
+        weights = jnp.where(live, jnp.exp(scores - top), 0.0)
+        total = jnp.sum(weights, axis=1, keepdims=True)
+        cut = slice(h * VH, (h + 1) * VH)
+        mixed = jnp.dot(
+            weights.astype(jnp.bfloat16), values[:, cut], preferred_element_type=jnp.float32
+        )
+        for s in range(owners):
+            factor = jnp.exp(log[s] - top)
+            total = total + factor
+            mixed = mixed + factor * came_ref[s, :, cut].astype(jnp.float32)
+        results.append((mixed / total).astype(jnp.bfloat16))
+    part = jnp.dot(
+        jnp.concatenate(results, axis=1), weight_ref[...], preferred_element_type=jnp.float32
+    )
+    for p in range(pieces):
+        out_ref[p] = part[:, p * share : (p + 1) * share].astype(out_ref.dtype)
+
+
+def merge_parts(reqs, count, pieces, came, queries, fresh, value_expand, mla_output):
+    each = came.shape[1]
+    share = mla_output.shape[1] // pieces
+    return pl.pallas_call(
+        functools.partial(merge_body, reqs, count),
+        out_shape=jax.ShapeDtypeStruct((pieces, each, share), jnp.bfloat16),
+        in_specs=[pl.BlockSpec(memory_space=pltpu.VMEM)] * 5,
+        out_specs=pl.BlockSpec(memory_space=pltpu.VMEM),
+        compiler_params=pltpu.CompilerParams(vmem_limit_bytes=40 * 1024 * 1024),
+        name="merge_parts",
+    )(came, queries, fresh, value_expand, mla_output)
+
+
+def sum_body(members, gather, part_ref, *refs):
+    if gather:
+        out_ref, came, send_sem, recv_sem, send_back, recv_back = refs
+    else:
+        base_ref, out_ref, came, send_sem, recv_sem = refs
+    me = lax.axis_index("grp")
+    peers = [lax.rem(me + step, members) for step in range(members)]
+    barrier = pltpu.get_barrier_semaphore()
+    for peer in peers[1:]:
+        pl.semaphore_signal(
+            barrier, inc=1, device_id={"grp": peer}, device_id_type=pl.DeviceIdType.MESH
+        )
+    pl.semaphore_wait(barrier, members - 1)
+    copies = []
+    for step in range(1, members):
+        copies.append(
+            pltpu.make_async_remote_copy(
+                src_ref=part_ref.at[peers[step]],
+                dst_ref=came.at[step],
+                send_sem=send_sem.at[step],
+                recv_sem=recv_sem.at[step],
+                device_id={"grp": peers[step]},
+                device_id_type=pl.DeviceIdType.MESH,
+            )
+        )
+        copies[-1].start()
+    total = part_ref[me].astype(jnp.float32)
+    for step in range(1, members):
+        copies[step - 1].wait()
+        total = total + came[step].astype(jnp.float32)
+    if not gather:
+        out_ref[...] = (base_ref[...] + total).astype(out_ref.dtype)
+        return
+    out_ref[me] = total.astype(out_ref.dtype)
+    copies = []
+    for step in range(1, members):
+        copies.append(
+            pltpu.make_async_remote_copy(
+                src_ref=out_ref.at[me],
+                dst_ref=out_ref.at[me],
+                send_sem=send_back.at[step],
+                recv_sem=recv_back.at[step],
+                device_id={"grp": peers[step]},
+                device_id_type=pl.DeviceIdType.MESH,
+            )
+        )
+        copies[-1].start()
+    for copy in copies:
+        copy.wait()
+
+
+def sum_over_grp(parts, base=None):
+    members, rows, share = parts.shape
+    gather = base is None
+    sems = [pltpu.SemaphoreType.DMA((members,))] * (4 if gather else 2)
+    operands = (parts,) if gather else (parts, base)
+    return pl.pallas_call(
+        functools.partial(sum_body, members, gather),
+        out_shape=jax.ShapeDtypeStruct(parts.shape if gather else (rows, share), jnp.bfloat16),
+        in_specs=[pl.BlockSpec(memory_space=pltpu.VMEM)] * len(operands),
+        out_specs=pl.BlockSpec(memory_space=pltpu.VMEM),
+        scratch_shapes=[pltpu.VMEM(parts.shape, jnp.bfloat16)] + sems,
+        compiler_params=pltpu.CompilerParams(
+            collective_id=1 if gather else 2, has_side_effects=True
+        ),
+        name="sum_hidden" if gather else "sum_output",
+    )(*operands)
+
+
+def delta_body(
+    steps,
+    reqs,
+    hidden_ref,
+    input_ref,
+    beta_ref,
+    decay_down_ref,
+    decay_up_ref,
+    gate_down_ref,
+    gate_up_ref,
+    rate_ref,
+    state_ref,
+    output_ref,
+    out_ref,
+    kin,
+    decay_low,
+    gate_low,
+    betas,
+    total,
+):
+    turn = pl.program_id(0)
+    sources, _, pair, _, _ = state_ref.shape
+    each = hidden_ref.shape[0]
+    pieces, _, share = out_ref.shape
+    f32, bf16 = jnp.float32, jnp.bfloat16
+    nt = (((1,), (1,)), ((), ()))
+
+    @pl.when(turn == 0)
+    def _():
+        kin[...] = norm_rows(hidden_ref[...]).astype(bf16)
+        rows = kin[...]
+        decay_low[...] = jnp.dot(rows, decay_down_ref[...], preferred_element_type=f32).astype(bf16)
+        gate_low[...] = jnp.dot(rows, gate_down_ref[...], preferred_element_type=f32).astype(bf16)
+        betas[...] = jax.nn.sigmoid(jnp.dot(rows, beta_ref[...], preferred_element_type=f32))
+        total[...] = jnp.zeros_like(total)
+
+    rows = kin[...]
+    query, key, value = [jnp.dot(rows, input_ref[i], preferred_element_type=f32) for i in range(3)]
+    raw = jnp.dot(decay_low[...], decay_up_ref[...], preferred_element_type=f32)
+    soft = jnp.maximum(raw, 0.0) + jnp.log1p(jnp.exp(-jnp.abs(raw)))
+    decays = jnp.exp(-rate_ref[...] * soft)
+    gate = jax.nn.sigmoid(jnp.dot(gate_low[...], gate_up_ref[...], preferred_element_type=f32))
+    lane = lax.broadcasted_iota(jnp.int32, betas.shape, 1)
+    owner_row = lax.rem(lax.broadcasted_iota(jnp.int32, (2 * steps * reqs, 1), 0), reqs)
+    results = []
+    for h in range(pair):
+        cut = slice(h * DK, (h + 1) * DK)
+        beta = jnp.sum(
+            jnp.where(lane == turn * pair + h, betas[...], 0.0), axis=1, keepdims=True
+        )
+        units = (unit_rows(key[:, cut]), unit_rows(query[:, cut]) * DK ** (-0.5))
+        at = [slice(t * reqs, (t + 1) * reqs) for t in range(steps)]
+        keys = [units[0][a] for a in at]
+        queries = [units[1][a] for a in at]
+        decay = [decays[a, cut] for a in at]
+        grown = [decay[0]]
+        for t in range(1, steps):
+            grown.append(grown[-1] * decay[t])
+        looks = jnp.concatenate(
+            [keys[t] * grown[t] for t in range(steps)]
+            + [queries[t] * grown[t] for t in range(steps)],
+            axis=0,
+        ).astype(bf16)
+        seen = jnp.zeros(looks.shape, f32)
+        for r in range(reqs):
+            state = state_ref[:, r, h].reshape(DV, DK)
+            found = lax.dot_general(looks, state, nt, preferred_element_type=f32)
+            seen = jnp.where(owner_row == r, found, seen)
+        written = []
+        reads = []
+        for t in range(steps):
+            if t:
+                written = [(e, k * decay[t]) for e, k in written]
+            err = value[at[t], cut] - seen[t * reqs : (t + 1) * reqs]
+            for e, k in written:
+                err = err - e * jnp.sum(k * keys[t], axis=1, keepdims=True)
+            written.append((beta[at[t]] * err, keys[t]))
+            read = seen[(steps + t) * reqs : (steps + t + 1) * reqs]
+            for e, k in written:
+                read = read + e * jnp.sum(k * queries[t], axis=1, keepdims=True)
+            reads.append(norm_rows(read) * gate[at[t], cut])
+        reads.append(jnp.zeros((each - steps * reqs, DV), f32))
+        results.append(jnp.concatenate(reads, axis=0).astype(bf16))
+    total[...] += jnp.dot(
+        jnp.concatenate(results, axis=1), output_ref[...], preferred_element_type=f32
+    )
+
+    @pl.when(turn == pl.num_programs(0) - 1)
+    def _():
+        for p in range(pieces):
+            out_ref[p] = total[:, p * share : (p + 1) * share].astype(out_ref.dtype)
+
+
+def delta_steps(
+    steps,
+    reqs,
+    pieces,
+    hidden,
+    kda_inputs,
+    kda_beta,
+    decay_down,
+    decay_up,
+    gate_down,
+    gate_up,
+    rate,
+    states,
+    kda_output,
+):
+    each, width = hidden.shape
+    heads = kda_beta.shape[1]
+    pair = 2
+    sources, _, _, part, _ = states.shape
+    whole = lambda h: (0, 0)
+    wide = lambda h: (0, h)
+    return pl.pallas_call(
+        functools.partial(delta_body, steps, reqs),
+        out_shape=jax.ShapeDtypeStruct((pieces, each, width // pieces), jnp.bfloat16),
+        grid=(heads // pair,),
+        in_specs=[
+            pl.BlockSpec((each, width), whole),
+            pl.BlockSpec((3, width, pair * DK), lambda h: (0, 0, h)),
+            pl.BlockSpec((width, heads), whole),
+            pl.BlockSpec(decay_down.shape, whole),
+            pl.BlockSpec((decay_up.shape[0], pair * DK), wide),
+            pl.BlockSpec(gate_down.shape, whole),
+            pl.BlockSpec((gate_up.shape[0], pair * DV), wide),
+            pl.BlockSpec((1, pair * DK), wide),
+            pl.BlockSpec((sources, reqs, pair, part, DK), lambda h: (0, 0, h, 0, 0)),
+            pl.BlockSpec((pair * DV, width), lambda h: (h, 0)),
+        ],
+        out_specs=pl.BlockSpec((pieces, each, width // pieces), lambda h: (0, 0, 0)),
+        scratch_shapes=[
+            pltpu.VMEM((each, width), jnp.bfloat16),
+            pltpu.VMEM((each, decay_down.shape[1]), jnp.bfloat16),
+            pltpu.VMEM((each, gate_down.shape[1]), jnp.bfloat16),
+            pltpu.VMEM((each, heads), jnp.float32),
+            pltpu.VMEM((each, width), jnp.float32),
+        ],
+        compiler_params=pltpu.CompilerParams(vmem_limit_bytes=40 * 1024 * 1024),
+        name="delta_steps",
+    )(
+        hidden,
+        kda_inputs,
+        kda_beta,
+        decay_down,
+        decay_up,
+        gate_down,
+        gate_up,
+        rate,
+        states,
+        kda_output,
+    )
+
+
 def shards(
     x_group,
     decode_input,
@@ -342,11 +616,9 @@
     grp_index = lax.axis_index("grp")
     owners = lax.axis_size("seq")
     heads = key_expand.shape[1] // NOPE
-    kheads = decay_log.shape[0]
     width = x_group.shape[1]
     share = width // lax.axis_size("grp")
     col = grp_index * share
-    scale = (NOPE + ROPE) ** (-0.5)
     steps, reqs, _ = decode_input.shape
     cap = slot_target.shape[2]
     n = steps * reqs
@@ -383,9 +655,8 @@
     counts = lax.dynamic_slice_in_dim(ints, 2 * reqs + seq_index, 1, 1)
     targets = lax.dynamic_slice_in_dim(ints, 2 * reqs + owners + seq_index * cap, cap, 1)
 
-    states = lax.all_to_all(
-        kda_state.astype(bf16), "seq", split_axis=0, concat_axis=2, tiled=True
-    )
+    states = kda_state.astype(bf16).reshape((owners, reqs) + kda_state.shape[1:])
+    states = lax.all_to_all(states, "seq", split_axis=0, concat_axis=0, tiled=True)
 
     position = seq_index * group_rows + jnp.arange(group_rows)
     dec_place = (lens_all[:, None, :] + jnp.arange(each // reqs)[None, :, None]).reshape(-1)
@@ -422,93 +693,40 @@
     came, prefill_part = lax.optimization_barrier((came, prefill_part))
     attended = lax.psum_scatter(
         prefill_part.astype(bf16), "grp", scatter_dimension=1, tiled=True
-    ).astype(f32)
+    )
+
+    pieces = lax.axis_size("grp")
+    fresh = jnp.pad(fresh, ((0, each - n), (0, 0)))
+    own_query = lax.dynamic_index_in_dim(qc, seq_index, 0, keepdims=False)
+    own_query = own_query.reshape(heads, each, LAT + ROPE)
+    mla_parts = merge_parts(
+        reqs, n, pieces, came, own_query, fresh, value_expand, mla_output
+    )
+    mla_total = sum_over_grp(mla_parts)
+    dec_rows = jnp.pad(dec_own, ((0, each - n), (0, 0))).astype(f32)
+    hidden = dec_rows + mla_total.transpose(1, 0, 2).reshape(each, width).astype(f32)
+
+    kda_parts = delta_steps(
+        steps,
+        reqs,
+        pieces,
+        hidden,
+        kda_inputs.transpose(1, 0, 2),
+        kda_beta,
+        decay_down,
+        decay_up,
+        gate_down,
+        gate_up,
+        jnp.repeat(jnp.exp(decay_log), DK)[None],
+        states,
+        kda_output,
+    )
+    kda_parts, attended = lax.optimization_barrier((kda_parts, attended))
+    decode_out = sum_over_grp(kda_parts, lax.dynamic_slice_in_dim(hidden, col, share, 1))
     prefill_out = (
-        lax.dynamic_slice_in_dim(x_group, col, share, 1).astype(f32) + attended
+        lax.dynamic_slice_in_dim(x_group, col, share, 1).astype(f32) + attended.astype(f32)
     ).astype(bf16)
-
-    came = came[:, :n]
-    own_query = lax.dynamic_index_in_dim(qc, seq_index, 0, keepdims=False)
-    own_query = own_query.reshape(heads, each, LAT + ROPE)[:, :n]
-    fresh_v = jnp.dot(fresh[:, :LAT], value_expand, preferred_element_type=f32).astype(bf16)
-    fresh_scores = jnp.einsum("hqc,kc->hqk", own_query, fresh, preferred_element_type=f32) * scale
-    at = jnp.arange(n)
-    fresh_live = (
-        (at[:, None] % reqs == at[None, :] % reqs) & (at[None, :] // reqs <= at[:, None] // reqs)
-    )[None]
-    fresh_scores = jnp.where(fresh_live, fresh_scores, masked_score)
-    lse_came = came[..., heads * VH :].astype(f32)[..., : 2 * heads]
-    lse_came = (lse_came[..., :heads] + lse_came[..., heads:]).transpose(0, 2, 1)
-    top = jnp.maximum(jnp.max(fresh_scores, axis=-1), jnp.max(lse_came, axis=0))
-    fresh_w = jnp.where(fresh_live, jnp.exp(fresh_scores - top[..., None]), 0.0)
-    came_w = jnp.exp(lse_came - top[None])
-    total = jnp.sum(fresh_w, axis=-1) + jnp.sum(came_w, axis=0)
-    mixed = jnp.einsum(
-        "hqk,khv->qhv",
-        fresh_w.astype(bf16),
-        fresh_v.reshape(n, heads, VH),
-        preferred_element_type=f32,
-    )
-    parts = came[..., : heads * VH].astype(f32).reshape(owners, n, heads, VH)
-    mixed = mixed + jnp.sum(parts * came_w.transpose(0, 2, 1)[..., None], axis=0)
-    head_values = (mixed / total.T[..., None]).astype(bf16).reshape(n, heads * VH)
-    mla_part = jnp.dot(head_values, mla_output, preferred_element_type=f32)
-    hidden = dec_own.astype(f32) + lax.psum(mla_part.astype(bf16), "grp").astype(f32)
-
-    kda_in = norm_rows(hidden).astype(bf16)
-    projected = jnp.dot(
-        kda_in, kda_inputs.reshape(width, -1), preferred_element_type=f32
-    ).reshape(n, 3, kheads, DK)
-    split = (steps, reqs, kheads, DK)
-    queries_kda = (unit_rows(projected[:, 0]) * DK ** (-0.5)).reshape(split)
-    keys_kda = unit_rows(projected[:, 1]).reshape(split)
-    values_kda = projected[:, 2].reshape(split)
-    beta = jax.nn.sigmoid(jnp.dot(kda_in, kda_beta, preferred_element_type=f32))
-    beta = beta.reshape(steps, reqs, kheads, 1)
-    decay_low = jnp.dot(kda_in, decay_down, preferred_element_type=f32).astype(bf16)
-    decays = jnp.exp(
-        -jnp.exp(decay_log)[None, :, None]
-        * jax.nn.softplus(
-            jnp.dot(decay_low, decay_up, preferred_element_type=f32).reshape(n, kheads, DK)
-        )
-    ).reshape(split)
-    gate_low = jnp.dot(kda_in, gate_down, preferred_element_type=f32).astype(bf16)
-    out_gate = jax.nn.sigmoid(
-        jnp.dot(gate_low, gate_up, preferred_element_type=f32).reshape(n, kheads, DV)
-    )
-    decayed = decays[0]
-    looks = []
-    for t in range(steps):
-        if t:
-            decayed = decayed * decays[t]
-        looks += [keys_kda[t] * decayed, queries_kda[t] * decayed]
-    seen = jnp.einsum(
-        "rhxk,rhvk->rhxv",
-        jnp.stack(looks, axis=2).astype(bf16),
-        states,
-        preferred_element_type=f32,
-    )
-    written = []
-    reads = []
-    for t in range(steps):
-        if t:
-            written = [(e, k * decays[t]) for e, k in written]
-        err = values_kda[t] - seen[:, :, 2 * t]
-        for e, k in written:
-            err = err - e * jnp.sum(k * keys_kda[t], axis=-1, keepdims=True)
-        written.append((beta[t] * err, keys_kda[t]))
-        read = seen[:, :, 2 * t + 1]
-        for e, k in written:
-            read = read + e * jnp.sum(k * queries_kda[t], axis=-1, keepdims=True)
-        reads.append(read)
-    readout = jnp.stack(reads).reshape(n, kheads, DV)
-    blended = (norm_rows(readout) * out_gate).astype(bf16).reshape(n, kheads * DV)
-    kda_part = jnp.dot(blended, kda_output, preferred_element_type=f32)
-    kda_share = lax.psum_scatter(
-        kda_part.astype(bf16), "grp", scatter_dimension=1, tiled=True
-    ).astype(f32)
-    decode_out = (lax.dynamic_slice_in_dim(hidden, col, share, 1) + kda_share).astype(bf16)
-    return (prefill_out, decode_out.reshape(steps, reqs, share))
+    return (prefill_out, decode_out[:n].reshape(steps, reqs, share))
 
 
 def solution(mesh):

time: 265 us -> 216 us (0.82)
  the two profiles are of different devices: /device:TPU:0 before, /device:TPU:31 now
where the time goes in v3:
time: 216 us; the launch traced here: 214 us
  Pallas kernels  107 us (50%)
  local copies, waits for them, and re-layouts  40.4 us (19%)
  waiting for transfers between devices  20.1 us (9%)
  other arithmetic  17.9 us (8%)
  between operations  14.5 us (7%)
  starting transfers between devices  10.9 us (5%)
  matrix products  3.36 us (2%)
    pallas_call x1, Pallas kernels, gather_rows(): pl.pallas_call(functools.partial(gather_body, owners), out_shape=jax.Shap...  32.4 us
    unnamed x70, local copies, waits for them, and re-layouts  30.1 us
    pallas_call x1, Pallas kernels, prefill_attend(): pl.pallas_call(prefill_body, out_shape=jax.ShapeDtypeStruct((group_rows,...  23.7 us
    pallas_call x2, Pallas kernels, sum_over_grp(): pl.pallas_call(functools.partial(sum_body, members, gather), out_shape=ja...  18.9 us
    all_to_all x1, waiting for transfers between devices, shards(): lax.all_to_all(sent.reshape(owners, each, -1), 'seq', split_axis=0, conca...  10.3 us
    all_gather x1, waiting for transfers between devices, shards(): lax.all_gather(latents[:rows_share], ('seq', 'grp'), axis=0, tiled=True)  9.76 us
    pallas_call x1, Pallas kernels, delta_steps(): pl.pallas_call(functools.partial(delta_body, steps, reqs), out_shape=jax....  9.59 us
    pallas_call x1, Pallas kernels, attend_pages(): pl.pallas_call(functools.partial(page_body, reqs), out_shape=jax.ShapeDty...  9.46 us
  transfers between devices with their start and end apart: 4, of which 2 were waited for; matrix products, arithmetic and copies ran while one was open for 11% of the time, Pallas kernels for 47%

profile of v3, /device:TPU:31, one launch (start us, length us, event | category | flops | bytes accessed | tf_op | source)
XLA Modules:
  0.0 214.4 jit_solution(14260700075135589016)
XLA Ops:
  7.3 1.2 multiply_reduce_fusion
  8.5 1.0 multiply_convert_fusion
  9.5 1.6 fusion
  11.1 2.6 %fusion.1 = bf16[256,2304]{1,0:T(8,128)(2,1)} fusion(bf16[256,2304]{1,0:T(8,128)(2,1)} %param.20, f32[256]{0:T(256)S(1)} %add_rsqrt_fusion.1), kind=kLoop, calls=%fused_computation.3 | loop fusion | flops 1769472 | bytes 2360320 | tf_op jit(solution)/shard_map/convert_element_type | solution.py:629
  13.8 1.0 constant_dynamic-slice_fusion.2
  14.8 0.9 fusion.2
  18.1 32.4 %gather_rows.1 = bf16[256,2304]{1,0:T(8,128)(2,1)} custom-call(bf16[32,2304]{1,0:T(8,128)(2,1)} %maximum_maximum_fusion.own_ref), custom_call_target="tpu_custom_call" | custom-call | tf_op jit(solution)/shard_map/gather_rows/pallas_call | solution.py:181
  52.8 1.0 fusion.6
  54.1 1.6 pad_maximum_fusion.rows_ref
  55.7 9.1 %make_queries.1 = (bf16[8,256,192]{2,1,0:T(8,128)(2,1)S(1)}, bf16[8,256,576]{2,1,0:T(8,128)(2,1)S(1)}) custom-call(bf16[512,2304]{1,0:T(8,128)(2,1)S(1)} %pad_maximum_fusion.rows_ref, bf16[2304,1536]{1,0:T(8,128)(2,1)} %weight_ref.2, bf16[512,1024]{1,0:T(8,128)(2,1)S(1)} %copy-done.19, f32[512,64]{1,0:T(8,128)S(1)} %get-tuple-element.41.cos_ref, ...), custom_call_target="tpu_custom_call" | custom-call | flops 3623878656 | bytes 9437184 | tf_op jit(solution)/shard_map/make_queries/pallas_call | solution.py:224
  64.9 1.1 copy-done.21
  66.0 9.5 %attend_pages.1 = bf16[256,1152]{1,0:T(8,128)(2,1)} custom-call(bf16[8,256,576]{2,1,0:T(8,128)(2,1)S(1)} %get-tuple-element.12.query_ref, bf16[8,768,576]{2,1,0:T(8,128)(2,1)S(1)} %bitcast.51, s32[8,1,768]{2,1,0:T(1,128)S(1)} %and_select_fusion.holder_ref, bf16[512,1024]{1,0:T(8,128)(2,1)S(1)} %copy-done.6), custom_call_target="tpu_custom_call" | custom-call | flops 3623878656 | bytes 7077888 | tf_op jit(solution)/shard_map/attend_pages/pallas_call | solution.py:293
  75.4 1.5 copy-done.17
  76.9 9.8 %all-gather.2.cloned.1.call-done.rows_ref = bf16[2048,576]{1,0:T(8,128)(2,1)} async-done(((bf16[64,576]{1,0:T(8,128)(2,1)}), bf16[2048,576]{1,0:T(8,128)(2,1)}) %all-gather.2.cloned.1.call-update) | async-done | bytes 2359312 | tf_op jit(solution)/shard_map/all_gather | solution.py:640
  86.7 5.5 %all-to-all-start = ((bf16[8,32,1152]{2,1,0:T(8,128)(2,1)}), bf16[8,32,1152]{2,1,0:T(8,128)(2,1)S(1)}, u32[]{:S(2)}, u32[]{:S(2)}) async-start(bf16[8,32,1152]{2,1,0:T(8,128)(2,1)} %bitcast.8), calls=%async_computation | async-start | bytes 1179648 | tf_op jit(solution)/shard_map/all_to_all | solution.py:687
  92.2 3.9 %convert_element_type.84 = bf16[64,8,16,128]{3,2,1,0:T(8,128)(2,1)} convert(f32[64,8,16,128]{3,2,1,0:T(8,128)} %param.26) | non-fusion elementwise | flops 1048576 | bytes 6291456 | tf_op jit(solution)/shard_map/convert_element_type | solution.py:658
  96.1 10.3 %all-to-all-done.came_ref = bf16[8,32,1152]{2,1,0:T(8,128)(2,1)S(1)} async-done(((bf16[8,32,1152]{2,1,0:T(8,128)(2,1)}), bf16[8,32,1152]{2,1,0:T(8,128)(2,1)S(1)}, u32[]{:S(2)}, u32[]{:S(2)}) %all-to-all-start) | async-done | bytes 589856 | tf_op jit(solution)/shard_map/all_to_all | solution.py:687
  107.2 5.4 %all-to-all-start.1 = ((bf16[8,8,8,16,128]{4,3,2,1,0:T(8,128)(2,1)}), bf16[8,8,8,16,128]{4,3,2,1,0:T(8,128)(2,1)S(1)}, u32[]{:S(2)}, u32[]{:S(2)}) async-start(bf16[8,8,8,16,128]{4,3,2,1,0:T(8,128)(2,1)} %bitcast.53), calls=%async_computation.1 | async-start | bytes 4194304 | tf_op jit(solution)/shard_map/all_to_all | solution.py:659
  112.7 2.3 %copy.62 = bf16[512,1024]{0,1:T(8,128)(2,1)} copy(bf16[512,1024]{1,0:T(8,128)(2,1)} %value_ref.3) | data formatting | bytes 2097152 | tf_op args[10]
  115.0 1.2 copy-done.10
  116.2 1.7 copy-done.18
  118.0 1.2 copy-done.20
  119.2 1.2 copy-done.22
  120.4 23.7 %prefill_attend.1 = bf16[256,1024]{1,0:T(8,128)(2,1)S(1)} custom-call(s32[1]{0:T(128)} %bitcast.9.place_ref, bf16[8,256,192]{2,1,0:T(8,128)(2,1)S(1)} %copy-done.22, bf16[2048,576]{1,0:T(8,128)(2,1)S(1)} %copy-done.18, bf16[512,1024]{1,0:T(8,128)(2,1)S(1)} %copy-done.20, bf16[1024,512]{1,0:T(8,128)(2,1)S(1)} %bitcast.47), custom_call_target="tpu_custom_call" | custom-call | flops 4294967296 | bytes 4718592 | tf_op jit(solution)/shard_map/prefill_attend/pallas_call | solution.py:118
  144.2 2.4 %fusion.30 = bf16[256,2304]{1,0:T(8,128)(2,1)} fusion(bf16[256,1024]{1,0:T(8,128)(2,1)S(1)} %prefill_attend.1, bf16[1024,2304]{1,0:T(8,128)(2,1)S(1)} %bitcast.45), kind=kOutput, calls=%fused_computation.82 | convolution fusion | flops 1207959552 | bytes 6422528 | tf_op jit(solution)/shard_map/dot_general | solution.py:692
  146.6 2.4 %copy.66 = bf16[256,2304]{0,1:T(8,128)(2,1)} copy(bf16[256,2304]{1,0:T(8,128)(2,1)} %fusion.30) | data formatting | bytes 2359296
  149.5 1.0 constant_dynamic-slice_fusion.1
  150.5 2.3 %copy-done.5 = bf16[1024,2304]{1,0:T(8,128)(2,1)S(1)} copy-done((bf16[1024,2304]{1,0:T(8,128)(2,1)S(1)}, bf16[1024,2304]{1,0:T(8,128)(2,1)}, u32[]{:S(2)}) %copy-start.5) | copy-done | bytes 4718616
  152.8 1.2 copy-done.7
  154.0 1.1 copy-done.9
  155.1 4.0 %merge_parts.1.part_ref = bf16[4,32,576]{2,1,0:T(8,128)(2,1)S(1)} custom-call(bf16[8,32,1152]{2,1,0:T(8,128)(2,1)S(1)} %copy-done.9, bf16[8,32,576]{2,1,0:T(8,128)(2,1)S(1)} %bitcast.46, bf16[32,576]{1,0:T(8,128)(2,1)S(1)} %pad.14.fresh_ref, bf16[512,1024]{1,0:T(8,128)(2,1)S(1)} %copy-done.7, bf16[1024,2304]{1,0:T(8,128)(2,1)S(1)} %copy-done.5), custom_call_target="tpu_custom_call" | custom-call | tf_op jit(solution)/shard_map/merge_parts/pallas_call | solution.py:359
  159.8 13.0 %sum_hidden.1 = bf16[4,32,576]{2,1,0:T(8,128)(2,1)} custom-call(bf16[4,32,576]{2,1,0:T(8,128)(2,1)} %copy-done.12), custom_call_target="tpu_custom_call" | custom-call | tf_op jit(solution)/shard_map/sum_hidden/pallas_call | solution.py:425
  172.8 0.9 convert_bitcast_fusion
  173.7 0.9 copy.63
  174.6 1.2 reshape.233
  175.9 0.9 convert_add_fusion.hidden_ref
  176.8 1.3 copy-done.2
  178.2 1.6 copy-done.3
  179.8 2.3 %copy-done.4 = bf16[1024,2304]{1,0:T(8,128)(2,1)S(1)} copy-done((bf16[1024,2304]{1,0:T(8,128)(2,1)S(1)}, bf16[1024,2304]{1,0:T(8,128)(2,1)}, u32[]{:S(2)}) %copy-start.4) | copy-done | bytes 4718616
  182.1 1.1 copy-done.13
  183.2 1.1 copy-done.14
  184.3 0.9 copy-done.15
  185.2 0.9 copy-done.16
  186.2 9.6 %delta_steps.1.part_ref = bf16[4,32,576]{2,1,0:T(8,128)(2,1)S(1)} custom-call(f32[32,2304]{1,0:T(8,128)S(1)} %convert_add_fusion.hidden_ref, bf16[3,2304,1024]{2,1,0:T(8,128)(2,1)} %bitcast.52, bf16[2304,8]{1,0:T(8,128)(2,1)S(1)} %copy.64.beta_ref, bf16[2304,128]{1,0:T(8,128)(2,1)S(1)} %copy-done.13, bf16[128,1024]{1,0:T(8,128)(2,1)S(1)} %copy-done.15, ...), custom_call_target="tpu_custom_call" | custom-call | tf_op jit(solution)/shard_map/delta_steps/pallas_call | solution.py:552
  197.1 1.2 copy.67
  198.3 1.1 add_convert_fusion
  200.3 5.9 %sum_output.1 = bf16[32,576]{1,0:T(8,128)(2,1)} custom-call(bf16[4,32,576]{2,1,0:T(8,128)(2,1)} %copy-done.11, f32[32,576]{1,0:T(8,128)} %constant_dynamic-slice_fusion.refs_0_), custom_call_target="tpu_custom_call" | custom-call | tf_op jit(solution)/shard_map/sum_output/pallas_call | solution.py:425
  206.2 1.4 slice_bitcast_fusion
  (111 shorter events, 9.2 us)
Async XLA Ops:
  7.2 7.6 %copy-start = (bf16[2304,576]{0,1:T(8,128)(2,1)S(1)}, bf16[2304,576]{0,1:T(8,128)(2,1)}, u32[]{:S(2)}) copy-start(bf16[2304,576]{0,1:T(8,128)(2,1)} %param.28) | copy-start | bytes 7962628
  7.2 6.5 %copy-start.26 = (s32[8]{0:T(128)S(1)}, s32[8]{0:T(128)}, u32[]{:S(2)}) copy-start(s32[8]{0:T(128)} %param.22) | copy-start | bytes 100
  7.2 79.5 %all-gather.2.cloned.1.call-start = ((), (), s32[]{:S(2)}) async-start(), calls=%async_computation.3 | async-start | bytes 2703360 | tf_op jit(solution)/shard_map/all_gather | solution.py:640
  13.8 3.3 %copy-start.25 = (s32[8,1,12]{2,1,0:T(1,128)S(1)}, s32[8,1,12]{2,1,0:T(1,128)}, u32[]{:S(2)}) copy-start(s32[8,1,12]{2,1,0:T(1,128)} %param.24) | copy-start | bytes 1156
  13.8 3.4 %copy-start.27 = (s32[8,1]{0,1:T(1,128)S(1)}, s32[8,1]{0,1:T(1,128)}, u32[]{:S(2)}) copy-start(s32[8,1]{0,1:T(1,128)} %param.25) | copy-start | bytes 100
  52.8 1.3 copy-start.23
  53.8 1.9 copy-start.19
  54.1 11.9 %slice-start.2 = ((s8[7864320]{0:T(1024)(128)(4,1)}), s8[4194304]{0:T(1024)(128)(4,1)S(1)}, s32[]{:S(2)}) async-start(s8[7864320]{0:T(1024)(128)(4,1)} %bitcast.49), calls=%async_computation.7 | async-start | bytes 8388608
  55.7 10.3 %copy-start.6 = (bf16[512,1024]{1,0:T(8,128)(2,1)S(1)}, bf16[512,1024]{1,0:T(8,128)(2,1)}, u32[]{:S(2)}) copy-start(bf16[512,1024]{1,0:T(8,128)(2,1)} %value_ref.3) | copy-start | bytes 3145732
  55.7 10.3 %slice-start.3 = ((s8[7864320]{0:T(1024)(128)(4,1)}), s8[3670016]{0:T(1024)(128)(4,1)S(1)}, s32[]{:S(2)}) async-start(s8[7864320]{0:T(1024)(128)(4,1)} %bitcast.49), calls=%async_computation.8 | async-start | bytes 7340032
  64.9 1.1 copy-start.21
  75.4 1.5 copy-start.17
  86.7 19.7 %all-to-all-start = ((bf16[8,32,1152]{2,1,0:T(8,128)(2,1)}), bf16[8,32,1152]{2,1,0:T(8,128)(2,1)S(1)}, u32[]{:S(2)}, u32[]{:S(2)}) async-start(bf16[8,32,1152]{2,1,0:T(8,128)(2,1)} %bitcast.8), calls=%async_computation | async-start | bytes 1179648 | tf_op jit(solution)/shard_map/all_to_all | solution.py:687
  106.4 0.8 copy-start.8
  107.2 69.6 %all-to-all-start.1 = ((bf16[8,8,8,16,128]{4,3,2,1,0:T(8,128)(2,1)}), bf16[8,8,8,16,128]{4,3,2,1,0:T(8,128)(2,1)S(1)}, u32[]{:S(2)}, u32[]{:S(2)}) async-start(bf16[8,8,8,16,128]{4,3,2,1,0:T(8,128)(2,1)} %bitcast.53), calls=%async_computation.1 | async-start | bytes 4194304 | tf_op jit(solution)/shard_map/all_to_all | solution.py:659
  112.7 84.5 %reduce-scatter.4.cloned.1.call-start = ((), (), s32[]{:S(2)}) async-start(), calls=%async_computation.4 | async-start | bytes 1474560
  112.7 31.5 %slice-start = ((s8[4718592]{0:T(1024)(128)(4,1)}), s8[524288]{0:T(1024)(128)(4,1)S(1)}, s32[]{:S(2)}) async-start(s8[4718592]{0:T(1024)(128)(4,1)} %bitcast.44), calls=%async_computation.5 | async-start | bytes 1048576
  115.0 1.2 copy-start.10
  116.2 1.7 copy-start.18
  118.0 1.2 copy-start.20
  119.2 1.2 copy-start.22
  120.4 23.7 %slice-start.1 = ((s8[4718592]{0:T(1024)(128)(4,1)}), s8[4194304]{0:T(1024)(128)(4,1)S(1)}, s32[]{:S(2)}) async-start(s8[4718592]{0:T(1024)(128)(4,1)} %bitcast.44), calls=%async_computation.6 | async-start | bytes 8388608
  146.6 2.5 %copy-start.24 = (bf16[2304,8]{0,1:T(8,128)(2,1)S(1)}, bf16[2304,8]{0,1:T(8,128)(2,1)}, u32[]{:S(2)}) copy-start(bf16[2304,8]{0,1:T(8,128)(2,1)} %param.33) | copy-start | bytes 110596
  146.6 2.8 %copy-start.28 = (f32[8]{0:T(128)S(1)}, f32[8]{0:T(128)}, u32[]{:S(2)}) copy-start(f32[8]{0:T(128)} %param.38) | copy-start | bytes 100
  150.5 2.3 %copy-start.5 = (bf16[1024,2304]{1,0:T(8,128)(2,1)S(1)}, bf16[1024,2304]{1,0:T(8,128)(2,1)}, u32[]{:S(2)}) copy-start(bf16[1024,2304]{1,0:T(8,128)(2,1)} %weight_ref.3) | copy-start | bytes 14155780
  152.8 1.2 copy-start.7
  154.0 1.1 copy-start.9
  159.1 0.7 copy-start.12
  176.8 1.4 copy-start.2
  178.2 1.6 copy-start.3
  179.8 2.3 %copy-start.4 = (bf16[1024,2304]{1,0:T(8,128)(2,1)S(1)}, bf16[1024,2304]{1,0:T(8,128)(2,1)}, u32[]{:S(2)}) copy-start(bf16[1024,2304]{1,0:T(8,128)(2,1)} %output_ref.1) | copy-start | bytes 14155780
  182.1 1.1 copy-start.13
  183.2 1.1 copy-start.14
  184.3 0.9 copy-start.15
  185.2 0.9 copy-start.16
  186.2 21.4 %copy-start.1 = (bf16[2304,576]{0,1:T(8,128)(2,1)S(1)}, bf16[2304,576]{0,1:T(8,128)(2,1)}, u32[]{:S(2)}) copy-start(bf16[2304,576]{0,1:T(8,128)(2,1)} %param.28) | copy-start | bytes 7962628
  195.8 0.7 copy-start.11
Sparse Core Ops, SparseCore 0:
  17.1 69.5 all-gather.1
  149.2 28.0 reduce-scatter.3

commit v4 on v3

--- a/solution.py
+++ b/solution.py
@@ -113,7 +113,7 @@
 
 def prefill_attend(seq_index, queries, rows, key_expand, value_expand):
     heads, group_rows, _ = queries.shape
-    pair = 2
+    pair = 4 if heads % 4 == 0 else 2
     row_count = rows.shape[0]
     return pl.pallas_call(
         prefill_body,
@@ -144,52 +144,106 @@
     )(seq_index.reshape(1).astype(jnp.int32), queries, rows, key_expand, value_expand.T)
 
 
-def gather_body(owners, own_ref, all_ref, send_sem, recv_sem, local_sem):
-    me = lax.axis_index("seq")
-    rows = own_ref.shape[0]
+def gather_body(sizes, own_ref, all_ref, *sems):
+    zs, ys, xs, cs = sizes
+    z_send, z_recv, y_send, y_recv, x_send, x_recv, c_send, c_recv, local_sem = sems
+    seq_at, grp_at = lax.axis_index("seq"), lax.axis_index("grp")
+    z, y = seq_at // ys, lax.rem(seq_at, ys)
+    x, c = grp_at // cs, lax.rem(grp_at, cs)
+
+    def seq_of(dz, dy):
+        return lax.rem(z + dz + zs, zs) * ys + lax.rem(y + dy + ys, ys)
+
+    def grp_of(dx, dc):
+        return lax.rem(x + dx + xs, xs) * cs + lax.rem(c + dc + cs, cs)
+
+    z_peers = [{"seq": seq_of(d, 0)} for d in range(zs)]
+    y_peers = [{"seq": seq_of(0, d)} for d in range(ys)]
+    x_peers = [{"grp": grp_of(d, 0)} for d in range(xs)]
+    c_peers = [{"grp": grp_of(0, d)} for d in range(cs)]
+    peers = z_peers[1:] + y_peers[1:] + x_peers[1:] + c_peers[1:]
     barrier = pltpu.get_barrier_semaphore()
-    for step in range(1, owners):
-        peer = lax.rem(me + step, owners)
+    for peer in peers:
         pl.semaphore_signal(
-            barrier, inc=1, device_id={"seq": peer}, device_id_type=pl.DeviceIdType.MESH
+            barrier, inc=1, device_id=peer, device_id_type=pl.DeviceIdType.MESH
         )
-    pl.semaphore_wait(barrier, owners - 1)
-    place = all_ref.at[pl.ds(pl.multiple_of(me * rows, rows), rows)]
-    copies = []
-    for step in range(1, owners):
-        peer = lax.rem(me + step, owners)
-        copies.append(
-            pltpu.make_async_remote_copy(
-                src_ref=own_ref,
-                dst_ref=place,
-                send_sem=send_sem.at[step],
-                recv_sem=recv_sem.at[step],
-                device_id={"seq": peer},
-                device_id_type=pl.DeviceIdType.MESH,
-            )
+    pl.semaphore_wait(barrier, len(peers))
+
+    started = []
+
+    def push(back, peer, send, recv):
+        dz, dy, dx = back
+        place = all_ref.at[seq_of(-dz, -dy), grp_of(-dx, 0)]
+        copy = pltpu.make_async_remote_copy(
+            src_ref=place if any(back) else own_ref,
+            dst_ref=place,
+            send_sem=send,
+            recv_sem=recv,
+            device_id=peer,
+            device_id_type=pl.DeviceIdType.MESH,
         )
-        copies[-1].start()
-    local = pltpu.make_async_copy(own_ref, place, local_sem)
+        copy.start()
+        started.append(copy)
+        return copy
+
+    by_z, by_y, by_x, by_c = {}, {}, {}, {}
+
+    def across(dz, dy):
+        for d in range(1, xs):
+            at = (d, dz, dy)
+            by_x[at] = push((dz, dy, 0), x_peers[d], x_send.at[at], x_recv.at[at])
+        to_core(0, dz, dy)
+
+    def to_core(dx, dz, dy):
+        for d in range(1, cs):
+            at = (dx, dz, dy)
+            by_c[(d,) + at] = push((dz, dy, dx), c_peers[d], c_send.at[at], c_recv.at[at])
+
+    def along(dz):
+        for d in range(1, ys):
+            by_y[d, dz] = push((dz, 0, 0), y_peers[d], y_send.at[d, dz], y_recv.at[d, dz])
+        across(dz, 0)
+
+    local = pltpu.make_async_copy(own_ref, all_ref.at[seq_at, grp_at], local_sem)
     local.start()
+    for d in range(1, zs):
+        by_z[d] = push((0, 0, 0), z_peers[d], z_send.at[d], z_recv.at[d])
+    along(0)
+    for dz in range(1, zs):
+        by_z[dz].wait_recv()
+        along(dz)
+    for dz in range(zs):
+        for dy in range(1, ys):
+            by_y[dy, dz].wait_recv()
+            across(dz, dy)
+    for at in list(by_x):
+        by_x[at].wait_recv()
+        to_core(*at)
+    for copy in by_c.values():
+        copy.wait_recv()
     local.wait()
-    for copy in copies:
-        copy.wait()
-
-
-def gather_rows(own, owners):
+    for copy in started:
+        copy.wait_send()
+
+
+def gather_blocks(own, owners, members):
     rows, width = own.shape
+    cs = 2 if members % 2 == 0 else 1
+    zs = 4 if owners % 4 == 0 else owners
+    sizes = (zs, owners // zs, members // cs, cs)
+    zs, ys, xs, cs = sizes
+    shapes = [(zs,), (ys, zs), (xs, zs, ys), (xs, zs, ys)]
+    sems = [pltpu.SemaphoreType.DMA(shape) for shape in shapes for _ in range(2)]
     return pl.pallas_call(
-        functools.partial(gather_body, owners),
-        out_shape=jax.ShapeDtypeStruct((owners * rows, width), own.dtype),
+        functools.partial(gather_body, sizes),
+        out_shape=jax.ShapeDtypeStruct((owners, members, rows, width), own.dtype),
         in_specs=[pl.BlockSpec(memory_space=pltpu.VMEM)],
         out_specs=pl.BlockSpec(memory_space=pltpu.VMEM),
-        scratch_shapes=[
-            pltpu.SemaphoreType.DMA((owners,)),
-            pltpu.SemaphoreType.DMA((owners,)),
-            pltpu.SemaphoreType.DMA,
-        ],
-        compiler_params=pltpu.CompilerParams(collective_id=0, has_side_effects=True),
-        name="gather_rows",
+        scratch_shapes=sems + [pltpu.SemaphoreType.DMA],
+        compiler_params=pltpu.CompilerParams(
+            collective_id=0, has_side_effects=True, vmem_limit_bytes=40 * 1024 * 1024
+        ),
+        name="gather_blocks",
     )(own)
 
 
@@ -637,8 +691,6 @@
         jnp.concatenate([share_place, own_place]),
     )
     fresh = latents[rows_share:]
-    shard_rows = lax.all_gather(latents[:rows_share], ("seq", "grp"), axis=0, tiled=True)
-
     each = -(-(n + 1) // 16) * 16
     numbers = jnp.concatenate(
         [prompt_len // PAGE, prompt_len % PAGE, page_counts[:, 0], slot_target.reshape(-1)]
@@ -647,8 +699,18 @@
     payload = jnp.concatenate(
         [own_normed, numbers, jnp.zeros((each - n - 1, width), bf16)], axis=0
     )
-    payload, latents = lax.optimization_barrier((payload, latents))
-    dec_all = gather_rows(payload, owners)
+    members = lax.axis_size("grp")
+    block = lax.dynamic_slice_in_dim(payload, col, share, 1).reshape(-1, LAT + ROPE)
+    blocks = gather_blocks(
+        jnp.concatenate([latents[:rows_share], block]), owners, members
+    )
+    shard_rows = blocks[:, :, :rows_share].reshape(-1, LAT + ROPE)
+    dec_all = (
+        blocks[:, :, rows_share:]
+        .reshape(owners, members, each, share)
+        .transpose(0, 2, 1, 3)
+        .reshape(owners * each, width)
+    )
     numbers = dec_all.reshape(owners, each, width)[:, n, : 2 * reqs + owners + owners * cap]
     ints = numbers.astype(jnp.int32)
     lens_all = ints[:, :reqs] * PAGE + ints[:, reqs : 2 * reqs]

time: 216 us -> 206 us (0.954)
  the two profiles are of different devices: /device:TPU:31 before, /device:TPU:0 now
where the time goes in v4:
time: 206 us; the launch traced here: 205 us
  Pallas kernels  83.2 us (40%)
  local copies, waits for them, and re-layouts  37.8 us (18%)
  waiting for transfers between devices  37.8 us (18%)
  other arithmetic  16.6 us (8%)
  between operations  14.6 us (7%)
  starting transfers between devices  11.9 us (6%)
  matrix products  3.43 us (2%)
    pallas_call x1, Pallas kernels, gather_blocks(): pl.pallas_call(functools.partial(gather_body, sizes), out_shape=jax.Shape...  32.9 us
    unnamed x2, waiting for transfers between devices  25.2 us
    unnamed x70, local copies, waits for them, and re-layouts  22.6 us
    pallas_call x2, Pallas kernels, sum_over_grp(): pl.pallas_call(functools.partial(sum_body, members, gather), out_shape=ja...  15 us
    all_to_all x1, waiting for transfers between devices, shards(): lax.all_to_all(sent.reshape(owners, each, -1), 'seq', split_axis=0, conca...  12.5 us
    pallas_call x1, Pallas kernels, delta_steps(): pl.pallas_call(functools.partial(delta_body, steps, reqs), out_shape=jax....  9.8 us
    pallas_call x1, Pallas kernels, attend_pages(): pl.pallas_call(functools.partial(page_body, reqs), out_shape=jax.ShapeDty...  9.35 us
    pallas_call x1, Pallas kernels, make_queries(): pl.pallas_call(query_body, out_shape=(jax.ShapeDtypeStruct((heads, group_...  9.14 us
  transfers between devices with their start and end apart: 3, of which 2 were waited for; matrix products, arithmetic and copies ran while one was open for 8% of the time, Pallas kernels for 8%

profile of v4, /device:TPU:0, one launch (start us, length us, event | category | flops | bytes accessed | tf_op | source)
XLA Modules:
  0.0 205.3 jit_solution(13059384895885684088)
XLA Ops:
  7.2 0.8 iota_add_fusion.1
  8.0 0.7 fusion.31
  8.7 1.6 fusion
  10.3 2.6 %fusion.1 = bf16[256,2304]{1,0:T(8,128)(2,1)} fusion(bf16[256,2304]{1,0:T(8,128)(2,1)} %param.20, f32[256]{0:T(256)S(1)} %add_rsqrt_fusion.1), kind=kLoop, calls=%fused_computation.3 | loop fusion | flops 1769472 | bytes 2360320 | tf_op jit(solution)/shard_map/convert_element_type | solution.py:683
  13.2 1.0 constant_dynamic-slice_fusion.3
  14.2 0.9 fusion.2
  16.3 32.9 %gather_blocks.1 = bf16[8,4,96,576]{3,2,1,0:T(8,128)(2,1)S(1)} custom-call(bf16[96,576]{1,0:T(8,128)(2,1)S(1)} %pad_maximum_fusion.3.own_ref), custom_call_target="tpu_custom_call" | custom-call | tf_op jit(solution)/shard_map/gather_blocks/pallas_call | solution.py:237
  49.2 1.9 copy-done.2
  51.3 0.7 copy.68
  52.0 1.0 reshape_reshape.3
  53.3 1.9 reshape.229
  55.1 3.5 %slice.44 = bf16[8,4,64,576]{3,2,1,0:T(8,128)(2,1)} slice(bf16[8,4,96,576]{3,2,1,0:T(8,128)(2,1)} %copy-done.2), slice={[0:8], [0:4], [0:64], [0:576]} | slice | bytes 4718592 | tf_op jit(solution)/shard_map/slice | solution.py:707
  60.2 1.0 fusion.6
  61.2 1.9 pad_maximum_fusion.rows_ref
  63.4 9.1 %make_queries.1 = (bf16[8,256,192]{2,1,0:T(8,128)(2,1)S(1)}, bf16[8,256,576]{2,1,0:T(8,128)(2,1)S(1)}) custom-call(bf16[512,2304]{1,0:T(8,128)(2,1)S(1)} %pad_maximum_fusion.rows_ref, bf16[2304,1536]{1,0:T(8,128)(2,1)} %weight_ref.2, bf16[512,1024]{1,0:T(8,128)(2,1)S(1)} %copy-done.19, f32[512,64]{1,0:T(8,128)S(1)} %get-tuple-element.41.cos_ref, ...), custom_call_target="tpu_custom_call" | custom-call | flops 3623878656 | bytes 9437184 | tf_op jit(solution)/shard_map/make_queries/pallas_call | solution.py:278
  72.6 9.3 %attend_pages.1 = bf16[256,1152]{1,0:T(8,128)(2,1)} custom-call(bf16[8,256,576]{2,1,0:T(8,128)(2,1)S(1)} %get-tuple-element.10.query_ref, bf16[8,768,576]{2,1,0:T(8,128)(2,1)S(1)} %bitcast.39, s32[8,1,768]{2,1,0:T(1,128)S(1)} %and_select_fusion.holder_ref, bf16[512,1024]{1,0:T(8,128)(2,1)S(1)} %copy-done.5), custom_call_target="tpu_custom_call" | custom-call | flops 3623878656 | bytes 7077888 | tf_op jit(solution)/shard_map/attend_pages/pallas_call | solution.py:347
  82.0 7.3 %all-to-all-start = ((bf16[8,32,1152]{2,1,0:T(8,128)(2,1)}), bf16[8,32,1152]{2,1,0:T(8,128)(2,1)S(1)}, u32[]{:S(2)}, u32[]{:S(2)}) async-start(bf16[8,32,1152]{2,1,0:T(8,128)(2,1)} %bitcast.8), calls=%async_computation | async-start | bytes 1179648 | tf_op jit(solution)/shard_map/all_to_all | solution.py:749
  89.3 3.9 %convert_element_type.84 = bf16[64,8,16,128]{3,2,1,0:T(8,128)(2,1)} convert(f32[64,8,16,128]{3,2,1,0:T(8,128)} %param.26) | non-fusion elementwise | flops 1048576 | bytes 6291456 | tf_op jit(solution)/shard_map/convert_element_type | solution.py:720
  93.2 12.5 %all-to-all-done.came_ref = bf16[8,32,1152]{2,1,0:T(8,128)(2,1)S(1)} async-done(((bf16[8,32,1152]{2,1,0:T(8,128)(2,1)}), bf16[8,32,1152]{2,1,0:T(8,128)(2,1)S(1)}, u32[]{:S(2)}, u32[]{:S(2)}) %all-to-all-start) | async-done | bytes 589856 | tf_op jit(solution)/shard_map/all_to_all | solution.py:749
  105.8 4.4 %all-to-all-start.1 = ((bf16[8,8,8,16,128]{4,3,2,1,0:T(8,128)(2,1)}), bf16[8,8,8,16,128]{4,3,2,1,0:T(8,128)(2,1)}, u32[]{:S(2)}, u32[]{:S(2)}) async-start(bf16[8,8,8,16,128]{4,3,2,1,0:T(8,128)(2,1)} %bitcast.41), calls=%async_computation.1 | async-start | bytes 4194304 | tf_op jit(solution)/shard_map/all_to_all | solution.py:721
  110.4 1.3 copy.76
  111.7 1.7 copy-done.8
  113.5 1.2 copy-done.11
  114.7 1.2 copy-done.20
  115.9 1.2 copy-done.22
  117.1 3.0 %prefill_attend.1 = bf16[256,1024]{1,0:T(8,128)(2,1)S(1)} custom-call(s32[1]{0:T(128)} %bitcast.9.place_ref, bf16[8,256,192]{2,1,0:T(8,128)(2,1)S(1)} %copy-done.22, bf16[2048,576]{1,0:T(8,128)(2,1)S(1)} %bitcast.33, bf16[512,1024]{1,0:T(8,128)(2,1)S(1)} %copy-done.20, bf16[1024,512]{1,0:T(8,128)(2,1)S(1)} %bitcast.35), custom_call_target="tpu_custom_call" | custom-call | flops 4294967296 | bytes 4718592 | tf_op jit(solution)/shard_map/prefill_attend/pallas_call | solution.py:118
  120.2 2.5 %fusion.33 = bf16[256,2304]{1,0:T(8,128)(2,1)} fusion(bf16[256,1024]{1,0:T(8,128)(2,1)S(1)} %prefill_attend.1, bf16[1024,2304]{1,0:T(8,128)(2,1)S(1)} %bitcast.32), kind=kOutput, calls=%fused_computation.92 | convolution fusion | flops 1207959552 | bytes 6422528 | tf_op jit(solution)/shard_map/dot_general | solution.py:754
  122.7 2.6 %copy.80 = bf16[256,2304]{0,1:T(8,128)(2,1)} copy(bf16[256,2304]{1,0:T(8,128)(2,1)} %fusion.33) | data formatting | bytes 2359296
  125.7 1.0 constant_dynamic-slice_fusion.1
  126.7 2.3 %copy-done.4 = bf16[1024,2304]{1,0:T(8,128)(2,1)S(1)} copy-done((bf16[1024,2304]{1,0:T(8,128)(2,1)S(1)}, bf16[1024,2304]{1,0:T(8,128)(2,1)}, u32[]{:S(2)}) %copy-start.4) | copy-done | bytes 4718616
  129.1 4.0 %merge_parts.1.part_ref = bf16[4,32,576]{2,1,0:T(8,128)(2,1)S(1)} custom-call(bf16[8,32,1152]{2,1,0:T(8,128)(2,1)S(1)} %copy-done.10, bf16[8,32,576]{2,1,0:T(8,128)(2,1)S(1)} %bitcast.34, bf16[32,576]{1,0:T(8,128)(2,1)S(1)} %fusion.19.fresh_ref, bf16[512,1024]{1,0:T(8,128)(2,1)S(1)} %copy-done.7, bf16[1024,2304]{1,0:T(8,128)(2,1)S(1)} %copy-done.4), custom_call_target="tpu_custom_call" | custom-call | tf_op jit(solution)/shard_map/merge_parts/pallas_call | solution.py:413
  133.1 0.7 copy-done.13
  133.7 9.0 %sum_hidden.1 = bf16[4,32,576]{2,1,0:T(8,128)(2,1)} custom-call(bf16[4,32,576]{2,1,0:T(8,128)(2,1)} %copy-done.13), custom_call_target="tpu_custom_call" | custom-call | tf_op jit(solution)/shard_map/sum_hidden/pallas_call | solution.py:479
  142.8 0.9 convert_bitcast_fusion
  144.2 0.7 constant_dynamic-slice_fusion.refs_0_
  144.9 25.2 %reduce-scatter.4.cloned.1.call-done = bf16[576,256]{1,0:T(8,128)(2,1)} async-done(((bf16[2304,256]{1,0:T(8,128)(2,1)}), bf16[576,256]{1,0:T(8,128)(2,1)}) %reduce-scatter.4.cloned.1.call-update) | async-done | bytes 294928
  170.2 1.8 copy.81
  172.1 2.3 %copy-done.3 = bf16[1024,2304]{1,0:T(8,128)(2,1)S(1)} copy-done((bf16[1024,2304]{1,0:T(8,128)(2,1)S(1)}, bf16[1024,2304]{1,0:T(8,128)(2,1)}, u32[]{:S(2)}) %copy-start.3) | copy-done | bytes 4718616
  174.4 1.1 copy-done.14
  175.5 1.1 copy-done.15
  176.5 0.9 copy-done.16
  177.5 0.9 copy-done.17
  178.4 9.8 %delta_steps.1.part_ref = bf16[4,32,576]{2,1,0:T(8,128)(2,1)S(1)} custom-call(f32[32,2304]{1,0:T(8,128)S(1)} %convert_add_fusion.hidden_ref, bf16[3,2304,1024]{2,1,0:T(8,128)(2,1)} %bitcast.40, bf16[2304,8]{1,0:T(8,128)(2,1)S(1)} %copy.78.beta_ref, bf16[2304,128]{1,0:T(8,128)(2,1)S(1)} %copy-done.14, bf16[128,1024]{1,0:T(8,128)(2,1)S(1)} %copy-done.16, ...), custom_call_target="tpu_custom_call" | custom-call | tf_op jit(solution)/shard_map/delta_steps/pallas_call | solution.py:606
  188.3 0.7 copy-done.12
  188.9 6.0 %sum_output.1 = bf16[32,576]{1,0:T(8,128)(2,1)} custom-call(bf16[4,32,576]{2,1,0:T(8,128)(2,1)} %copy-done.12, f32[32,576]{1,0:T(8,128)} %constant_dynamic-slice_fusion.refs_0_), custom_call_target="tpu_custom_call" | custom-call | tf_op jit(solution)/shard_map/sum_output/pallas_call | solution.py:479
  194.9 1.4 slice_bitcast_fusion.1
  196.3 1.3 add_convert_fusion
  197.6 0.9 copy.79
  (114 shorter events, 4.8 us)
Async XLA Ops:
  7.2 7.0 %copy-start = (bf16[2304,576]{0,1:T(8,128)(2,1)S(1)}, bf16[2304,576]{0,1:T(8,128)(2,1)}, u32[]{:S(2)}) copy-start(bf16[2304,576]{0,1:T(8,128)(2,1)} %param.28) | copy-start | bytes 7962628
  7.2 5.7 %copy-start.23 = (bf16[3,8,2304]{2,1,0:T(8,128)(2,1)S(1)}, bf16[3,8,2304]{2,1,0:T(8,128)(2,1)}, u32[]{:S(2)}) copy-start(bf16[3,8,2304]{2,1,0:T(8,128)(2,1)} %param.21) | copy-start | bytes 331780
  13.2 2.7 %copy-start.26 = (s32[8,1,12]{2,1,0:T(1,128)S(1)}, s32[8,1,12]{2,1,0:T(1,128)}, u32[]{:S(2)}) copy-start(s32[8,1,12]{2,1,0:T(1,128)} %param.24) | copy-start | bytes 1156
  13.2 2.8 %copy-start.27 = (s32[8,1]{0,1:T(1,128)S(1)}, s32[8,1]{0,1:T(1,128)}, u32[]{:S(2)}) copy-start(s32[8,1]{0,1:T(1,128)} %param.25) | copy-start | bytes 100
  49.2 1.9 copy-start.2
  61.2 2.2 %copy-start.19 = (bf16[512,1024]{1,0:T(8,128)(2,1)S(1)}, bf16[512,1024]{1,0:T(8,128)(2,1)}, u32[]{:S(2)}) copy-start(bf16[512,1024]{1,0:T(8,128)(2,1)} %key_ref.3) | copy-start | bytes 3145732
  61.2 11.4 %slice-start.2 = ((s8[7864320]{0:T(1024)(128)(4,1)}), s8[4194304]{0:T(1024)(128)(4,1)S(1)}, s32[]{:S(2)}) async-start(s8[7864320]{0:T(1024)(128)(4,1)} %bitcast.37), calls=%async_computation.6 | async-start | bytes 8388608
  63.4 9.2 %copy-start.5 = (bf16[512,1024]{1,0:T(8,128)(2,1)S(1)}, bf16[512,1024]{1,0:T(8,128)(2,1)}, u32[]{:S(2)}) copy-start(bf16[512,1024]{1,0:T(8,128)(2,1)} %value_ref.3) | copy-start | bytes 3145732
  63.4 9.2 %slice-start.3 = ((s8[7864320]{0:T(1024)(128)(4,1)}), s8[3670016]{0:T(1024)(128)(4,1)S(1)}, s32[]{:S(2)}) async-start(s8[7864320]{0:T(1024)(128)(4,1)} %bitcast.37), calls=%async_computation.7 | async-start | bytes 7340032
  72.6 9.4 %copy-start.18 = (bf16[8,256,576]{2,1,0:T(8,128)(2,1)}, bf16[8,256,576]{2,1,0:T(8,128)(2,1)S(1)}, u32[]{:S(2)}) copy-start(bf16[8,256,576]{2,1,0:T(8,128)(2,1)S(1)} %get-tuple-element.10.query_ref) | copy-start | bytes 7077892
  72.6 9.4 %copy-start.21 = (bf16[8,256,192]{2,1,0:T(8,128)(2,1)}, bf16[8,256,192]{2,1,0:T(8,128)(2,1)S(1)}, u32[]{:S(2)}) copy-start(bf16[8,256,192]{2,1,0:T(8,128)(2,1)S(1)} %get-tuple-element.12.query_ref) | copy-start | bytes 2359300
  82.0 23.8 %all-to-all-start = ((bf16[8,32,1152]{2,1,0:T(8,128)(2,1)}), bf16[8,32,1152]{2,1,0:T(8,128)(2,1)S(1)}, u32[]{:S(2)}, u32[]{:S(2)}) async-start(bf16[8,32,1152]{2,1,0:T(8,128)(2,1)} %bitcast.8), calls=%async_computation | async-start | bytes 1179648 | tf_op jit(solution)/shard_map/all_to_all | solution.py:749
  93.2 17.1 %copy-start.6 = (bf16[512,1024]{1,0:T(8,128)(2,1)S(1)}, bf16[512,1024]{1,0:T(8,128)(2,1)}, u32[]{:S(2)}) copy-start(bf16[512,1024]{1,0:T(8,128)(2,1)} %value_ref.3) | copy-start | bytes 3145732
  105.8 5.9 %copy-start.9 = (bf16[8,32,1152]{2,1,0:T(8,128)(2,1)}, bf16[8,32,1152]{2,1,0:T(8,128)(2,1)S(1)}, u32[]{:S(2)}) copy-start(bf16[8,32,1152]{2,1,0:T(8,128)(2,1)S(1)} %all-to-all-done.came_ref) | copy-start | bytes 1769476
  105.8 66.2 %all-to-all-start.1 = ((bf16[8,8,8,16,128]{4,3,2,1,0:T(8,128)(2,1)}), bf16[8,8,8,16,128]{4,3,2,1,0:T(8,128)(2,1)}, u32[]{:S(2)}, u32[]{:S(2)}) async-start(bf16[8,8,8,16,128]{4,3,2,1,0:T(8,128)(2,1)} %bitcast.41), calls=%async_computation.1 | async-start | bytes 4194304 | tf_op jit(solution)/shard_map/all_to_all | solution.py:721
  110.1 60.0 %reduce-scatter.4.cloned.1.call-start = ((), (), s32[]{:S(2)}) async-start(), calls=%async_computation.3 | async-start | bytes 1474560
  110.4 9.8 %slice-start = ((s8[4718592]{0:T(1024)(128)(4,1)}), s8[524288]{0:T(1024)(128)(4,1)S(1)}, s32[]{:S(2)}) async-start(s8[4718592]{0:T(1024)(128)(4,1)} %bitcast.31), calls=%async_computation.4 | async-start | bytes 1048576
  111.7 1.7 copy-start.8
  113.5 1.2 copy-start.11
  114.7 1.2 copy-start.20
  115.9 1.2 copy-start.22
  117.1 3.0 %slice-start.1 = ((s8[4718592]{0:T(1024)(128)(4,1)}), s8[4194304]{0:T(1024)(128)(4,1)S(1)}, s32[]{:S(2)}) async-start(s8[4718592]{0:T(1024)(128)(4,1)} %bitcast.31), calls=%async_computation.5 | async-start | bytes 8388608
  122.7 2.6 %copy-start.25 = (bf16[2304,8]{0,1:T(8,128)(2,1)S(1)}, bf16[2304,8]{0,1:T(8,128)(2,1)}, u32[]{:S(2)}) copy-start(bf16[2304,8]{0,1:T(8,128)(2,1)} %param.33) | copy-start | bytes 110596
  122.7 2.9 %copy-start.28 = (f32[8]{0:T(128)S(1)}, f32[8]{0:T(128)}, u32[]{:S(2)}) copy-start(f32[8]{0:T(128)} %param.38) | copy-start | bytes 100
  122.7 4.0 %copy-start.7 = (bf16[512,1024]{1,0:T(8,128)(2,1)S(1)}, bf16[512,1024]{1,0:T(8,128)(2,1)}, u32[]{:S(2)}) copy-start(bf16[512,1024]{1,0:T(8,128)(2,1)} %value_ref.3) | copy-start | bytes 3145732
  122.7 4.0 %copy-start.10 = (bf16[8,32,1152]{2,1,0:T(8,128)(2,1)S(1)}, bf16[8,32,1152]{2,1,0:T(8,128)(2,1)}, u32[]{:S(2)}) copy-start(bf16[8,32,1152]{2,1,0:T(8,128)(2,1)} %copy-done.9) | copy-start | bytes 1769476
  126.7 2.3 %copy-start.4 = (bf16[1024,2304]{1,0:T(8,128)(2,1)S(1)}, bf16[1024,2304]{1,0:T(8,128)(2,1)}, u32[]{:S(2)}) copy-start(bf16[1024,2304]{1,0:T(8,128)(2,1)} %weight_ref.3) | copy-start | bytes 14155780
  129.1 15.1 %copy-start.24 = (bf16[3,8,2304]{2,1,0:T(8,128)(2,1)S(1)}, bf16[3,8,2304]{2,1,0:T(8,128)(2,1)}, u32[]{:S(2)}) copy-start(bf16[3,8,2304]{2,1,0:T(8,128)(2,1)} %param.21) | copy-start | bytes 331780
  133.0 0.7 copy-start.13
  172.1 2.3 %copy-start.3 = (bf16[1024,2304]{1,0:T(8,128)(2,1)S(1)}, bf16[1024,2304]{1,0:T(8,128)(2,1)}, u32[]{:S(2)}) copy-start(bf16[1024,2304]{1,0:T(8,128)(2,1)} %output_ref.1) | copy-start | bytes 14155780
  174.4 1.1 copy-start.14
  175.5 1.1 copy-start.15
  176.5 0.9 copy-start.16
  177.5 0.9 copy-start.17
  178.4 20.0 %copy-start.1 = (bf16[2304,576]{0,1:T(8,128)(2,1)S(1)}, bf16[2304,576]{0,1:T(8,128)(2,1)}, u32[]{:S(2)}) copy-start(bf16[2304,576]{0,1:T(8,128)(2,1)} %param.28) | copy-start | bytes 7962628
  188.3 0.7 copy-start.12
Sparse Core Ops, SparseCore 0:
  125.4 44.7 reduce-scatter.3

commit v5 on v4

--- a/solution.py
+++ b/solution.py
@@ -29,40 +29,19 @@
     return values * lax.rsqrt(jnp.sum(values * values, axis=-1, keepdims=True) + epsilon)
 
 
-def rotate(values, position):
-    halfway = values.shape[-1] // 2
-    frequency = jnp.exp(-jnp.log(10000.0) * jnp.arange(halfway, dtype=jnp.float32) / halfway)
-    angles = position.astype(jnp.float32)[..., None] * frequency
-    leading = values[..., :halfway]
-    trailing = values[..., halfway:]
-    return jnp.concatenate(
-        [
-            leading * jnp.cos(angles) - trailing * jnp.sin(angles),
-            leading * jnp.sin(angles) + trailing * jnp.cos(angles),
-        ],
-        axis=-1,
-    )
-
-
-def make_latent(normed, latent_proj, position):
-    projected = jnp.dot(normed, latent_proj, preferred_element_type=jnp.float32)
-    return jnp.concatenate(
-        [norm_rows(projected[:, :LAT]), rotate(projected[:, LAT:], position)], axis=-1
-    ).astype(jnp.bfloat16)
-
-
-def make_query(normed, query_proj, position):
-    head_count = query_proj.shape[1] // (NOPE + ROPE)
-    projected = jnp.dot(normed, query_proj, preferred_element_type=jnp.float32).reshape(
-        normed.shape[0], head_count, NOPE + ROPE
-    )
-    return (
-        projected[..., :NOPE].astype(jnp.bfloat16),
-        rotate(projected[..., NOPE:], position[:, None]).astype(jnp.bfloat16),
-    )
-
-
-def prefill_body(place_ref, query_ref, rows_ref, key_ref, value_ref, out_ref, peak, total, mixed):
+def prefill_body(
+    place_ref,
+    query_ref,
+    rows_ref,
+    key_ref,
+    value_ref,
+    weight_ref,
+    out_ref,
+    peak,
+    total,
+    mixed,
+    result,
+):
     pair, group_rows, _ = query_ref.shape
     nt = (((1,), (1,)), ((), ()))
     factor = (NOPE + ROPE) ** (-0.5) * 1.4426950408889634
@@ -107,17 +86,38 @@
     def _(index):
         chunk(index, False)
 
-    for h in range(pair):
-        out_ref[:, h * VH : (h + 1) * VH] = (mixed[h] / total[h]).T.astype(out_ref.dtype)
-
-
-def prefill_attend(seq_index, queries, rows, key_expand, value_expand):
+    attended = jnp.concatenate(
+        [(mixed[h] / total[h]).T.astype(jnp.bfloat16) for h in range(pair)], axis=1
+    )
+    pieces, _, share = out_ref.shape
+    turn = pl.program_id(0)
+
+    @pl.when(turn == 0)
+    def _():
+        result[...] = jnp.zeros_like(result)
+
+    width = result.shape[1]
+    step = width // 3 if width % 384 == 0 else width
+    for at in range(0, width, step):
+        cut = slice(at, at + step)
+        result[:, cut] += jnp.dot(
+            attended, weight_ref[:, cut], preferred_element_type=jnp.float32
+        )
+
+    @pl.when(turn == pl.num_programs(0) - 1)
+    def _():
+        for p in range(pieces):
+            out_ref[p] = result[:, p * share : (p + 1) * share].astype(out_ref.dtype)
+
+
+def prefill_attend(seq_index, pieces, queries, rows, key_expand, value_expand, mla_output):
     heads, group_rows, _ = queries.shape
     pair = 4 if heads % 4 == 0 else 2
     row_count = rows.shape[0]
+    width = mla_output.shape[1]
     return pl.pallas_call(
         prefill_body,
-        out_shape=jax.ShapeDtypeStruct((group_rows, heads * VH), jnp.bfloat16),
+        out_shape=jax.ShapeDtypeStruct((pieces, group_rows, width // pieces), jnp.bfloat16),
         grid_spec=pltpu.PrefetchScalarGridSpec(
             num_scalar_prefetch=1,
             grid=(heads // pair,),
@@ -126,22 +126,70 @@
                 pl.BlockSpec((row_count, LAT + ROPE), lambda h, p: (0, 0)),
                 pl.BlockSpec((LAT, pair * NOPE), lambda h, p: (0, h)),
                 pl.BlockSpec((pair * VH, LAT), lambda h, p: (h, 0)),
+                pl.BlockSpec((pair * VH, width), lambda h, p: (h, 0)),
             ],
-            out_specs=pl.BlockSpec((group_rows, pair * VH), lambda h, p: (0, h)),
+            out_specs=pl.BlockSpec((pieces, group_rows, width // pieces), lambda h, p: (0, 0, 0)),
             scratch_shapes=[
                 pltpu.VMEM((pair, 1, group_rows), jnp.float32),
                 pltpu.VMEM((pair, 1, group_rows), jnp.float32),
                 pltpu.VMEM((pair, VH, group_rows), jnp.float32),
+                pltpu.VMEM((group_rows, width), jnp.float32),
             ],
         ),
-        compiler_params=pltpu.CompilerParams(vmem_limit_bytes=40 * 1024 * 1024),
+        compiler_params=pltpu.CompilerParams(vmem_limit_bytes=56 * 1024 * 1024),
         cost_estimate=pl.CostEstimate(
             flops=2 * heads * group_rows * row_count * 4 * NOPE,
             bytes_accessed=row_count * (LAT + ROPE) * 4,
             transcendentals=heads * group_rows * row_count,
         ),
         name="prefill_attend",
-    )(seq_index.reshape(1).astype(jnp.int32), queries, rows, key_expand, value_expand.T)
+    )(
+        seq_index.reshape(1).astype(jnp.int32),
+        queries,
+        rows,
+        key_expand,
+        value_expand.T,
+        mla_output,
+    )
+
+
+def prepare_body(count, rows_ref, weight_ref, cos_ref, sin_ref, own_ref, block_ref, fresh_ref):
+    rows = norm_rows(rows_ref[...].astype(jnp.float32)).astype(jnp.bfloat16)
+    nt = (((1,), (1,)), ((), ()))
+    projected = lax.dot_general(rows, weight_ref[...], nt, preferred_element_type=jnp.float32)
+    rope = projected[:, LAT:]
+    turned = jnp.concatenate([rope[:, ROPE // 2 :], rope[:, : ROPE // 2]], axis=1)
+    rope = rope * cos_ref[...] + turned * sin_ref[...]
+    latents = jnp.concatenate([norm_rows(projected[:, :LAT]), rope], axis=1).astype(jnp.bfloat16)
+    block_ref[:count] = latents[:count]
+    block_ref[count:] = own_ref[...]
+    fresh_ref[...] = latents[count:]
+
+
+def prepare(count, rows, latent_proj, cosine, sine, own):
+    depth = latent_proj.shape[1]
+    return pl.pallas_call(
+        functools.partial(prepare_body, count),
+        out_shape=(
+            jax.ShapeDtypeStruct((count + own.shape[0], depth), jnp.bfloat16),
+            jax.ShapeDtypeStruct((rows.shape[0] - count, depth), jnp.bfloat16),
+        ),
+        in_specs=[pl.BlockSpec(memory_space=pltpu.VMEM)] * 5,
+        out_specs=[pl.BlockSpec(memory_space=pltpu.VMEM)] * 2,
+        compiler_params=pltpu.CompilerParams(vmem_limit_bytes=32 * 1024 * 1024),
+        name="prepare",
+    )(rows, latent_proj.T, cosine, sine, own)
+
+
+def turns(place):
+    half = ROPE // 2
+    frequency = jnp.exp(-jnp.log(10000.0) * jnp.arange(half, dtype=jnp.float32) / half)
+    angles = place.astype(jnp.float32)[:, None] * frequency
+    cosine, sine = jnp.cos(angles), jnp.sin(angles)
+    return (
+        jnp.concatenate([cosine, cosine], axis=1),
+        jnp.concatenate([-sine, sine], axis=1),
+    )
 
 
 def gather_body(sizes, own_ref, all_ref, *sems):
@@ -241,17 +289,29 @@
         out_specs=pl.BlockSpec(memory_space=pltpu.VMEM),
         scratch_shapes=sems + [pltpu.SemaphoreType.DMA],
         compiler_params=pltpu.CompilerParams(
-            collective_id=0, has_side_effects=True, vmem_limit_bytes=40 * 1024 * 1024
+            collective_id=0, has_side_effects=True, vmem_limit_bytes=56 * 1024 * 1024
         ),
         name="gather_blocks",
     )(own)
 
 
-def query_body(rows_ref, weight_ref, key_ref, cos_ref, sin_ref, prefill_ref, decode_ref):
+def query_body(
+    group_ref, dec_ref, weight_ref, key_ref, cos_ref, sin_ref, prefill_ref, decode_ref, rows_ref
+):
     pair, group_rows, _ = prefill_ref.shape
     owners, slab, _ = decode_ref.shape
     each = slab // pair
     nt = (((1,), (1,)), ((), ()))
+
+    @pl.when(pl.program_id(0) == 0)
+    def _():
+        half = dec_ref.shape[0] // 2
+        rows_ref[:group_rows] = norm_rows(group_ref[...].astype(jnp.float32)).astype(jnp.bfloat16)
+        for at in range(0, 2 * half, half):
+            rows_ref[group_rows + at : group_rows + at + half] = norm_rows(
+                dec_ref[at : at + half].astype(jnp.float32)
+            ).astype(jnp.bfloat16)
+
     projected = jnp.dot(rows_ref[...], weight_ref[...], preferred_element_type=jnp.float32)
     for h in range(pair):
         start = h * (NOPE + ROPE)
@@ -270,9 +330,10 @@
         decode_ref[:, h * each : (h + 1) * each, :] = full.reshape(owners, each, LAT + ROPE)
 
 
-def make_queries(rows, group_rows, owners, query_proj, key_expand, cosine, sine):
+def make_queries(group, dec, owners, query_proj, key_expand, cosine, sine):
     pair = 2
-    total, width = rows.shape
+    group_rows, width = group.shape
+    total = group_rows + dec.shape[0]
     heads = key_expand.shape[1] // NOPE
     each = (total - group_rows) // owners
     return pl.pallas_call(
@@ -283,7 +344,8 @@
         ),
         grid=(heads // pair,),
         in_specs=[
-            pl.BlockSpec((total, width), lambda h: (0, 0)),
+            pl.BlockSpec(group.shape, lambda h: (0, 0)),
+            pl.BlockSpec(dec.shape, lambda h: (0, 0)),
             pl.BlockSpec((width, pair * (NOPE + ROPE)), lambda h: (0, h)),
             pl.BlockSpec((LAT, pair * NOPE), lambda h: (0, h)),
             pl.BlockSpec((total, ROPE), lambda h: (0, 0)),
@@ -293,14 +355,15 @@
             pl.BlockSpec((pair, group_rows, NOPE + ROPE), lambda h: (h, 0, 0)),
             pl.BlockSpec((owners, pair * each, LAT + ROPE), lambda h: (0, h, 0)),
         ),
-        compiler_params=pltpu.CompilerParams(vmem_limit_bytes=40 * 1024 * 1024),
+        scratch_shapes=[pltpu.VMEM((total, width), jnp.bfloat16)],
+        compiler_params=pltpu.CompilerParams(vmem_limit_bytes=56 * 1024 * 1024),
         cost_estimate=pl.CostEstimate(
             flops=2 * total * width * query_proj.shape[1],
             bytes_accessed=2 * width * (query_proj.shape[1] + total),
             transcendentals=0,
         ),
         name="make_queries",
-    )(rows, query_proj, key_expand, cosine, sine)
+    )(group, dec, query_proj, key_expand, cosine, sine)
 
 
 def page_body(reqs, query_ref, page_ref, holder_ref, value_ref, out_ref, parts, logs):
@@ -359,7 +422,7 @@
             pltpu.VMEM((heads, total, LAT), jnp.bfloat16),
             pltpu.VMEM((heads, total, 1), jnp.float32),
         ],
-        compiler_params=pltpu.CompilerParams(vmem_limit_bytes=40 * 1024 * 1024),
+        compiler_params=pltpu.CompilerParams(vmem_limit_bytes=56 * 1024 * 1024),
         cost_estimate=pl.CostEstimate(
             flops=4 * owners * rows * keys * depth,
             bytes_accessed=2 * owners * keys * depth,
@@ -415,7 +478,7 @@
         out_shape=jax.ShapeDtypeStruct((pieces, each, share), jnp.bfloat16),
         in_specs=[pl.BlockSpec(memory_space=pltpu.VMEM)] * 5,
         out_specs=pl.BlockSpec(memory_space=pltpu.VMEM),
-        compiler_params=pltpu.CompilerParams(vmem_limit_bytes=40 * 1024 * 1024),
+        compiler_params=pltpu.CompilerParams(vmem_limit_bytes=56 * 1024 * 1024),
         name="merge_parts",
     )(came, queries, fresh, value_expand, mla_output)
 
@@ -424,7 +487,7 @@
     if gather:
         out_ref, came, send_sem, recv_sem, send_back, recv_back = refs
     else:
-        base_ref, out_ref, came, send_sem, recv_sem = refs
+        mla_ref, dec_ref, out_ref, came, send_sem, recv_sem = refs
     me = lax.axis_index("grp")
     peers = [lax.rem(me + step, members) for step in range(members)]
     barrier = pltpu.get_barrier_semaphore()
@@ -451,7 +514,8 @@
         copies[step - 1].wait()
         total = total + came[step].astype(jnp.float32)
     if not gather:
-        out_ref[...] = (base_ref[...] + total).astype(out_ref.dtype)
+        hidden = dec_ref[...].astype(jnp.float32) + mla_ref[me].astype(jnp.float32)
+        out_ref[...] = (hidden + total).astype(out_ref.dtype)
         return
     out_ref[me] = total.astype(out_ref.dtype)
     copies = []
@@ -471,11 +535,11 @@
         copy.wait()
 
 
-def sum_over_grp(parts, base=None):
+def sum_over_grp(parts, *base):
     members, rows, share = parts.shape
-    gather = base is None
+    gather = not base
     sems = [pltpu.SemaphoreType.DMA((members,))] * (4 if gather else 2)
-    operands = (parts,) if gather else (parts, base)
+    operands = (parts,) + base
     return pl.pallas_call(
         functools.partial(sum_body, members, gather),
         out_shape=jax.ShapeDtypeStruct(parts.shape if gather else (rows, share), jnp.bfloat16),
@@ -492,7 +556,8 @@
 def delta_body(
     steps,
     reqs,
-    hidden_ref,
+    mla_ref,
+    dec_ref,
     input_ref,
     beta_ref,
     decay_down_ref,
@@ -511,18 +576,21 @@
 ):
     turn = pl.program_id(0)
     sources, _, pair, _, _ = state_ref.shape
-    each = hidden_ref.shape[0]
+    each = dec_ref.shape[0]
     pieces, _, share = out_ref.shape
     f32, bf16 = jnp.float32, jnp.bfloat16
     nt = (((1,), (1,)), ((), ()))
 
     @pl.when(turn == 0)
     def _():
-        kin[...] = norm_rows(hidden_ref[...]).astype(bf16)
+        added = jnp.concatenate([mla_ref[p].astype(f32) for p in range(pieces)], axis=1)
+        kin[...] = norm_rows(dec_ref[...].astype(f32) + added).astype(bf16)
         rows = kin[...]
         decay_low[...] = jnp.dot(rows, decay_down_ref[...], preferred_element_type=f32).astype(bf16)
         gate_low[...] = jnp.dot(rows, gate_down_ref[...], preferred_element_type=f32).astype(bf16)
-        betas[...] = jax.nn.sigmoid(jnp.dot(rows, beta_ref[...], preferred_element_type=f32))
+        betas[...] = jax.nn.sigmoid(
+            lax.dot_general(rows, beta_ref[...], nt, preferred_element_type=f32)
+        )
         total[...] = jnp.zeros_like(total)
 
     rows = kin[...]
@@ -585,8 +653,8 @@
 def delta_steps(
     steps,
     reqs,
-    pieces,
-    hidden,
+    mla_total,
+    dec_rows,
     kda_inputs,
     kda_beta,
     decay_down,
@@ -597,7 +665,8 @@
     states,
     kda_output,
 ):
-    each, width = hidden.shape
+    each, width = dec_rows.shape
+    pieces = mla_total.shape[0]
     heads = kda_beta.shape[1]
     pair = 2
     sources, _, _, part, _ = states.shape
@@ -608,9 +677,10 @@
         out_shape=jax.ShapeDtypeStruct((pieces, each, width // pieces), jnp.bfloat16),
         grid=(heads // pair,),
         in_specs=[
+            pl.BlockSpec(mla_total.shape, lambda h: (0, 0, 0)),
             pl.BlockSpec((each, width), whole),
             pl.BlockSpec((3, width, pair * DK), lambda h: (0, 0, h)),
-            pl.BlockSpec((width, heads), whole),
+            pl.BlockSpec((heads, width), whole),
             pl.BlockSpec(decay_down.shape, whole),
             pl.BlockSpec((decay_up.shape[0], pair * DK), wide),
             pl.BlockSpec(gate_down.shape, whole),
@@ -627,12 +697,13 @@
             pltpu.VMEM((each, heads), jnp.float32),
             pltpu.VMEM((each, width), jnp.float32),
         ],
-        compiler_params=pltpu.CompilerParams(vmem_limit_bytes=40 * 1024 * 1024),
+        compiler_params=pltpu.CompilerParams(vmem_limit_bytes=56 * 1024 * 1024),
         name="delta_steps",
     )(
-        hidden,
+        mla_total,
+        dec_rows,
         kda_inputs,
-        kda_beta,
+        kda_beta.T,
         decay_down,
         decay_up,
         gate_down,
@@ -680,30 +751,25 @@
     dec_own = decode_input.reshape(n, width)
     group_rows = x_group.shape[0]
     rows_share = group_rows // lax.axis_size("grp")
-    x_normed = norm_rows(x_group.astype(f32)).astype(bf16)
-    own_normed = norm_rows(dec_own.astype(f32)).astype(bf16)
-    own_place = (prompt_len[None, :] + jnp.arange(steps)[:, None]).reshape(n)
-    share_normed = lax.dynamic_slice_in_dim(x_normed, grp_index * rows_share, rows_share, 0)
-    share_place = seq_index * group_rows + grp_index * rows_share + jnp.arange(rows_share)
-    latents = make_latent(
-        jnp.concatenate([share_normed, own_normed]),
-        latent_proj,
-        jnp.concatenate([share_place, own_place]),
-    )
-    fresh = latents[rows_share:]
     each = -(-(n + 1) // 16) * 16
     numbers = jnp.concatenate(
         [prompt_len // PAGE, prompt_len % PAGE, page_counts[:, 0], slot_target.reshape(-1)]
     ).astype(bf16)
     numbers = jnp.pad(numbers, (0, width - numbers.shape[0]))[None]
-    payload = jnp.concatenate(
-        [own_normed, numbers, jnp.zeros((each - n - 1, width), bf16)], axis=0
-    )
+    payload = jnp.concatenate([dec_own, numbers, jnp.zeros((each - n - 1, width), bf16)], axis=0)
     members = lax.axis_size("grp")
     block = lax.dynamic_slice_in_dim(payload, col, share, 1).reshape(-1, LAT + ROPE)
-    blocks = gather_blocks(
-        jnp.concatenate([latents[:rows_share], block]), owners, members
-    )
+    share_rows = lax.dynamic_slice_in_dim(x_group, grp_index * rows_share, rows_share, 0)
+    share_place = seq_index * group_rows + grp_index * rows_share + jnp.arange(rows_share)
+    own_place = (prompt_len[None, :] + jnp.arange(each // reqs)[:, None]).reshape(-1)
+    block, fresh = prepare(
+        rows_share,
+        jnp.concatenate([share_rows, payload]),
+        latent_proj,
+        *turns(jnp.concatenate([share_place, own_place])),
+        block,
+    )
+    blocks = gather_blocks(block, owners, members)
     shard_rows = blocks[:, :, :rows_share].reshape(-1, LAT + ROPE)
     dec_all = (
         blocks[:, :, rows_share:]
@@ -722,18 +788,13 @@
 
     position = seq_index * group_rows + jnp.arange(group_rows)
     dec_place = (lens_all[:, None, :] + jnp.arange(each // reqs)[None, :, None]).reshape(-1)
-    place = jnp.concatenate([position, dec_place]).astype(f32)
-    half = ROPE // 2
-    angles = place[:, None] * jnp.exp(-jnp.log(10000.0) * jnp.arange(half, dtype=f32) / half)
-    cosine, sine = jnp.cos(angles), jnp.sin(angles)
     queries, qc = make_queries(
-        jnp.concatenate([x_normed, dec_all]),
-        group_rows,
+        x_group,
+        dec_all,
         owners,
         query_proj,
         key_expand,
-        jnp.concatenate([cosine, cosine], axis=1),
-        jnp.concatenate([-sine, sine], axis=1),
+        *turns(jnp.concatenate([position, dec_place])),
     )
 
     pages = latent_pages.reshape(owners, cap * PAGE, LAT + ROPE)
@@ -750,29 +811,24 @@
         sent.reshape(owners, each, -1), "seq", split_axis=0, concat_axis=0, tiled=True
     )
 
-    heads_out = prefill_attend(seq_index, queries, shard_rows, key_expand, value_expand)
-    prefill_part = jnp.dot(heads_out, mla_output, preferred_element_type=f32)
+    prefill_part = prefill_attend(
+        seq_index, members, queries, shard_rows, key_expand, value_expand, mla_output
+    )
     came, prefill_part = lax.optimization_barrier((came, prefill_part))
-    attended = lax.psum_scatter(
-        prefill_part.astype(bf16), "grp", scatter_dimension=1, tiled=True
-    )
+    attended = lax.psum_scatter(prefill_part, "grp", scatter_dimension=0, tiled=False)
 
     pieces = lax.axis_size("grp")
-    fresh = jnp.pad(fresh, ((0, each - n), (0, 0)))
     own_query = lax.dynamic_index_in_dim(qc, seq_index, 0, keepdims=False)
     own_query = own_query.reshape(heads, each, LAT + ROPE)
     mla_parts = merge_parts(
         reqs, n, pieces, came, own_query, fresh, value_expand, mla_output
     )
     mla_total = sum_over_grp(mla_parts)
-    dec_rows = jnp.pad(dec_own, ((0, each - n), (0, 0))).astype(f32)
-    hidden = dec_rows + mla_total.transpose(1, 0, 2).reshape(each, width).astype(f32)
-
     kda_parts = delta_steps(
         steps,
         reqs,
-        pieces,
-        hidden,
+        mla_total,
+        payload,
         kda_inputs.transpose(1, 0, 2),
         kda_beta,
         decay_down,
@@ -784,7 +840,8 @@
         kda_output,
     )
     kda_parts, attended = lax.optimization_barrier((kda_parts, attended))
-    decode_out = sum_over_grp(kda_parts, lax.dynamic_slice_in_dim(hidden, col, share, 1))
+    dec_share = lax.dynamic_slice_in_dim(payload, col, share, 1)
+    decode_out = sum_over_grp(kda_parts, mla_total, dec_share)
     prefill_out = (
         lax.dynamic_slice_in_dim(x_group, col, share, 1).astype(f32) + attended.astype(f32)
     ).astype(bf16)

time: 206 us -> 198 us (0.961)
  Pallas kernels: 83.2 us -> 104 us
  local copies, waits for them, and re-layouts: 37.8 us -> 21.4 us
  waiting for transfers between devices: 37.8 us -> 31.8 us
  matrix products: 3.43 us -> 0 us
  other arithmetic: 16.6 us -> 14.2 us
    unnamed x2 -> x1, waiting for transfers between devices: 25.2 us -> 0.02 us
    all_to_all x1, waiting for transfers between devices: 0.01 us -> 19.3 us  [shards(): lax.all_to_all(states, 'seq', split_axis=0, concat_axis=0, tiled=True)]
    unnamed x70 -> x20, local copies, waits for them, and re-layouts: 22.6 us -> 6.65 us
    pallas_call x1 -> x2, Pallas kernels: 3 us -> 10.2 us  [the longest x1 9.05 us: prefill_attend(): pl.pallas_call(prefill_body, out_shape=jax.ShapeDtypeStruct((pieces, grou...]
    pallas_call x1, Pallas kernels: 3.97 us -> 7.61 us  [merge_parts(): pl.pallas_call(functools.partial(merge_body, reqs, count), out_shape=jax....]
    convert_element_type x5 -> x2, other arithmetic: 3.68 us -> 0.09 us  [turns(): angles = place.astype(jnp.float32)[:, None] * frequency]
    dot_general x2 -> x0, matrix products: 3.43 us -> none  [the longest x1 2.49 us: shards(): prefill_part = jnp.dot(heads_out, mla_output, preferred_element_type=f32)]
    pallas_call x1, Pallas kernels: 9.35 us -> 12.5 us  [attend_pages(): pl.pallas_call(functools.partial(page_body, reqs), out_shape=jax.ShapeDty...]
  transfers between devices with their start and end apart: 3 -> 3, of which waited for: 2 -> 2; matrix products, arithmetic and copies ran while one was open for 8% -> 4% of each run, Pallas kernels for 8% -> 19%
where the time goes in v5:
time: 198 us; the launch traced here: 197 us
  Pallas kernels  104 us (53%)
  waiting for transfers between devices  31.8 us (16%)
  local copies, waits for them, and re-layouts  21.4 us (11%)
  between operations  14.3 us (7%)
  other arithmetic  14.2 us (7%)
  starting transfers between devices  11.1 us (6%)
    pallas_call x1, Pallas kernels, gather_blocks(): pl.pallas_call(functools.partial(gather_body, sizes), out_shape=jax.Shape...  35.6 us
    all_to_all x1, waiting for transfers between devices, shards(): lax.all_to_all(states, 'seq', split_axis=0, concat_axis=0, tiled=True)  19.3 us
    pallas_call x2, Pallas kernels, sum_over_grp(): pl.pallas_call(functools.partial(sum_body, members, gather), out_shape=ja...  15.1 us
    all_to_all x1, waiting for transfers between devices, shards(): lax.all_to_all(sent.reshape(owners, each, -1), 'seq', split_axis=0, conca...  12.5 us
    pallas_call x1, Pallas kernels, attend_pages(): pl.pallas_call(functools.partial(page_body, reqs), out_shape=jax.ShapeDty...  12.5 us
    pallas_call x1, Pallas kernels, delta_steps(): pl.pallas_call(functools.partial(delta_body, steps, reqs), out_shape=jax....  11.9 us
    pallas_call x1, Pallas kernels, make_queries(): pl.pallas_call(query_body, out_shape=(jax.ShapeDtypeStruct((heads, group_...  11.4 us
    pallas_call x1, Pallas kernels, prefill_attend(): pl.pallas_call(prefill_body, out_shape=jax.ShapeDtypeStruct((pieces, grou...  9.05 us
  transfers between devices with their start and end apart: 3, of which 2 were waited for; matrix products, arithmetic and copies ran while one was open for 4% of the time, Pallas kernels for 19%

profile of v5, /device:TPU:0, one launch (start us, length us, event | category | flops | bytes accessed | tf_op | source)
XLA Modules:
  0.0 197.2 jit_solution(4451172065801745905)
XLA Ops:
  7.2 0.7 iota_add_fusion.1
  7.8 0.7 fusion.11
  8.6 0.7 convert_reduce_fusion
  9.4 0.7 convert_bitcast_fusion
  10.2 1.0 constant_dynamic-slice_fusion.3
  11.2 0.9 pad_maximum_fusion.3.dec_ref
  12.1 1.0 pad_maximum_fusion.rows_ref
  13.2 0.3 fusion.1
  13.6 1.7 copy-done
  15.4 1.1 prepare.1
  16.5 0.6 copy-done.2
  17.2 0.6 copy-done.3
  17.8 35.6 %gather_blocks.1 = bf16[8,4,96,576]{3,2,1,0:T(8,128)(2,1)} custom-call(bf16[96,576]{1,0:T(8,128)(2,1)} %copy-done.2), custom_call_target="tpu_custom_call" | custom-call | tf_op jit(solution)/shard_map/gather_blocks/pallas_call | solution.py:285
  53.4 1.5 slice_bitcast_fusion
  54.9 0.7 copy.49
  55.6 1.0 reshape_reshape.3
  56.8 1.8 reshape.193.dec_ref
  58.7 3.5 %slice.22 = bf16[8,4,64,576]{3,2,1,0:T(8,128)(2,1)} slice(bf16[8,4,96,576]{3,2,1,0:T(8,128)(2,1)} %gather_blocks.1), slice={[0:8], [0:4], [0:64], [0:576]} | slice | bytes 4718592 | tf_op jit(solution)/shard_map/slice | solution.py:773
  62.4 0.1 lt.77
  62.6 0.1 add.157
  62.8 0.1 broadcast_in_dim.60
  62.9 0.3 dynamic-slice_reduce_fusion
  63.4 0.1 and.44
  63.7 1.0 fusion
  64.7 0.8 pad_maximum_fusion.1.cos_ref
  65.5 0.8 pad_maximum_fusion.2.sin_ref
  66.4 0.7 and_select_fusion.holder_ref
  67.0 11.4 %make_queries.1 = (bf16[8,256,192]{2,1,0:T(8,128)(2,1)}, bf16[8,256,576]{2,1,0:T(8,128)(2,1)}) custom-call(bf16[256,2304]{1,0:T(8,128)(2,1)} %group_ref.1, bf16[256,2304]{1,0:T(8,128)(2,1)} %reshape.193.dec_ref, bf16[2304,1536]{1,0:T(8,128)(2,1)} %weight_ref.3, bf16[512,1024]{1,0:T(8,128)(2,1)} %key_ref.3, f32[512,64]{1,0:T(8,128)} %pad_maximum_fusion.1.cos_ref, ...), custom_call_target="tpu_custom_call" | custom-call | flops 3623878656 | bytes 9437184 | tf_op jit(solution)/shard_map/make_queries/pallas_call | solution.py:339
  78.5 12.5 %attend_pages.1 = bf16[256,1152]{1,0:T(8,128)(2,1)} custom-call(bf16[8,256,576]{2,1,0:T(8,128)(2,1)} %get-tuple-element.13.query_ref, bf16[8,768,576]{2,1,0:T(8,128)(2,1)} %bitcast.41, s32[8,1,768]{2,1,0:T(1,128)} %and_select_fusion.holder_ref, bf16[512,1024]{1,0:T(8,128)(2,1)} %value_ref.3), custom_call_target="tpu_custom_call" | custom-call | flops 3623878656 | bytes 7077888 | tf_op jit(solution)/shard_map/attend_pages/pallas_call | solution.py:410
  91.0 7.2 %all-to-all-start = ((bf16[8,32,1152]{2,1,0:T(8,128)(2,1)}), bf16[8,32,1152]{2,1,0:T(8,128)(2,1)S(1)}, u32[]{:S(2)}, u32[]{:S(2)}) async-start(bf16[8,32,1152]{2,1,0:T(8,128)(2,1)} %bitcast.32), calls=%async_computation | async-start | bytes 1179648 | tf_op jit(solution)/shard_map/all_to_all | solution.py:810
  98.2 4.0 %convert_element_type.40 = bf16[64,8,16,128]{3,2,1,0:T(8,128)(2,1)} convert(f32[64,8,16,128]{3,2,1,0:T(8,128)} %param.26) | non-fusion elementwise | flops 1048576 | bytes 6291456 | tf_op jit(solution)/shard_map/convert_element_type | solution.py:786
  102.2 12.5 %all-to-all-done.came_ref = bf16[8,32,1152]{2,1,0:T(8,128)(2,1)S(1)} async-done(((bf16[8,32,1152]{2,1,0:T(8,128)(2,1)}), bf16[8,32,1152]{2,1,0:T(8,128)(2,1)S(1)}, u32[]{:S(2)}, u32[]{:S(2)}) %all-to-all-start) | async-done | bytes 589856 | tf_op jit(solution)/shard_map/all_to_all | solution.py:810
  114.7 0.8 copy-done.6
  115.5 3.6 %all-to-all-start.1 = ((bf16[8,8,8,16,128]{4,3,2,1,0:T(8,128)(2,1)}), bf16[8,8,8,16,128]{4,3,2,1,0:T(8,128)(2,1)S(1)}, u32[]{:S(2)}, u32[]{:S(2)}) async-start(bf16[8,8,8,16,128]{4,3,2,1,0:T(8,128)(2,1)} %bitcast.28), calls=%async_computation.1 | async-start | bytes 4194304 | tf_op jit(solution)/shard_map/all_to_all | solution.py:787
  119.1 0.2 reduce-scatter.2.cloned.1.call-start
  119.4 1.3 copy.57
  120.7 9.1 %prefill_attend.1 = bf16[4,256,576]{2,1,0:T(8,128)(2,1)} custom-call(s32[1]{0:T(128)} %bitcast.10.place_ref, bf16[8,256,192]{2,1,0:T(8,128)(2,1)} %get-tuple-element.15.query_ref, bf16[2048,576]{1,0:T(8,128)(2,1)} %bitcast.29, bf16[512,1024]{1,0:T(8,128)(2,1)} %key_ref.3, bf16[1024,512]{1,0:T(8,128)(2,1)} %bitcast.31, bf16[1024,2304]{1,0:T(8,128)(2,1)} %weight_ref.5), custom_call_target="tpu_custom_call" | custom-call | flops 4294967296 | bytes 4718592 | tf_op jit(solution)/shard_map/prefill_attend/pallas_call | solution.py:118
  129.8 1.7 constant_dynamic-slice_fusion
  131.6 7.6 %merge_parts.1.part_ref = bf16[4,32,576]{2,1,0:T(8,128)(2,1)} custom-call(bf16[8,32,1152]{2,1,0:T(8,128)(2,1)} %copy-done.6, bf16[8,32,576]{2,1,0:T(8,128)(2,1)} %bitcast.30, bf16[32,576]{1,0:T(8,128)(2,1)} %copy-done.3, bf16[512,1024]{1,0:T(8,128)(2,1)} %value_ref.3, bf16[1024,2304]{1,0:T(8,128)(2,1)} %weight_ref.5), custom_call_target="tpu_custom_call" | custom-call | tf_op jit(solution)/shard_map/merge_parts/pallas_call | solution.py:476
  139.2 9.0 %sum_hidden.1.mla_ref.refs_0_ = bf16[4,32,576]{2,1,0:T(8,128)(2,1)} custom-call(bf16[4,32,576]{2,1,0:T(8,128)(2,1)} %merge_parts.1.part_ref), custom_call_target="tpu_custom_call" | custom-call | tf_op jit(solution)/shard_map/sum_hidden/pallas_call | solution.py:543
  148.2 19.3 %all-to-all-done.1.state_ref = bf16[8,8,8,16,128]{4,3,2,1,0:T(8,128)(2,1)S(1)} async-done(((bf16[8,8,8,16,128]{4,3,2,1,0:T(8,128)(2,1)}), bf16[8,8,8,16,128]{4,3,2,1,0:T(8,128)(2,1)S(1)}, u32[]{:S(2)}, u32[]{:S(2)}) %all-to-all-start.1) | async-done | bytes 2097184 | tf_op jit(solution)/shard_map/all_to_all | solution.py:787
  167.6 0.7 broadcast_in_dim.59
  168.3 0.6 copy-done.4
  168.9 11.9 %delta_steps.1.part_ref = bf16[4,32,576]{2,1,0:T(8,128)(2,1)} custom-call(bf16[4,32,576]{2,1,0:T(8,128)(2,1)} %sum_hidden.1.mla_ref.refs_0_, bf16[32,2304]{1,0:T(8,128)(2,1)} %copy-done.7, bf16[3,2304,1024]{2,1,0:T(8,128)(2,1)} %bitcast.27, bf16[8,2304]{1,0:T(8,128)(2,1)} %bitcast.37, bf16[2304,128]{1,0:T(8,128)(2,1)} %decay_down_ref.1, ...), custom_call_target="tpu_custom_call" | custom-call | tf_op jit(solution)/shard_map/delta_steps/pallas_call | solution.py:675
  180.8 6.0 %sum_output.1 = bf16[32,576]{1,0:T(8,128)(2,1)} custom-call(bf16[4,32,576]{2,1,0:T(8,128)(2,1)} %delta_steps.1.part_ref, bf16[4,32,576]{2,1,0:T(8,128)(2,1)} %sum_hidden.1.mla_ref.refs_0_, bf16[32,576]{1,0:T(8,128)(2,1)} %copy-done.1), custom_call_target="tpu_custom_call" | custom-call | tf_op jit(solution)/shard_map/sum_output/pallas_call | solution.py:543
  186.8 1.4 slice_bitcast_fusion.1
  188.2 1.3 add_convert_fusion
  189.4 0.9 copy.58
  (43 shorter events, 1.5 us)
Async XLA Ops:
  12.1 41.3 %copy-start.7 = (bf16[32,2304]{1,0:T(8,128)(2,1)}, bf16[32,2304]{1,0:T(8,128)(2,1)S(1)}, u32[]{:S(2)}) copy-start(bf16[32,2304]{1,0:T(8,128)(2,1)S(1)} %pad_maximum_fusion.3.dec_ref) | copy-start | bytes 442372
  13.5 39.9 %copy-start.1 = (bf16[32,576]{1,0:T(8,128)(2,1)}, bf16[32,576]{1,0:T(8,128)(2,1)S(1)}, u32[]{:S(2)}) copy-start(bf16[32,576]{1,0:T(8,128)(2,1)S(1)} %constant_dynamic-slice_fusion.2.own_ref.refs_1_) | copy-start | bytes 110596
  13.6 1.8 copy-start
  16.5 0.7 copy-start.2
  17.1 0.6 copy-start.3
  91.0 23.7 %all-to-all-start = ((bf16[8,32,1152]{2,1,0:T(8,128)(2,1)}), bf16[8,32,1152]{2,1,0:T(8,128)(2,1)S(1)}, u32[]{:S(2)}, u32[]{:S(2)}) async-start(bf16[8,32,1152]{2,1,0:T(8,128)(2,1)} %bitcast.32), calls=%async_computation | async-start | bytes 1179648 | tf_op jit(solution)/shard_map/all_to_all | solution.py:810
  102.2 17.2 %copy-start.5 = (bf16[512,1024]{1,0:T(8,128)(2,1)S(1)}, bf16[512,1024]{1,0:T(8,128)(2,1)}, u32[]{:S(2)}) copy-start(bf16[512,1024]{1,0:T(8,128)(2,1)} %value_ref.3) | copy-start | bytes 3145732
  114.7 0.8 copy-start.6
  115.5 52.1 %all-to-all-start.1 = ((bf16[8,8,8,16,128]{4,3,2,1,0:T(8,128)(2,1)}), bf16[8,8,8,16,128]{4,3,2,1,0:T(8,128)(2,1)S(1)}, u32[]{:S(2)}, u32[]{:S(2)}) async-start(bf16[8,8,8,16,128]{4,3,2,1,0:T(8,128)(2,1)} %bitcast.28), calls=%async_computation.1 | async-start | bytes 4194304 | tf_op jit(solution)/shard_map/all_to_all | solution.py:787
  119.1 61.6 %reduce-scatter.2.cloned.1.call-start = ((), (), s32[]{:S(2)}) async-start(), calls=%async_computation.3 | async-start | bytes 1638400 | tf_op jit(solution)/shard_map/reduce_scatter | solution.py:818
  120.7 9.1 %copy-start.8 = (f32[8]{0:T(128)S(1)}, f32[8]{0:T(128)}, u32[]{:S(2)}) copy-start(f32[8]{0:T(128)} %param.38) | copy-start | bytes 100
  167.6 1.3 copy-start.4
Sparse Core Ops, SparseCore 0:
  129.9 45.6 reduce-scatter.1
